TPU v7x, 32 devices: a whole 2x2x4 slice. The times are simulated.
32 devices in a mesh: section: 4 (over y, x), tensor: 8 (over z, core).
Axes of the slice: x: 2, y: 2, z: 4, core: 2. Of those that a mesh axis runs over, the one named last changes fastest.
Arguments:
- inputs: bfloat16 [4, 1024, 8192], P('section', None, 'tensor'), may hold values from -6 to 6
- preact: bfloat16 [4, 1024, 32768], P('section', None, 'tensor'), may hold values from -6 to 6
- handoff: bfloat16 [4, 1024, 8192], P('section', None, 'tensor'), may hold values from -6 to 6
- first_blocks: bfloat16 [4, 128, 6, 256, 256], P('section', 'tensor'), may hold values from -0.15625 to 0.15625
- second_blocks: bfloat16 [4, 128, 6, 256, 256], P('section', 'tensor'), may hold values from -0.078125 to 0.078125
- left_one: bfloat16 [4, 8192, 256], P('section', 'tensor'), may hold values from -0.0625 to 0.0625
- right_one: bfloat16 [4, 256, 32768], P('section', None, 'tensor'), may hold values from -0.375 to 0.375
- left_two: bfloat16 [4, 32768, 256], P('section', 'tensor'), may hold values from -0.03125 to 0.03125
- right_two: bfloat16 [4, 256, 8192], P('section', None, 'tensor'), may hold values from -0.375 to 0.375
Outputs:
- input_grad: bfloat16 [4, 1024, 8192], P('section', None, 'tensor')
- first_grad: bfloat16 [4, 128, 6, 256, 256], P('section', 'tensor')
- second_grad: bfloat16 [4, 128, 6, 256, 256], P('section', 'tensor')
- leftone_grad: bfloat16 [4, 8192, 256], P('section', 'tensor')
- rightone_grad: bfloat16 [4, 256, 32768], P('section', None, 'tensor')
- lefttwo_grad: bfloat16 [4, 32768, 256], P('section', 'tensor')
- righttwo_grad: bfloat16 [4, 256, 8192], P('section', None, 'tensor')
All inputs are finite; a program needn't handle non-finite values.
Results may differ from a plain program's by a relative error of at most 0.0061.
Values may be sent and summed in bfloat16 or wider, within the bound.
No kernel may reach another device: no remote copies, remote signals or barrier semaphores. Data moves between devices by JAX's collectives and lax.ppermute only.
A program may use at most 256 MiB of HBM per device.

v0:
```python
import jax
import jax.numpy as jnp
from jax import lax
from jax.sharding import PartitionSpec as P


def swapped(value, axis, apart):
    mask = 2**apart
    pairs = [(source, source ^ mask) for source in range(lax.axis_size(axis))]
    return lax.ppermute(value, axis, pairs)


def shifted(shard, axis, by):
    peers = lax.axis_size(axis)
    return lax.ppermute(shard, axis, [(i, (i + by) % peers) for i in range(peers)])


def gelu_pair(preact):
    values = preact.astype(jnp.float32)
    normal_cdf = 0.5 * (1.0 + jax.scipy.special.erf(values * 0.7071067811865476))
    density = jnp.exp(-0.5 * values * values) * 0.3989422804014327
    return (values * normal_cdf, normal_cdf + values * density)


def flip_blocks(values, stride, block_size):
    full_shape = values.shape
    folded = values.reshape(
        full_shape[:-1] + (full_shape[-1] // (2 * stride * block_size), 2, stride * block_size)
    )
    return folded[..., ::-1, :].reshape(full_shape)


def partner_sets(values, count_in, block_size, link_count, swapper):
    local_bits = count_in.bit_length() - 1
    result = [values]
    for degree in range(1, link_count):
        stride = 1 << degree - 1
        if stride < count_in:
            result.append(flip_blocks(values, stride, block_size))
        else:
            result.append(swapper(values, degree - 1 - local_bits))
    return result


def body(
    inputs, preact, handoff, first_blocks, second_blocks, left_one, right_one, left_two, right_two
):
    own_inputs = inputs[0]
    blocks_one = first_blocks[0]
    blocks_two = second_blocks[0]
    hid_count = blocks_one.shape[0]
    link_count = blocks_one.shape[1]
    block_size = blocks_one.shape[-1]
    row_count = own_inputs.shape[0]
    feat_width = own_inputs.shape[1]
    count_in = feat_width // block_size
    group_size = hid_count // count_in
    local_bits = count_in.bit_length() - 1
    activated, slope_vals = gelu_pair(preact[0])
    activated = activated.astype(jnp.bfloat16)
    proj_in, proj_act = lax.psum(
        (
            jnp.dot(own_inputs, left_one[0], preferred_element_type=jnp.float32),
            jnp.dot(activated, left_two[0], preferred_element_type=jnp.float32),
        ),
        "tensor",
    )
    proj_in = proj_in.astype(jnp.bfloat16)
    proj_act = proj_act.astype(jnp.bfloat16)

    def swap_inputs(values, bit_pos):
        return swapped(values, "tensor", bit_pos)

    def swap_grads(values, bit_pos):
        return swapped(values, "tensor", bit_pos)

    input_sets = jnp.stack(partner_sets(own_inputs, count_in, block_size, link_count, swap_inputs))
    upstream = shifted(handoff[0], "section", -1)
    grad_sets = jnp.stack(partner_sets(upstream, count_in, block_size, link_count, swap_grads))
    proj_grad = lax.psum(
        jnp.dot(upstream, right_two[0].T, preferred_element_type=jnp.float32), "tensor"
    ).astype(jnp.bfloat16)
    grad_view = grad_sets.reshape(link_count, row_count, count_in, block_size)
    second_view = blocks_two.reshape(count_in, group_size, link_count, block_size, block_size)
    grad_act = jnp.einsum(
        "ktcb,cjkeb->tcje", grad_view, second_view, preferred_element_type=jnp.float32
    ).reshape(row_count, hid_count * block_size)
    grad_act = grad_act + jnp.dot(proj_grad, left_two[0].T, preferred_element_type=jnp.float32)
    hidden_grad = (grad_act * slope_vals).astype(jnp.bfloat16)
    back_rank = lax.psum(
        jnp.dot(hidden_grad, right_one[0].T, preferred_element_type=jnp.float32), "tensor"
    ).astype(jnp.bfloat16)
    hidden_view = hidden_grad.reshape(row_count, count_in, group_size, block_size)
    first_view = blocks_one.reshape(count_in, group_size, link_count, block_size, block_size)
    partials = jnp.einsum(
        "tcje,cjkbe->ktcb", hidden_view, first_view, preferred_element_type=jnp.float32
    ).reshape(link_count, row_count, feat_width)
    summed_grad = partials[0] + jnp.dot(
        back_rank, left_one[0].T, preferred_element_type=jnp.float32
    )
    degree_order = list(range(1, link_count))
    for degree in degree_order:
        stride = 1 << degree - 1
        if stride < count_in:
            summed_grad = summed_grad + flip_blocks(partials[degree], stride, block_size)
        else:
            summed_grad = summed_grad + swapped(partials[degree], "tensor", degree - 1 - local_bits)
    input_grad = summed_grad.astype(jnp.bfloat16)[None]
    input_view = input_sets.reshape(link_count, row_count, count_in, block_size)
    first_grad = jnp.einsum(
        "ktcb,tcje->cjkbe", input_view, hidden_view, preferred_element_type=jnp.float32
    )
    first_grad = first_grad.reshape(hid_count, link_count, block_size, block_size).astype(
        jnp.bfloat16
    )[None]
    activ_view = activated.reshape(row_count, count_in, group_size, block_size)
    second_grad = jnp.einsum(
        "tcje,ktcb->cjkeb", activ_view, grad_view, preferred_element_type=jnp.float32
    )
    second_grad = second_grad.reshape(hid_count, link_count, block_size, block_size).astype(
        jnp.bfloat16
    )[None]
    leftone_grad = jnp.dot(own_inputs.T, back_rank, preferred_element_type=jnp.float32).astype(
        jnp.bfloat16
    )[None]
    rightone_grad = jnp.dot(proj_in.T, hidden_grad, preferred_element_type=jnp.float32).astype(
        jnp.bfloat16
    )[None]
    lefttwo_grad = jnp.dot(activated.T, proj_grad, preferred_element_type=jnp.float32).astype(
        jnp.bfloat16
    )[None]
    righttwo_grad = jnp.dot(proj_act.T, upstream, preferred_element_type=jnp.float32).astype(
        jnp.bfloat16
    )[None]
    return (
        input_grad,
        first_grad,
        second_grad,
        leftone_grad,
        rightone_grad,
        lefttwo_grad,
        righttwo_grad,
    )


def solution(mesh):
    in_specs = (
        P("section", None, "tensor"),
        P("section", None, "tensor"),
        P("section", None, "tensor"),
        P("section", "tensor", None, None, None),
        P("section", "tensor", None, None, None),
        P("section", "tensor", None),
        P("section", None, "tensor"),
        P("section", "tensor", None),
        P("section", None, "tensor"),
    )
    out_specs = (
        P("section", None, "tensor"),
        P("section", "tensor", None, None, None),
        P("section", "tensor", None, None, None),
        P("section", "tensor", None),
        P("section", None, "tensor"),
        P("section", "tensor", None),
        P("section", None, "tensor"),
    )
    return jax.shard_map(body, mesh=mesh, in_specs=in_specs, out_specs=out_specs, check_vma=False)
```

profile of v0, /device:TPU:0, one launch (start us, length us, event | category | flops | bytes accessed | tf_op | source)
XLA Modules:
  0.0 779.7 jit_solution(17381575283158847368)
XLA Ops:
  24.6 19.9 %reshape.108 = f32[1024,4,4,256]{3,2,1,0:T(4,128)} reshape(bf16[1,1024,4096]{2,1,0:T(8,128)(2,1)} %param.10) | data formatting | bytes 25165824 | tf_op jit(solution)/shard_map/convert_element_type | solution.py:19
  44.4 7.3 fusion.26
  95.5 10.4 %collective-permute-done.9 = bf16[1024,1024]{0,1:T(8,128)(2,1)} collective-permute-done((bf16[1024,1024]{0,1:T(8,128)(2,1)}, bf16[1024,1024]{0,1:T(8,128)(2,1)}, u32[]{:S(2)}, u32[]{:S(2)}) %collective-permute-start.9) | collective-permute-done | bytes 2097184 | tf_op jit(solution)/shard_map/ppermute | solution.py:10
  132.8 140.7 %all-reduce.3 = bf16[1024,256]{1,0:T(8,128)(2,1)} all-reduce(f32[1024,256]{1,0:T(8,128)S(1)} %fusion.60), channel_id=1, replica_groups=mesh['section'=4,'tensor'=8] {'tensor'}, use_global_device_ids=true, to_apply=%region_0.0 | all-reduce | flops 262144 | bytes 1572864 | tf_op jit(solution)/shard_map/psum | solution.py:80
  273.5 8.7 %fusion.38 = bf16[1,4096,256]{2,1,0:T(8,128)(2,1)} fusion(bf16[1,1024,4096]{2,1,0:T(8,128)(2,1)} %param.10, bf16[1024,256]{1,0:T(8,128)(2,1)} %all-reduce.3), kind=kOutput, calls=%fused_computation.37 | convolution fusion | flops 2173698048 | bytes 11010048 | tf_op jit(solution)/shard_map/dot_general | solution.py:129
  301.7 23.1 %fusion.18 = f32[4,1024,4,256,1]{1,3,4,2,0:T(8,128)} fusion(bf16[4,4,6,256,256]{4,3,2,1,0:T(8,128)(2,1)} %bitcast.176, bf16[6,1024,4,256]{3,1,0,2:T(8,128)(2,1)} %constant_dynamic-update-slice_fusion), kind=kOutput, calls=%fused_computation.24 | convolution fusion | flops 12884901888 | bytes 41943040 | tf_op jit(solution)/shard_map/ktcb,cjkeb->tcje/dot_general | solution.py:85
  324.8 17.5 %copy.40 = f32[1024,4096]{1,0:T(8,128)} copy(f32[1024,4096]{0,1:T(8,128)} %bitcast.166) | data formatting | bytes 33554432 | tf_op jit(solution)/shard_map/reshape | solution.py:87
  342.3 15.9 %fusion.5 = bf16[1024,4096]{1,0:T(8,128)(2,1)} fusion(bf16[1,1024,4096]{2,1,0:T(8,128)(2,1)} %param.10, f32[1024,4096]{1,0:T(8,128)} %copy.40, bf16[1,4096,256]{2,1,0:T(8,128)(2,1)S(1)} %copy-done, bf16[1024,256]{1,0:T(8,128)(2,1)S(1)} %copy-done.16), kind=kOutput, calls=%fused_computation.6 | convolution fusion | flops 2197815296 | bytes 36175872 | tf_op jit(solution)/shard_map/dot_general | solution.py:88
  358.2 14.6 %reshape.104 = bf16[1024,4,4,256]{3,2,1,0:T(4,128)(2,1)} reshape(bf16[1024,4096]{1,0:T(8,128)(2,1)} %fusion.5) | data formatting | bytes 16777216 | tf_op jit(solution)/shard_map/reshape | solution.py:93
  372.8 7.5 fusion.46
  380.2 71.4 %all-reduce.4 = (bf16[1024,256]{1,0:T(8,128)(2,1)S(1)}, bf16[1024,256]{1,0:T(8,128)(2,1)}, bf16[1024,256]{1,0:T(8,128)(2,1)}) all-reduce(f32[1024,256]{1,0:T(8,128)} %fusion.46, f32[1024,256]{1,0:T(8,128)} %fusion.42, f32[1024,256]{1,0:T(8,128)} %fusion.26), channel_id=1, replica_groups=mesh['section'=4,'tensor'=8] {'tensor'}, use_global_device_ids=true, to_apply=%region_1.0 | all-reduce | flops 786432 | bytes 4718592 | tf_op jit(solution)/shard_map/psum | solution.py:90
  453.3 13.8 %copy.69 = bf16[1024,4,4,256,1]{0,3,4,2,1:T(8,128)(2,1)} copy(bf16[1024,4,4,256,1]{3,2,1,0,4:T(4,128)(2,1)} %bitcast.154) | data formatting | bytes 16777216 | tf_op jit(solution)/shard_map/reshape | solution.py:93
  467.1 21.9 %fusion.32 = bf16[4,4,256,6,256]{4,2,3,1,0:T(8,128)(2,1)} fusion(bf16[1024,4,4,256,1]{0,3,4,2,1:T(8,128)(2,1)} %copy.69, bf16[6,1024,4,256]{3,1,0,2:T(8,128)(2,1)} %constant_dynamic-update-slice_fusion.6), kind=kOutput, calls=%fused_computation.34 | convolution fusion | flops 12891193344 | bytes 33554432 | tf_op jit(solution)/shard_map/ktcb,tcje->cjkbe/dot_general | solution.py:110
  489.0 16.6 %copy.63 = bf16[1,16,6,256,256]{4,3,2,1,0:T(8,128)(2,1)} copy(bf16[1,16,6,256,256]{3,4,2,1,0:T(8,128)(2,1)} %bitcast.170) | data formatting | bytes 25165824
  505.6 21.5 %convolution_bitcast_fusion = f32[6,1024,4,256]{1,3,0,2:T(8,128)} fusion(bf16[1024,4,4,256,1]{0,3,4,2,1:T(8,128)(2,1)} %copy.69, bf16[4,4,6,256,256]{4,3,2,1,0:T(8,128)(2,1)} %bitcast.177), kind=kOutput, calls=%fused_computation.27 | convolution fusion | flops 12884901888 | bytes 46137344 | tf_op jit(solution)/shard_map/tcje,cjkbe->ktcb/dot_general | solution.py:95
  527.1 18.0 %fusion.75 = (f32[1,1024,4,256]{1,3,0,2:T(8,128)}, f32[1,1024,4,256]{1,3,0,2:T(8,128)}, f32[1,1024,4,256]{1,3,0,2:T(8,128)}, f32[1,1024,4,256]{1,3,0,2:T(8,128)}...) fusion(f32[6,1024,4,256]{1,3,0,2:T(8,128)} %convolution_bitcast_fusion), kind=kLoop, calls=%fused_computation.81 | loop fusion | bytes 50331648 | tf_op jit(solution)/shard_map/slice | solution.py:98
  550.4 5.6 copy.48
  556.0 5.4 copy.47
  571.5 5.4 copy.76
  590.0 23.2 %convert_bitcast_fusion = bf16[4,4,6,256,256]{3,4,1,2,0:T(8,128)(2,1)} fusion(f32[1024,4,4,256]{3,2,1,0:T(4,128)} %reshape.108, bf16[6,1024,4,256]{3,1,0,2:T(8,128)(2,1)} %constant_dynamic-update-slice_fusion), kind=kOutput, calls=%fused_computation.26 | convolution fusion | flops 12912164864 | bytes 41943040 | tf_op jit(solution)/shard_map/tcje,ktcb->cjkeb/dot_general | solution.py:117
  613.2 16.7 %copy.62 = bf16[4,4,6,256,256]{4,3,2,1,0:T(8,128)(2,1)} copy(bf16[4,4,6,256,256]{3,4,1,2,0:T(8,128)(2,1)} %convert_bitcast_fusion) | data formatting | bytes 25165824 | tf_op jit(solution)/shard_map/convert_element_type | solution.py:120
  633.3 7.9 %fusion.41 = bf16[1,256,4096]{2,1,0:T(8,128)(2,1)} fusion(bf16[1024,4096]{1,0:T(8,128)(2,1)} %fusion.5, bf16[1024,256]{1,0:T(8,128)(2,1)S(1)} %copy-done.12), kind=kOutput, calls=%fused_computation.38 | convolution fusion | flops 2148532224 | bytes 11010048 | tf_op jit(solution)/shard_map/dot_general | solution.py:126
  641.1 128.4 %collective-permute-done.5 = f32[1024,1024]{1,0:T(8,128)} collective-permute-done((f32[1024,1024]{1,0:T(8,128)}, f32[1024,1024]{1,0:T(8,128)}, u32[]{:S(2)}, u32[]{:S(2)}) %collective-permute-start.5) | collective-permute-done | bytes 4194336 | tf_op jit(solution)/shard_map/ppermute | solution.py:10
  771.1 8.1 %fusion.50 = bf16[1,1024,1024]{2,1,0:T(8,128)(2,1)} fusion(f32[1024,1024]{1,0:T(8,128)} %collective-permute-done.6, f32[1024,1024]{1,0:T(8,128)} %collective-permute-done.5, f32[1024,1024]{1,0:T(8,128)} %collective-permute-done.4, f32[1024,1024]{1,0:T(8,128)S(1)} %copy-done.4, f32[1024,1024]{1,0:T(8,128)S(1)} %copy-done.5, f32[1024,1024]{1,0:T(8,128)S(1)} %copy-done.3, ...), kind=kOutput, calls=%fused_computation.48 | convolution fusion | flops 544210944 | bytes 28311552 | tf_op jit(solution)/shard_map/dot_general | solution.py:98
  (99 shorter events, 149.1 us)
Async XLA Ops:
  0.6 43.8 %copy-start = (bf16[1,4096,256]{2,1,0:T(8,128)(2,1)S(1)}, bf16[1,4096,256]{2,1,0:T(8,128)(2,1)}, u32[]{:S(2)}) copy-start(bf16[1,4096,256]{2,1,0:T(8,128)(2,1)} %param.16) | copy-start | bytes 6291460
  0.6 16.1 %copy-start.13 = (bf16[1,1024,256]{2,1,0:T(8,128)(2,1)S(1)}, bf16[1,1024,256]{2,1,0:T(8,128)(2,1)}, u32[]{:S(2)}) copy-start(bf16[1,1024,256]{2,1,0:T(8,128)(2,1)} %param.14) | copy-start | bytes 1572868
  4.8 67.9 %collective-permute-start = (bf16[1024,1024]{0,1:T(8,128)(2,1)}, bf16[1024,1024]{0,1:T(8,128)(2,1)}, u32[]{:S(2)}, u32[]{:S(2)}) collective-permute-start(bf16[1024,1024]{0,1:T(8,128)(2,1)} %bitcast.175), channel_id=1, source_target_pairs={{0,24},{8,0},{16,8},{24,16},{1,25},{9,1},{17,9},{25,17},{2,26},{10... | collective-permute-start | bytes 6291464 | tf_op jit(solution)/shard_map/ppermute | solution.py:15
  12.6 93.4 %collective-permute-start.9 = (bf16[1024,1024]{0,1:T(8,128)(2,1)}, bf16[1024,1024]{0,1:T(8,128)(2,1)}, u32[]{:S(2)}, u32[]{:S(2)}) collective-permute-start(bf16[1024,1024]{0,1:T(8,128)(2,1)} %bitcast.155), channel_id=1, source_target_pairs={{0,4},{1,5},{2,6},{3,7},{4,0},{5,1},{6,2},{7,3},{8,12},{9,13},{10,... | collective-permute-start | bytes 6291464 | tf_op jit(solution)/shard_map/ppermute | solution.py:10
  15.2 94.7 %collective-permute-start.8 = (bf16[1024,1024]{0,1:T(8,128)(2,1)}, bf16[1024,1024]{0,1:T(8,128)(2,1)}, u32[]{:S(2)}, u32[]{:S(2)}) collective-permute-start(bf16[1024,1024]{0,1:T(8,128)(2,1)} %bitcast.156), channel_id=1, source_target_pairs={{0,2},{1,3},{2,0},{3,1},{4,6},{5,7},{6,4},{7,5},{8,10},{9,11},{10,... | collective-permute-start | bytes 6291464 | tf_op jit(solution)/shard_map/ppermute | solution.py:10
  16.8 97.1 %collective-permute-start.7 = (bf16[1024,1024]{0,1:T(8,128)(2,1)}, bf16[1024,1024]{0,1:T(8,128)(2,1)}, u32[]{:S(2)}, u32[]{:S(2)}) collective-permute-start(bf16[1024,1024]{0,1:T(8,128)(2,1)} %bitcast.157), channel_id=1, source_target_pairs={{0,1},{1,0},{2,3},{3,2},{4,5},{5,4},{6,7},{7,6},{8,9},{9,8},{10,11... | collective-permute-start | bytes 6291464 | tf_op jit(solution)/shard_map/ppermute | solution.py:10
  119.7 6.1 copy-start.6
  122.2 6.7 copy-start.18
  128.9 153.3 %collective-permute-start.3 = (bf16[1024,1024]{0,1:T(8,128)(2,1)}, bf16[1024,1024]{0,1:T(8,128)(2,1)}, u32[]{:S(2)}, u32[]{:S(2)}) collective-permute-start(bf16[1024,1024]{0,1:T(8,128)(2,1)} %collective-permute-done), channel_id=1, source_target_pairs={{0,4},{1,5},{2,6},{3,7},{4,0},{5,1},{6,2},{7,3},{8,12},{9,13},{10,... | collective-permute-start | bytes 6291464 | tf_op jit(solution)/shard_map/ppermute | solution.py:10
  128.9 157.2 %collective-permute-start.2 = (bf16[1024,1024]{0,1:T(8,128)(2,1)}, bf16[1024,1024]{0,1:T(8,128)(2,1)}, u32[]{:S(2)}, u32[]{:S(2)}) collective-permute-start(bf16[1024,1024]{0,1:T(8,128)(2,1)} %collective-permute-done), channel_id=1, source_target_pairs={{0,2},{1,3},{2,0},{3,1},{4,6},{5,7},{6,4},{7,5},{8,10},{9,11},{10,... | collective-permute-start | bytes 6291464 | tf_op jit(solution)/shard_map/ppermute | solution.py:10
  132.8 157.2 %collective-permute-start.1 = (bf16[1024,1024]{0,1:T(8,128)(2,1)}, bf16[1024,1024]{0,1:T(8,128)(2,1)}, u32[]{:S(2)}, u32[]{:S(2)}) collective-permute-start(bf16[1024,1024]{0,1:T(8,128)(2,1)} %collective-permute-done), channel_id=1, source_target_pairs={{0,1},{1,0},{2,3},{3,2},{4,5},{5,4},{6,7},{7,6},{8,9},{9,8},{10,11... | collective-permute-start | bytes 6291464 | tf_op jit(solution)/shard_map/ppermute | solution.py:10
  294.0 6.2 copy-start.9
  324.7 17.5 %copy-start.16 = (bf16[1024,256]{1,0:T(8,128)(2,1)S(1)}, bf16[1024,256]{1,0:T(8,128)(2,1)}, u32[]{:S(2)}) copy-start(bf16[1024,256]{1,0:T(8,128)(2,1)} %all-reduce.3) | copy-start | bytes 1572868
  372.8 78.8 %copy-start.2 = (bf16[1,1024,1024]{2,1,0:T(8,128)(2,1)S(1)}, bf16[1,1024,1024]{2,1,0:T(8,128)(2,1)}, u32[]{:S(2)}) copy-start(bf16[1,1024,1024]{2,1,0:T(8,128)(2,1)} %param.9) | copy-start | bytes 6291460
  587.0 54.1 %collective-permute-start.4 = (f32[1024,1024]{1,0:T(8,128)}, f32[1024,1024]{1,0:T(8,128)}, u32[]{:S(2)}, u32[]{:S(2)}) collective-permute-start(f32[1024,1024]{1,0:T(8,128)} %copy.46), channel_id=1, source_target_pairs={{0,1},{1,0},{2,3},{3,2},{4,5},{5,4},{6,7},{7,6},{8,9},{9,8},{10,11... | collective-permute-start | bytes 12582920 | tf_op jit(solution)/shard_map/ppermute | solution.py:10
  587.0 182.6 %collective-permute-start.5 = (f32[1024,1024]{1,0:T(8,128)}, f32[1024,1024]{1,0:T(8,128)}, u32[]{:S(2)}, u32[]{:S(2)}) collective-permute-start(f32[1024,1024]{1,0:T(8,128)} %copy.47), channel_id=1, source_target_pairs={{0,2},{1,3},{2,0},{3,1},{4,6},{5,7},{6,4},{7,5},{8,10},{9,11},{10,... | collective-permute-start | bytes 12582920 | tf_op jit(solution)/shard_map/ppermute | solution.py:10
  587.0 184.1 %collective-permute-start.6 = (f32[1024,1024]{1,0:T(8,128)}, f32[1024,1024]{1,0:T(8,128)}, u32[]{:S(2)}, u32[]{:S(2)}) collective-permute-start(f32[1024,1024]{1,0:T(8,128)} %copy.48), channel_id=1, source_target_pairs={{0,4},{1,5},{2,6},{3,7},{4,0},{5,1},{6,2},{7,3},{8,12},{9,13},{10,... | collective-permute-start | bytes 12582920 | tf_op jit(solution)/shard_map/ppermute | solution.py:10
  613.2 16.7 %copy-start.19 = (bf16[1024,256]{1,0:T(8,128)(2,1)S(1)}, bf16[1024,256]{1,0:T(8,128)(2,1)}, u32[]{:S(2)}) copy-start(bf16[1024,256]{1,0:T(8,128)(2,1)} %get-tuple-element.23) | copy-start | bytes 1572868
  613.2 20.0 %copy-start.12 = (bf16[1024,256]{1,0:T(8,128)(2,1)S(1)}, bf16[1024,256]{1,0:T(8,128)(2,1)}, u32[]{:S(2)}) copy-start(bf16[1024,256]{1,0:T(8,128)(2,1)} %get-tuple-element.22) | copy-start | bytes 1572868
  629.9 141.2 %copy-start.3 = (f32[1024,1024]{1,0:T(8,128)S(1)}, f32[1024,1024]{1,0:T(8,128)}, u32[]{:S(2)}) copy-start(f32[1024,1024]{1,0:T(8,128)} %copy.43) | copy-start | bytes 12582916
  629.9 141.2 %copy-start.4 = (f32[1024,1024]{1,0:T(8,128)S(1)}, f32[1024,1024]{1,0:T(8,128)}, u32[]{:S(2)}) copy-start(f32[1024,1024]{1,0:T(8,128)} %copy.76) | copy-start | bytes 12582916
  629.9 141.2 %copy-start.5 = (f32[1024,1024]{1,0:T(8,128)S(1)}, f32[1024,1024]{1,0:T(8,128)}, u32[]{:S(2)}) copy-start(f32[1024,1024]{1,0:T(8,128)} %copy.75) | copy-start | bytes 12582916
  629.9 141.2 %copy-start.14 = (bf16[1,1024,256]{2,1,0:T(8,128)(2,1)S(1)}, bf16[1,1024,256]{2,1,0:T(8,128)(2,1)}, u32[]{:S(2)}) copy-start(bf16[1,1024,256]{2,1,0:T(8,128)(2,1)} %param.14) | copy-start | bytes 1572868
  633.3 146.0 %copy-start.1 = (bf16[1,4096,256]{2,1,0:T(8,128)(2,1)S(1)}, bf16[1,4096,256]{2,1,0:T(8,128)(2,1)}, u32[]{:S(2)}) copy-start(bf16[1,4096,256]{2,1,0:T(8,128)(2,1)} %param.16) | copy-start | bytes 6291460
  (6 other events, 27.0 us)
where the time goes:
time: 790 us; the launch traced here: 780 us
  local copies, waits for them, and re-layouts  255 us (32%)
  blocking collectives  212 us (27%)
  matrix products  156 us (20%)
  waiting for transfers between devices  140 us (18%)
  starting transfers between devices  15 us (2%)
    psum x1, blocking collectives, body(): lax.psum(jnp.dot(upstream, right_two[0].T, preferred_element_type=jnp.flo...  141 us
    ppermute x9, waiting for transfers between devices, swapped(): return lax.ppermute(value, axis, pairs)  140 us
    psum x1, blocking collectives, body(): lax.psum(jnp.dot(hidden_grad, right_one[0].T, preferred_element_type=jnp....  71.4 us
    unnamed x54, local copies, waits for them, and re-layouts  45.5 us
    reshape x2, local copies, waits for them, and re-layouts, body(): hidden_grad.reshape(row_count, count_in, group_size, block_size)  28.3 us
    dot_general x1, matrix products, body(): jnp.einsum('tcje,ktcb->cjkeb', activ_view, grad_view, preferred_element_t...  23.2 us
    dot_general x1, matrix products, body(): jnp.einsum('ktcb,cjkeb->tcje', grad_view, second_view, preferred_element_...  23.1 us
    dot_general x1, matrix products, body(): jnp.einsum('ktcb,tcje->cjkbe', input_view, hidden_view, preferred_element...  21.9 us
  transfers between devices with their start and end apart: 10, of which 3 were waited for; matrix products, arithmetic and copies ran while one was open for 20% of the time, Pallas kernels for 0%

commit v1 on v0

v1 whole, which is shorter than its diff:
```python
import functools

import jax
import jax.numpy as jnp
from jax import lax
from jax.experimental import pallas as pl
from jax.experimental.pallas import tpu as pltpu
from jax.sharding import PartitionSpec as P

CHUNKS = 2
BF16 = jnp.bfloat16
F32 = jnp.float32


def swapped(value, bit):
    pairs = [(source, source ^ (1 << bit)) for source in range(lax.axis_size("tensor"))]
    return lax.ppermute(value, "tensor", pairs)


def shifted(value):
    peers = lax.axis_size("section")
    return lax.ppermute(value, "section", [(i, (i - 1) % peers) for i in range(peers)])


def tree_sum(value):
    bits = lax.axis_size("tensor").bit_length() - 1
    place = lax.axis_index("tensor")
    for bit in range(bits - 1):
        half = value.shape[0] // 2
        mine = (place >> bit) & 1
        keep = lax.dynamic_slice_in_dim(value, mine * half, half)
        give = lax.dynamic_slice_in_dim(value, (1 - mine) * half, half)
        value = keep + swapped(give.astype(BF16), bit).astype(F32)
    value = (value + swapped(value.astype(BF16), bits - 1).astype(F32)).astype(BF16)
    for bit in reversed(range(bits - 1)):
        mine = (place >> bit) & 1
        other = swapped(value, bit)
        first = jnp.where(mine == 0, value, other)
        second = jnp.where(mine == 0, other, value)
        value = jnp.concatenate([first, second])
    return value


def nt(left, right):
    return lax.dot_general(left, right, (((1,), (1,)), ((), ())), preferred_element_type=F32)


def nn(left, right):
    return jnp.dot(left, right, preferred_element_type=F32)


def wide(parts):
    return parts[0] if len(parts) == 1 else jnp.concatenate(parts, axis=1)


def slope_of(values):
    normal_cdf = 0.5 * (1.0 + lax.erf(values * 0.7071067811865476))
    density = jnp.exp(-0.5 * values * values) * 0.3989422804014327
    return normal_cdf + values * density


def params(flops, moved, steps):
    return dict(
        cost_estimate=pl.CostEstimate(flops=flops, bytes_accessed=moved, transcendentals=0),
        compiler_params=pltpu.CompilerParams(
            dimension_semantics=("arbitrary",) * steps, vmem_limit_bytes=56 * 2**20
        ),
    )


def hidden_kernel(links, late, group, *refs):
    ups, refs = refs[:links], refs[links:]
    proj, refs = refs[0], refs[1:]
    seconds, refs = refs[:links], refs[links:]
    left_two, preact, right_one, refs = refs[0], refs[1], refs[2], refs[3:]
    firsts, refs = refs[:late], refs[late:]
    hidden, refs = refs[0], refs[1:]
    parts, refs = refs[:late], refs[late:]
    rank, up_all, hid_all = refs
    c, j = pl.program_id(0), pl.program_id(1)
    size = hidden.shape[1]

    @pl.when(j == 0)
    def _():
        for k in range(links):
            up_all[:, k * size : (k + 1) * size] = ups[k][...]
        up_all[:, links * size :] = proj[...]

    weights = wide([ref[...] for ref in seconds] + [left_two[...]])
    grad = nt(up_all[...], weights)
    hid = (grad * slope_of(preact[...].astype(F32))).astype(BF16)
    hidden[...] = hid
    hid_all[:, pl.ds(pl.multiple_of(j * size, size), size)] = hid

    @pl.when(j == group - 1)
    def _():
        group_grad = hid_all[...]
        for ref, part in zip(firsts, parts):
            part[...] = nt(group_grad, wide([ref[g] for g in range(group)])).astype(BF16)
        term = nt(group_grad, right_one[...])

        @pl.when(c == 0)
        def _():
            rank[...] = term

        @pl.when(c > 0)
        def _():
            rank[...] += term


def hidden_call(ups, flips, proj, second, left_two, preact, right_one, first, late_from, chunk):
    rows = ups[0].shape[0]
    _, hid_count, links, size, _ = first.shape
    count_in = ups[0].shape[1] // size
    group = hid_count // count_in
    rank = proj.shape[1]
    late = links - late_from
    in_specs = [
        pl.BlockSpec((rows, size), lambda c, j, flip=flip: (0, c ^ flip)) for flip in flips
    ]
    in_specs.append(pl.BlockSpec((rows, rank), lambda c, j: (chunk, 0)))
    in_specs += [
        pl.BlockSpec((None, None, None, size, size), lambda c, j, k=k: (0, c * group + j, k, 0, 0))
        for k in range(links)
    ]
    in_specs.append(pl.BlockSpec((None, size, rank), lambda c, j: (0, c * group + j, 0)))
    in_specs.append(pl.BlockSpec((None, rows, size), lambda c, j: (0, chunk, c * group + j)))
    in_specs.append(pl.BlockSpec((None, rank, group * size), lambda c, j: (0, 0, c)))
    in_specs += [
        pl.BlockSpec((None, group, None, size, size), lambda c, j, k=k: (0, c, k, 0, 0))
        for k in range(late_from, links)
    ]
    out_specs = [pl.BlockSpec((rows, size), lambda c, j: (0, c * group + j))]
    out_specs += [pl.BlockSpec((rows, size), lambda c, j: (0, c))] * late
    out_specs.append(pl.BlockSpec((rows, rank), lambda c, j: (0, 0)))
    width = hid_count * size
    out_shape = [jax.ShapeDtypeStruct((rows, width), BF16)]
    out_shape += [jax.ShapeDtypeStruct((rows, count_in * size), BF16)] * late
    out_shape.append(jax.ShapeDtypeStruct((rows, rank), F32))
    flops = 2 * rows * width * (size * links + rank * 2 + size * late)
    moved = 2 * width * (2 * rows + size * (links + late) + 2 * rank)
    return pl.pallas_call(
        functools.partial(hidden_kernel, links, late, group),
        grid=(count_in, group),
        in_specs=in_specs,
        out_specs=out_specs,
        out_shape=out_shape,
        scratch_shapes=[
            pltpu.VMEM((rows, links * size + rank), BF16),
            pltpu.VMEM((rows, group * size), BF16),
        ],
        name="hidden_grad",
        **params(flops, moved, 2),
    )(
        *ups, proj, *[second] * links, left_two, preact, right_one, *[first] * late
    )


def near_kernel(near, group, hid, *refs):
    weights, refs = refs[0], refs[1:]
    far_weights, rank, left_one, base, far, total = refs
    kk = pl.program_id(1)
    term = nt(hid[...], wide([weights[g] for g in range(group)]))

    @pl.when(kk == 0)
    def _():
        total[...] = term + nt(rank[...], left_one[...])
        far[...] = nt(hid[...], wide([far_weights[g] for g in range(group)])).astype(BF16)

    @pl.when(kk > 0)
    def _():
        total[...] += term

    @pl.when(kk == near - 1)
    def _():
        base[...] = total[...]


def near_call(hidden, first, rank, left_one, near, chunk):
    rows = hidden.shape[0]
    _, hid_count, links, size, _ = first.shape
    count_in = left_one.shape[1] // size
    group = hid_count // count_in
    ranks = rank.shape[1]

    def mate(c, kk):
        return c ^ ((1 << kk) >> 1)

    width = count_in * size
    return pl.pallas_call(
        functools.partial(near_kernel, near, group),
        grid=(count_in, near),
        in_specs=[
            pl.BlockSpec((rows, group * size), lambda c, kk: (0, mate(c, kk))),
            pl.BlockSpec(
                (None, group, None, size, size), lambda c, kk: (0, mate(c, kk), kk, 0, 0)
            ),
            pl.BlockSpec((None, group, None, size, size), lambda c, kk: (0, c, near, 0, 0)),
            pl.BlockSpec((rows, ranks), lambda c, kk: (chunk, 0)),
            pl.BlockSpec((None, size, ranks), lambda c, kk: (0, c, 0)),
        ],
        out_specs=[
            pl.BlockSpec((rows, size), lambda c, kk: (0, c)),
            pl.BlockSpec((rows, size), lambda c, kk: (0, c)),
        ],
        out_shape=[
            jax.ShapeDtypeStruct((rows, width), F32),
            jax.ShapeDtypeStruct((rows, width), BF16),
        ],
        scratch_shapes=[pltpu.VMEM((rows, size), F32)],
        name="near_parts",
        **params(
            2 * rows * width * (group * size * (near + 1) + ranks),
            2 * hid_count * size * (size * (near + 1) + rows * near) + 6 * rows * width,
            2,
        ),
    )(hidden, first, first, rank, left_one)


def second_kernel(links, chunks, rows, *refs):
    ups, refs = refs[: links * chunks], refs[links * chunks :]
    proj, act, out, left_two, up_all = refs
    size = act.shape[1]

    @pl.when(pl.program_id(1) == 0)
    def _():
        for m in range(chunks):
            for k in range(links):
                up_all[m * rows : (m + 1) * rows, k * size : (k + 1) * size] = ups[m * links + k][
                    ...
                ]
        up_all[:, links * size :] = proj[...]

    grads = nn(act[...].T, up_all[...]).astype(BF16)
    for k in range(links):
        out[k] = grads[:, k * size : (k + 1) * size]
    left_two[...] = grads[:, links * size :]


def second_call(ups, flips, proj, act, shape):
    chunks = len(ups)
    rows = ups[0][0].shape[0]
    tokens = rows * chunks
    _, hid_count, links, size, _ = shape
    count_in = ups[0][0].shape[1] // size
    group = hid_count // count_in
    rank = proj.shape[1]
    in_specs = [
        pl.BlockSpec((rows, size), lambda c, j, flip=flip: (0, c ^ flip))
        for _ in range(chunks)
        for flip in flips
    ]
    in_specs.append(pl.BlockSpec((tokens, rank), lambda c, j: (0, 0)))
    in_specs.append(pl.BlockSpec((tokens, size), lambda c, j: (0, c * group + j)))
    width = hid_count * size
    return pl.pallas_call(
        functools.partial(second_kernel, links, chunks, rows),
        grid=(count_in, group),
        in_specs=in_specs,
        out_specs=[
            pl.BlockSpec(
                (None, None, links, size, size), lambda c, j: (0, c * group + j, 0, 0, 0)
            ),
            pl.BlockSpec((None, size, rank), lambda c, j: (0, c * group + j, 0)),
        ],
        out_shape=[
            jax.ShapeDtypeStruct(shape, BF16),
            jax.ShapeDtypeStruct((1, width, rank), BF16),
        ],
        scratch_shapes=[pltpu.VMEM((tokens, links * size + rank), BF16)],
        name="second_grad",
        **params(
            2 * tokens * width * (links * size + rank),
            2 * width * (tokens + links * size + rank),
            2,
        ),
    )(*[up for chunk in ups for up in chunk], proj, act)


def first_kernel(links, chunks, rows, *refs):
    ins, refs = refs[: links * chunks], refs[links * chunks :]
    proj, refs = refs[0], refs[1:]
    hids, refs = refs[:chunks], refs[chunks:]
    out, right_one, in_all = refs
    size = hids[0].shape[1]

    @pl.when(pl.program_id(1) == 0)
    def _():
        for m in range(chunks):
            for k in range(links):
                in_all[k * size : (k + 1) * size, m * rows : (m + 1) * rows] = ins[m * links + k][
                    ...
                ].T
        in_all[links * size :, :] = proj[...].T

    hid = jnp.concatenate([ref[...] for ref in hids], axis=0)
    grads = nn(in_all[...], hid).astype(BF16)
    for k in range(links):
        out[k] = grads[k * size : (k + 1) * size]
    right_one[...] = grads[links * size :]


def first_call(ins, flips, proj, hids, shape):
    chunks = len(ins)
    rows = ins[0][0].shape[0]
    tokens = rows * chunks
    _, hid_count, links, size, _ = shape
    count_in = ins[0][0].shape[1] // size
    group = hid_count // count_in
    rank = proj.shape[1]
    in_specs = [
        pl.BlockSpec((rows, size), lambda c, j, flip=flip: (0, c ^ flip))
        for _ in range(chunks)
        for flip in flips
    ]
    in_specs.append(pl.BlockSpec((tokens, rank), lambda c, j: (0, 0)))
    in_specs += [pl.BlockSpec((rows, size), lambda c, j: (0, c * group + j))] * chunks
    width = hid_count * size
    return pl.pallas_call(
        functools.partial(first_kernel, links, chunks, rows),
        grid=(count_in, group),
        in_specs=in_specs,
        out_specs=[
            pl.BlockSpec(
                (None, None, links, size, size), lambda c, j: (0, c * group + j, 0, 0, 0)
            ),
            pl.BlockSpec((None, rank, size), lambda c, j: (0, 0, c * group + j)),
        ],
        out_shape=[
            jax.ShapeDtypeStruct(shape, BF16),
            jax.ShapeDtypeStruct((1, rank, width), BF16),
        ],
        scratch_shapes=[pltpu.VMEM((links * size + rank, tokens), BF16)],
        name="first_grad",
        **params(
            2 * tokens * width * (links * size + rank),
            2 * width * (tokens + links * size + rank),
            2,
        ),
    )(*[value for chunk in ins for value in chunk], proj, *hids)


def body(
    inputs, preact, handoff, first_blocks, second_blocks, left_one, right_one, left_two, right_two
):
    shape = first_blocks.shape
    links, size = shape[2], shape[-1]
    tokens, feats = inputs.shape[1:]
    count_in = feats // size
    near = count_in.bit_length()
    flips = [(1 << k) >> 1 if k < near else 0 for k in range(links)]
    rows = tokens // CHUNKS
    spans = [slice(m * rows, (m + 1) * rows) for m in range(CHUNKS)]

    def spread(value):
        return [value] * near + [swapped(value, k - near) for k in range(near, links)]

    upstream = [shifted(handoff[0, span]) for span in spans]
    in_parts = [inputs[0, span] for span in spans]
    in_sets = [spread(in_parts[0])]
    up_sets = [spread(value) for value in upstream]
    for m in range(1, CHUNKS):
        value, _ = lax.optimization_barrier((in_parts[m], up_sets[m - 1][-1]))
        sets = spread(value)
        in_sets.append([in_parts[m]] * near + sets[near:])

    values = preact[0].astype(F32)
    act = (values * (0.5 * (1.0 + lax.erf(values * 0.7071067811865476)))).astype(BF16)
    early = jnp.concatenate([nn(inputs[0], left_one[0]), nn(act, left_two[0])], axis=1)
    early = tree_sum(early)
    ranks = left_one.shape[2]
    proj_in, proj_act = early[:, :ranks], early[:, ranks:]
    proj_grad = tree_sum(
        jnp.concatenate([nt(value, right_two[0]) for value in upstream], axis=0)
    )

    hids, far, back = [], [], []
    for m in range(CHUNKS):
        hid, *parts, rank = hidden_call(
            up_sets[m],
            flips,
            proj_grad,
            second_blocks,
            left_two,
            preact,
            right_one,
            first_blocks,
            near + 1,
            m,
        )
        hids.append(hid)
        back.append(rank)
        far.append([swapped(part, k + 1) for k, part in enumerate(parts)])
    back_rank = tree_sum(jnp.concatenate(back, axis=0))

    second_grad, lefttwo_grad = second_call(up_sets, flips, proj_grad, act, shape)
    first_grad, rightone_grad = first_call(in_sets, flips, proj_in, hids, shape)
    leftone_grad = nn(inputs[0].T, back_rank).astype(BF16)[None]
    righttwo_grad = nn(proj_act.T, jnp.concatenate(upstream, axis=0)).astype(BF16)[None]
    input_grad = []
    for m in range(CHUNKS):
        base, beside = near_call(hids[m], first_blocks, back_rank, left_one, near, m)
        total = base + swapped(beside, 0).astype(F32)
        for part in far[m]:
            total = total + part.astype(F32)
        input_grad.append(total.astype(BF16))
    return (
        jnp.concatenate(input_grad, axis=0)[None],
        first_grad,
        second_grad,
        leftone_grad,
        rightone_grad,
        lefttwo_grad,
        righttwo_grad,
    )


def solution(mesh):
    by_feature = P("section", None, "tensor")
    by_block = P("section", "tensor", None, None, None)
    by_row = P("section", "tensor", None)
    in_specs = (
        by_feature,
        by_feature,
        by_feature,
        by_block,
        by_block,
        by_row,
        by_feature,
        by_row,
        by_feature,
    )
    out_specs = (
        by_feature,
        by_block,
        by_block,
        by_row,
        by_feature,
        by_row,
        by_feature,
    )
    return jax.shard_map(body, mesh=mesh, in_specs=in_specs, out_specs=out_specs, check_vma=False)
```

time: 790 us -> 425 us (0.54); the launches traced: 780 us -> 423 us
  local copies, waits for them, and re-layouts: 255 us -> 10.8 us
  blocking collectives: 212 us -> 0 us
  matrix products: 156 us -> 14.3 us
  Pallas kernels: 0 us -> 141 us
  waiting for transfers between devices: 140 us -> 192 us
  other arithmetic: 0 us -> 26.3 us
  starting transfers between devices: 15 us -> 37 us
    psum x2 -> x0, blocking collectives: 212 us -> none  [the longest x1 141 us: body(): lax.psum(jnp.dot(upstream, right_two[0].T, preferred_element_type=jnp.flo...]
    dot_general x14 -> x6, matrix products: 156 us -> 14.3 us  [the longest x4 13.4 us: nn(): return jnp.dot(left, right, preferred_element_type=F32)]
    pallas_call x0 -> x6, Pallas kernels: none -> 141 us  [the longest x2 49.3 us: hidden_call(): pl.pallas_call(functools.partial(hidden_kernel, links, late, group), grid...]
    reshape x6 -> x0, local copies, waits for them, and re-layouts: 60.5 us -> none  [the longest x2 28.3 us: body(): hidden_grad.reshape(row_count, count_in, group_size, block_size)]
    ppermute x10 -> x35, waiting for transfers between devices: 140 us -> 192 us  [the longest x33 159 us: swapped(): return lax.ppermute(value, 'tensor', pairs)]
    another operation x14 -> x0, local copies, waits for them, and re-layouts: 50.7 us -> none  [the longest x6 21.9 us: body(): jnp.stack(partner_sets(own_inputs, count_in, block_size, link_count, swap...]
    unnamed x54, local copies, waits for them, and re-layouts: 45.5 us -> 6.04 us
    convert_element_type x2 -> x4, local copies, waits for them, and re-layouts: 36.6 us -> 0.11 us  [tree_sum(): value = keep + swapped(give.astype(BF16), bit).astype(F32)]
  transfers between devices with their start and end apart: 10 -> 35, of which waited for: 3 -> 14; matrix products, arithmetic and copies ran while one was open for 20% -> 10% of each run, Pallas kernels for 0% -> 33%
where the time goes in v1:
time: 425 us; the launch traced here: 423 us
  waiting for transfers between devices  192 us (45%)
  Pallas kernels  141 us (33%)
  starting transfers between devices  37 us (9%)
  other arithmetic  26.3 us (6%)
  matrix products  14.3 us (3%)
  local copies, waits for them, and re-layouts  10.8 us (3%)
    ppermute x33, waiting for transfers between devices, swapped(): return lax.ppermute(value, 'tensor', pairs)  159 us
    pallas_call x2, Pallas kernels, hidden_call(): pl.pallas_call(functools.partial(hidden_kernel, links, late, group), grid...  49.3 us
    ppermute x2, waiting for transfers between devices, shifted(): lax.ppermute(value, 'section', [(i, (i - 1) % peers) for i in range(peers)])  33 us
    ppermute x33, starting transfers between devices, swapped(): return lax.ppermute(value, 'tensor', pairs)  32.5 us
    pallas_call x2, Pallas kernels, near_call(): pl.pallas_call(functools.partial(near_kernel, near, group), grid=(count_i...  32.2 us
    pallas_call x1, Pallas kernels, first_call(): pl.pallas_call(functools.partial(first_kernel, links, chunks, rows), grid...  30.9 us
    pallas_call x1, Pallas kernels, second_call(): pl.pallas_call(functools.partial(second_kernel, links, chunks, rows), gri...  28.6 us
    dot_general x4, matrix products, nn(): return jnp.dot(left, right, preferred_element_type=F32)  13.4 us
  transfers between devices with their start and end apart: 35, of which 14 were waited for; matrix products, arithmetic and copies ran while one was open for 10% of the time, Pallas kernels for 33%

profile of v1, /device:TPU:0, one launch (start us, length us, event | category | flops | bytes accessed | tf_op | source)
XLA Modules:
  0.0 422.7 jit_solution(13491840353280754560)
XLA Ops:
  0.7 3.1 slice_bitcast_fusion.3
  3.8 3.9 collective-permute-start
  10.7 8.7 %fusion.11 = f32[1024,256]{1,0:T(8,128)S(1)} fusion(bf16[1,1024,4096]{2,1,0:T(8,128)(2,1)} %refs_14_.3, bf16[1,4096,256]{2,1,0:T(8,128)(2,1)S(1)} %copy-done.6), kind=kOutput, calls=%fused_computation.14 | convolution fusion | flops 2172649472 | bytes 11534336 | tf_op jit(solution)/shard_map/dot_general | solution.py:49
  19.4 12.2 %collective-permute-done.refs_0_.refs_1_.refs_2_ = bf16[512,1024]{1,0:T(8,128)(2,1)S(1)} collective-permute-done((bf16[512,1024]{1,0:T(8,128)(2,1)}, bf16[512,1024]{1,0:T(8,128)(2,1)S(1)}, u32[]{:S(2)}, u32[]{:S(2)}) %collective-permute-start) | collective-permute-done | bytes 1048608 | tf_op jit(solution)/shard_map/ppermute | solution.py:22
  32.0 20.8 %collective-permute-done.4.refs_0_.refs_1_.refs_2_.refs_6_.refs_7_.refs_8_ = bf16[512,1024]{1,0:T(8,128)(2,1)S(1)} collective-permute-done((bf16[512,1024]{1,0:T(8,128)(2,1)}, bf16[512,1024]{1,0:T(8,128)(2,1)S(1)}, u32[]{:S(2)}, u32[]{:S(2)}) %collective-permute-start.4) | collective-permute-done | bytes 1048608 | tf_op jit(solution)/shard_map/ppermute | solution.py:22
  67.5 4.2 collective-permute-done.7
  83.4 30.3 %collective-permute-done.32 = bf16[256,512]{1,0:T(8,128)(2,1)S(1)} collective-permute-done((bf16[256,512]{1,0:T(8,128)(2,1)}, bf16[256,512]{1,0:T(8,128)(2,1)S(1)}, u32[]{:S(2)}, u32[]{:S(2)}) %collective-permute-start.32) | collective-permute-done | bytes 262176 | tf_op jit(solution)/shard_map/ppermute | solution.py:17
  114.8 3.7 collective-permute-start.2
  119.5 39.2 %collective-permute-done.12.refs_5_.refs_11_ = bf16[512,1024]{1,0:T(8,128)(2,1)} collective-permute-done((bf16[512,1024]{1,0:T(8,128)(2,1)S(1)}, bf16[512,1024]{1,0:T(8,128)(2,1)}, u32[]{:S(2)}, u32[]{:S(2)}) %collective-permute-start.12) | collective-permute-done | bytes 1048608 | tf_op jit(solution)/shard_map/ppermute | solution.py:17
  159.6 3.6 collective-permute-start.25
  163.2 24.6 %hidden_grad.3 = (bf16[512,4096]{1,0:T(8,128)(2,1)}, bf16[512,1024]{1,0:T(8,128)(2,1)}, bf16[512,1024]{1,0:T(8,128)(2,1)}, f32[512,256]{1,0:T(8,128)}) custom-call(bf16[512,1024]{1,0:T(8,128)(2,1)} %copy-done.4, bf16[512,1024]{1,0:T(8,128)(2,1)} %copy-done.4, bf16[512,1024]{1,0:T(8,128)(2,1)} %copy-done.4, ...), custom_call_target="tpu_custom_call" | custom-call | flops 10737418240 | bytes 29360128 | tf_op jit(solution)/shard_map/hidden_grad/pallas_call | solution.py:142
  187.8 15.8 %collective-permute-done.3.refs_5_ = bf16[512,1024]{1,0:T(8,128)(2,1)S(1)} collective-permute-done((bf16[512,1024]{1,0:T(8,128)(2,1)S(1)}, bf16[512,1024]{1,0:T(8,128)(2,1)S(1)}, u32[]{:S(2)}, u32[]{:S(2)}) %collective-permute-start.3) | collective-permute-done | bytes 1048608 | tf_op jit(solution)/shard_map/ppermute | solution.py:17
  206.0 24.6 %hidden_grad.2 = (bf16[512,4096]{1,0:T(8,128)(2,1)}, bf16[512,1024]{1,0:T(8,128)(2,1)}, bf16[512,1024]{1,0:T(8,128)(2,1)}, f32[512,256]{1,0:T(8,128)}) custom-call(bf16[512,1024]{1,0:T(8,128)(2,1)} %copy-done.2, bf16[512,1024]{1,0:T(8,128)(2,1)} %copy-done.2, bf16[512,1024]{1,0:T(8,128)(2,1)} %copy-done.2, bf16[512,1024]{1,0:T(8,128)(2,1)} %copy-done.22, ...), custom_call_target="tpu_custom_call" | custom-call | flops 10737418240 | bytes 29360128 | tf_op jit(solution)/shard_map/hidden_grad/pallas_call | solution.py:142
  234.3 10.1 %fusion.5.refs_13_ = bf16[1024,4096]{1,0:T(8,128)(2,1)} fusion(bf16[1,1024,4096]{2,1,0:T(8,128)(2,1)} %refs_14_.3), kind=kLoop, calls=%fused_computation.8 | loop fusion | flops 25165824 | bytes 16777216 | tf_op jit(solution)/shard_map/convert_element_type | solution.py:368
  244.5 2.9 collective-permute-start.15
  247.6 6.1 %collective-permute-done.15 = bf16[256,256]{1,0:T(8,128)(2,1)S(1)} collective-permute-done((bf16[256,256]{1,0:T(8,128)(2,1)S(1)}, bf16[256,256]{1,0:T(8,128)(2,1)S(1)}, u32[]{:S(2)}, u32[]{:S(2)}) %collective-permute-start.15) | collective-permute-done | bytes 131104 | tf_op jit(solution)/shard_map/ppermute | solution.py:17
  256.3 3.4 collective-permute-start.29
  259.8 28.6 %second_grad.1 = (bf16[1,16,6,256,256]{4,3,2,1,0:T(8,128)(2,1)}, bf16[1,4096,256]{2,1,0:T(8,128)(2,1)}) custom-call(bf16[512,1024]{1,0:T(8,128)(2,1)} %copy-done.2, bf16[512,1024]{1,0:T(8,128)(2,1)} %copy-done.2, bf16[512,1024]{1,0:T(8,128)(2,1)} %copy-done.2, bf16[512,1024]{1,0:T(8,128)(2,1)} %copy-done.22, bf16[512,1024]{1,0:T(8,128)(2,1)} %copy-done.21, ...), custom_call_target="tpu_custom_call" | custom-call | flops 15032385536 | bytes 23068672 | tf_op jit(solution)/shard_map/second_grad/pallas_call | solution.py:256
  294.3 16.0 %near_parts.3 = (f32[512,1024]{1,0:T(8,128)}, bf16[512,1024]{1,0:T(8,128)(2,1)}) custom-call(bf16[512,4096]{1,0:T(8,128)(2,1)} %get-tuple-element.31.hid.refs_14_, bf16[1,16,6,256,256]{4,3,2,1,0:T(8,128)(2,1)} %refs_1_.3, bf16[1,16,6,256,256]{4,3,2,1,0:T(8,128)(2,1)} %refs_1_.3, bf16[1024,256]{1,0:T(8,128)(2,1)} %pad_maximum_fusion.3.refs_2_, ...), custom_call_target="tpu_custom_call" | custom-call | flops 4563402752 | bytes 24117248 | tf_op jit(solution)/shard_map/near_parts/pallas_call | solution.py:190
  310.3 16.1 %near_parts.2 = (f32[512,1024]{1,0:T(8,128)}, bf16[512,1024]{1,0:T(8,128)(2,1)}) custom-call(bf16[512,4096]{1,0:T(8,128)(2,1)} %get-tuple-element.24.hid.refs_13_, bf16[1,16,6,256,256]{4,3,2,1,0:T(8,128)(2,1)} %refs_1_.3, bf16[1,16,6,256,256]{4,3,2,1,0:T(8,128)(2,1)} %refs_1_.3, bf16[1024,256]{1,0:T(8,128)(2,1)} %pad_maximum_fusion.3.refs_2_, ...), custom_call_target="tpu_custom_call" | custom-call | flops 4563402752 | bytes 24117248 | tf_op jit(solution)/shard_map/near_parts/pallas_call | solution.py:190
  329.8 25.9 %collective-permute-done.22 = bf16[512,1024]{1,0:T(8,128)(2,1)S(1)} collective-permute-done((bf16[512,1024]{1,0:T(8,128)(2,1)}, bf16[512,1024]{1,0:T(8,128)(2,1)S(1)}, u32[]{:S(2)}, u32[]{:S(2)}) %collective-permute-start.22) | collective-permute-done | bytes 1048608 | tf_op jit(solution)/shard_map/ppermute | solution.py:17
  355.7 30.9 %first_grad.1 = (bf16[1,16,6,256,256]{4,3,2,1,0:T(8,128)(2,1)}, bf16[1,256,4096]{2,1,0:T(8,128)(2,1)}) custom-call(bf16[512,1024]{1,0:T(8,128)(2,1)} %get-tuple-element.49.refs_0_.refs_1_.refs_2_, bf16[512,1024]{1,0:T(8,128)(2,1)} %get-tuple-element.49.refs_0_.refs_1_.refs_2_, bf16[512,1024]{1,0:T(8,128)(2,1)} %get-tuple-element.49.refs_0_.refs_1_.refs_2_, ...), custom_call_target="tpu_custom_call" | custom-call | flops 15032385536 | bytes 23068672 | tf_op jit(solution)/shard_map/first_grad/pallas_call | solution.py:319
  388.7 11.8 %collective-permute-done.19 = bf16[512,1024]{1,0:T(8,128)(2,1)S(1)} collective-permute-done((bf16[512,1024]{1,0:T(8,128)(2,1)}, bf16[512,1024]{1,0:T(8,128)(2,1)S(1)}, u32[]{:S(2)}, u32[]{:S(2)}) %collective-permute-start.19) | collective-permute-done | bytes 1048608 | tf_op jit(solution)/shard_map/ppermute | solution.py:17
  400.5 19.8 %collective-permute-done.20 = bf16[512,1024]{1,0:T(8,128)(2,1)S(1)} collective-permute-done((bf16[512,1024]{1,0:T(8,128)(2,1)}, bf16[512,1024]{1,0:T(8,128)(2,1)S(1)}, u32[]{:S(2)}, u32[]{:S(2)}) %collective-permute-start.20) | collective-permute-done | bytes 1048608 | tf_op jit(solution)/shard_map/ppermute | solution.py:17
  (146 shorter events, 55.2 us)
Async XLA Ops:
  3.8 27.8 %collective-permute-start = (bf16[512,1024]{1,0:T(8,128)(2,1)}, bf16[512,1024]{1,0:T(8,128)(2,1)S(1)}, u32[]{:S(2)}, u32[]{:S(2)}) collective-permute-start(bf16[512,1024]{1,0:T(8,128)(2,1)} %get-tuple-element.50), channel_id=1, source_target_pairs={{0,24},{8,0},{16,8},{24,16},{1,25},{9,1},{17,9},{25,17},{2,26},{10... | collective-permute-start | bytes 3145736 | tf_op jit(solution)/shard_map/ppermute | solution.py:22
  7.7 45.2 %collective-permute-start.4 = (bf16[512,1024]{1,0:T(8,128)(2,1)}, bf16[512,1024]{1,0:T(8,128)(2,1)S(1)}, u32[]{:S(2)}, u32[]{:S(2)}) collective-permute-start(bf16[512,1024]{1,0:T(8,128)(2,1)} %get-tuple-element.51), channel_id=1, source_target_pairs={{0,24},{8,0},{16,8},{24,16},{1,25},{9,1},{17,9},{25,17},{2,26},{10... | collective-permute-start | bytes 3145736 | tf_op jit(solution)/shard_map/ppermute | solution.py:22
  77.5 36.1 %collective-permute-start.32 = (bf16[256,512]{1,0:T(8,128)(2,1)}, bf16[256,512]{1,0:T(8,128)(2,1)S(1)}, u32[]{:S(2)}, u32[]{:S(2)}) collective-permute-start(bf16[256,512]{1,0:T(8,128)(2,1)} %fusion.49), channel_id=1, source_target_pairs={{0,4},{1,5},{2,6},{3,7},{4,0},{5,1},{6,2},{7,3},{8,12},{9,13},{10,... | collective-permute-start | bytes 786440 | tf_op jit(solution)/shard_map/ppermute | solution.py:17
  78.7 80.0 %collective-permute-start.12 = (bf16[512,1024]{1,0:T(8,128)(2,1)S(1)}, bf16[512,1024]{1,0:T(8,128)(2,1)}, u32[]{:S(2)}, u32[]{:S(2)}) collective-permute-start(bf16[512,1024]{1,0:T(8,128)(2,1)S(1)} %collective-permute-done.4.refs_0_.refs_1_.refs_2_.refs_6_.refs_7_.refs_8_), channel_id=1, source_target_pairs={{0,4},{1,5},{2,6},{3,7},{4,0},{5,1},{6,2},{7,3},{8,12},{9,13},{10,... | collective-permute-start | bytes 3145736 | tf_op jit(solution)/shard_map/ppermute | solution.py:17
  80.4 79.1 %collective-permute-start.11 = (bf16[512,1024]{1,0:T(8,128)(2,1)S(1)}, bf16[512,1024]{1,0:T(8,128)(2,1)}, u32[]{:S(2)}, u32[]{:S(2)}) collective-permute-start(bf16[512,1024]{1,0:T(8,128)(2,1)S(1)} %collective-permute-done.4.refs_0_.refs_1_.refs_2_.refs_6_.refs_7_.refs_8_), channel_id=1, source_target_pairs={{0,2},{1,3},{2,0},{3,1},{4,6},{5,7},{6,4},{7,5},{8,10},{9,11},{10,... | collective-permute-start | bytes 3145736 | tf_op jit(solution)/shard_map/ppermute | solution.py:17
  81.3 78.3 %collective-permute-start.10 = (bf16[512,1024]{1,0:T(8,128)(2,1)S(1)}, bf16[512,1024]{1,0:T(8,128)(2,1)}, u32[]{:S(2)}, u32[]{:S(2)}) collective-permute-start(bf16[512,1024]{1,0:T(8,128)(2,1)S(1)} %collective-permute-done.4.refs_0_.refs_1_.refs_2_.refs_6_.refs_7_.refs_8_), channel_id=1, source_target_pairs={{0,1},{1,0},{2,3},{3,2},{4,5},{5,4},{6,7},{7,6},{8,9},{9,8},{10,11... | collective-permute-start | bytes 3145736 | tf_op jit(solution)/shard_map/ppermute | solution.py:17
  81.3 33.5 %collective-permute-start.9 = (bf16[512,256]{1,0:T(8,128)(2,1)S(1)}, bf16[512,256]{1,0:T(8,128)(2,1)}, u32[]{:S(2)}, u32[]{:S(2)}) collective-permute-start(bf16[512,256]{1,0:T(8,128)(2,1)S(1)} %pad_maximum_fusion.5), channel_id=1, source_target_pairs={{0,1},{1,0},{2,3},{3,2},{4,5},{5,4},{6,7},{7,6},{8,9},{9,8},{10,11... | collective-permute-start | bytes 786440 | tf_op jit(solution)/shard_map/ppermute | solution.py:17
  113.6 90.0 %collective-permute-start.3 = (bf16[512,1024]{1,0:T(8,128)(2,1)S(1)}, bf16[512,1024]{1,0:T(8,128)(2,1)S(1)}, u32[]{:S(2)}, u32[]{:S(2)}) collective-permute-start(bf16[512,1024]{1,0:T(8,128)(2,1)S(1)} %collective-permute-done.refs_0_.refs_1_.refs_2_), channel_id=1, source_target_pairs={{0,4},{1,5},{2,6},{3,7},{4,0},{5,1},{6,2},{7,3},{8,12},{9,13},{10,... | collective-permute-start | bytes 3145736 | tf_op jit(solution)/shard_map/ppermute | solution.py:17
  114.8 88.8 %collective-permute-start.2 = (bf16[512,1024]{1,0:T(8,128)(2,1)S(1)}, bf16[512,1024]{1,0:T(8,128)(2,1)S(1)}, u32[]{:S(2)}, u32[]{:S(2)}) collective-permute-start(bf16[512,1024]{1,0:T(8,128)(2,1)S(1)} %collective-permute-done.refs_0_.refs_1_.refs_2_), channel_id=1, source_target_pairs={{0,2},{1,3},{2,0},{3,1},{4,6},{5,7},{6,4},{7,5},{8,10},{9,11},{10,... | collective-permute-start | bytes 3145736 | tf_op jit(solution)/shard_map/ppermute | solution.py:17
  158.7 45.2 %collective-permute-start.1 = (bf16[512,1024]{1,0:T(8,128)(2,1)S(1)}, bf16[512,1024]{1,0:T(8,128)(2,1)S(1)}, u32[]{:S(2)}, u32[]{:S(2)}) collective-permute-start(bf16[512,1024]{1,0:T(8,128)(2,1)S(1)} %collective-permute-done.refs_0_.refs_1_.refs_2_), channel_id=1, source_target_pairs={{0,1},{1,0},{2,3},{3,2},{4,5},{5,4},{6,7},{7,6},{8,9},{9,8},{10,11... | collective-permute-start | bytes 3145736 | tf_op jit(solution)/shard_map/ppermute | solution.py:17
  159.6 129.0 %collective-permute-start.26 = (bf16[512,1024]{1,0:T(8,128)(2,1)}, bf16[512,1024]{1,0:T(8,128)(2,1)}, u32[]{:S(2)}, u32[]{:S(2)}) collective-permute-start(bf16[512,1024]{1,0:T(8,128)(2,1)} %get-tuple-element.49.refs_0_.refs_1_.refs_2_), channel_id=1, source_target_pairs={{0,4},{1,5},{2,6},{3,7},{4,0},{5,1},{6,2},{7,3},{8,12},{9,13},{10,... | collective-permute-start | bytes 3145736 | tf_op jit(solution)/shard_map/ppermute | solution.py:17
  159.6 129.4 %collective-permute-start.25 = (bf16[512,1024]{1,0:T(8,128)(2,1)}, bf16[512,1024]{1,0:T(8,128)(2,1)S(1)}, u32[]{:S(2)}, u32[]{:S(2)}) collective-permute-start(bf16[512,1024]{1,0:T(8,128)(2,1)} %get-tuple-element.49.refs_0_.refs_1_.refs_2_), channel_id=1, source_target_pairs={{0,2},{1,3},{2,0},{3,1},{4,6},{5,7},{6,4},{7,5},{8,10},{9,11},{10,... | collective-permute-start | bytes 3145736 | tf_op jit(solution)/shard_map/ppermute | solution.py:17
  203.6 122.8 %collective-permute-start.24 = (bf16[512,1024]{1,0:T(8,128)(2,1)}, bf16[512,1024]{1,0:T(8,128)(2,1)}, u32[]{:S(2)}, u32[]{:S(2)}) collective-permute-start(bf16[512,1024]{1,0:T(8,128)(2,1)} %get-tuple-element.49.refs_0_.refs_1_.refs_2_), channel_id=1, source_target_pairs={{0,1},{1,0},{2,3},{3,2},{4,5},{5,4},{6,7},{7,6},{8,9},{9,8},{10,11... | collective-permute-start | bytes 3145736 | tf_op jit(solution)/shard_map/ppermute | solution.py:17
  203.6 28.4 %collective-permute-start.33 = (bf16[256,512]{1,0:T(8,128)(2,1)S(1)}, bf16[256,512]{1,0:T(8,128)(2,1)S(1)}, u32[]{:S(2)}, u32[]{:S(2)}) collective-permute-start(bf16[256,512]{1,0:T(8,128)(2,1)S(1)} %add_convert_fusion.2), channel_id=1, source_target_pairs={{0,2},{1,3},{2,0},{3,1},{4,6},{5,7},{6,4},{7,5},{8,10},{9,11},{10,... | collective-permute-start | bytes 786440 | tf_op jit(solution)/shard_map/ppermute | solution.py:17
  256.3 71.1 %collective-permute-start.29 = (bf16[512,1024]{1,0:T(8,128)(2,1)S(1)}, bf16[512,1024]{1,0:T(8,128)(2,1)}, u32[]{:S(2)}, u32[]{:S(2)}) collective-permute-start(bf16[512,1024]{1,0:T(8,128)(2,1)S(1)} %copy-done.23), channel_id=1, source_target_pairs={{0,4},{1,5},{2,6},{3,7},{4,0},{5,1},{6,2},{7,3},{8,12},{9,13},{10,... | collective-permute-start | bytes 3145736 | tf_op jit(solution)/shard_map/ppermute | solution.py:17
  259.7 28.6 %collective-permute-start.17 = (bf16[512,256]{1,0:T(8,128)(2,1)S(1)}, bf16[512,256]{1,0:T(8,128)(2,1)S(1)}, u32[]{:S(2)}, u32[]{:S(2)}) collective-permute-start(bf16[512,256]{1,0:T(8,128)(2,1)S(1)} %pad_maximum_fusion.6), channel_id=1, source_target_pairs={{0,1},{1,0},{2,3},{3,2},{4,5},{5,4},{6,7},{7,6},{8,9},{9,8},{10,11... | collective-permute-start | bytes 786440 | tf_op jit(solution)/shard_map/ppermute | solution.py:17
  288.3 40.8 %collective-permute-start.28 = (bf16[512,1024]{1,0:T(8,128)(2,1)S(1)}, bf16[512,1024]{1,0:T(8,128)(2,1)}, u32[]{:S(2)}, u32[]{:S(2)}) collective-permute-start(bf16[512,1024]{1,0:T(8,128)(2,1)S(1)} %copy-done.23), channel_id=1, source_target_pairs={{0,2},{1,3},{2,0},{3,1},{4,6},{5,7},{6,4},{7,5},{8,10},{9,11},{10,... | collective-permute-start | bytes 3145736 | tf_op jit(solution)/shard_map/ppermute | solution.py:17
  288.6 41.2 %collective-permute-start.27 = (bf16[512,1024]{1,0:T(8,128)(2,1)S(1)}, bf16[512,1024]{1,0:T(8,128)(2,1)}, u32[]{:S(2)}, u32[]{:S(2)}) collective-permute-start(bf16[512,1024]{1,0:T(8,128)(2,1)S(1)} %copy-done.23), channel_id=1, source_target_pairs={{0,1},{1,0},{2,3},{3,2},{4,5},{5,4},{6,7},{7,6},{8,9},{9,8},{10,11... | collective-permute-start | bytes 3145736 | tf_op jit(solution)/shard_map/ppermute | solution.py:17
  290.0 65.7 %collective-permute-start.22 = (bf16[512,1024]{1,0:T(8,128)(2,1)}, bf16[512,1024]{1,0:T(8,128)(2,1)S(1)}, u32[]{:S(2)}, u32[]{:S(2)}) collective-permute-start(bf16[512,1024]{1,0:T(8,128)(2,1)} %get-tuple-element.34), channel_id=1, source_target_pairs={{0,2},{1,3},{2,0},{3,1},{4,6},{5,7},{6,4},{7,5},{8,10},{9,11},{10,... | collective-permute-start | bytes 3145736 | tf_op jit(solution)/shard_map/ppermute | solution.py:17
  326.5 60.1 %collective-permute-start.23 = (bf16[512,1024]{1,0:T(8,128)(2,1)}, bf16[512,1024]{1,0:T(8,128)(2,1)S(1)}, u32[]{:S(2)}, u32[]{:S(2)}) collective-permute-start(bf16[512,1024]{1,0:T(8,128)(2,1)} %get-tuple-element.35), channel_id=1, source_target_pairs={{0,4},{1,5},{2,6},{3,7},{4,0},{5,1},{6,2},{7,3},{8,12},{9,13},{10,... | collective-permute-start | bytes 3145736 | tf_op jit(solution)/shard_map/ppermute | solution.py:17
  327.4 73.2 %collective-permute-start.19 = (bf16[512,1024]{1,0:T(8,128)(2,1)}, bf16[512,1024]{1,0:T(8,128)(2,1)S(1)}, u32[]{:S(2)}, u32[]{:S(2)}) collective-permute-start(bf16[512,1024]{1,0:T(8,128)(2,1)} %get-tuple-element.29), channel_id=1, source_target_pairs={{0,2},{1,3},{2,0},{3,1},{4,6},{5,7},{6,4},{7,5},{8,10},{9,11},{10,... | collective-permute-start | bytes 3145736 | tf_op jit(solution)/shard_map/ppermute | solution.py:17
  329.1 91.3 %collective-permute-start.20 = (bf16[512,1024]{1,0:T(8,128)(2,1)}, bf16[512,1024]{1,0:T(8,128)(2,1)S(1)}, u32[]{:S(2)}, u32[]{:S(2)}) collective-permute-start(bf16[512,1024]{1,0:T(8,128)(2,1)} %get-tuple-element.30), channel_id=1, source_target_pairs={{0,4},{1,5},{2,6},{3,7},{4,0},{5,1},{6,2},{7,3},{8,12},{9,13},{10,... | collective-permute-start | bytes 3145736 | tf_op jit(solution)/shard_map/ppermute | solution.py:17
  329.8 56.8 %collective-permute-start.21 = (bf16[512,1024]{1,0:T(8,128)(2,1)}, bf16[512,1024]{1,0:T(8,128)(2,1)}, u32[]{:S(2)}, u32[]{:S(2)}) collective-permute-start(bf16[512,1024]{1,0:T(8,128)(2,1)} %get-tuple-element.33), channel_id=1, source_target_pairs={{0,1},{1,0},{2,3},{3,2},{4,5},{5,4},{6,7},{7,6},{8,9},{9,8},{10,11... | collective-permute-start | bytes 3145736 | tf_op jit(solution)/shard_map/ppermute | solution.py:17
  355.7 64.7 %collective-permute-start.18 = (bf16[512,1024]{1,0:T(8,128)(2,1)}, bf16[512,1024]{1,0:T(8,128)(2,1)S(1)}, u32[]{:S(2)}, u32[]{:S(2)}) collective-permute-start(bf16[512,1024]{1,0:T(8,128)(2,1)} %get-tuple-element.28), channel_id=1, source_target_pairs={{0,1},{1,0},{2,3},{3,2},{4,5},{5,4},{6,7},{7,6},{8,9},{9,8},{10,11... | collective-permute-start | bytes 3145736 | tf_op jit(solution)/shard_map/ppermute | solution.py:17
  (37 other events, 559.7 us)

commit v2 on v1

v2 whole, which is shorter than its diff:
```python
import functools

import jax
import jax.numpy as jnp
from jax import lax
from jax.experimental import pallas as pl
from jax.experimental.pallas import tpu as pltpu
from jax.sharding import PartitionSpec as P

CHUNKS = 2
BF16 = jnp.bfloat16
F32 = jnp.float32


def swapped(value, bit):
    pairs = [(source, source ^ (1 << bit)) for source in range(lax.axis_size("tensor"))]
    return lax.ppermute(value, "tensor", pairs)


def shifted(value):
    peers = lax.axis_size("section")
    return lax.ppermute(value, "section", [(i, (i - 1) % peers) for i in range(peers)])


def tree_sum(value):
    bits = lax.axis_size("tensor").bit_length() - 1
    place = lax.axis_index("tensor")
    for bit in range(bits - 1):
        half = value.shape[0] // 2
        mine = (place >> bit) & 1
        keep = lax.dynamic_slice_in_dim(value, mine * half, half)
        give = lax.dynamic_slice_in_dim(value, (1 - mine) * half, half)
        give = give if bit == 0 else give.astype(BF16)
        value = keep + swapped(give, bit).astype(F32)
    value = (value + swapped(value.astype(BF16), bits - 1).astype(F32)).astype(BF16)
    for bit in reversed(range(bits - 1)):
        mine = (place >> bit) & 1
        other = swapped(value, bit)
        first = jnp.where(mine == 0, value, other)
        second = jnp.where(mine == 0, other, value)
        value = jnp.concatenate([first, second])
    return value


def nt(left, right):
    return lax.dot_general(left, right, (((1,), (1,)), ((), ())), preferred_element_type=F32)


def nn(left, right):
    return jnp.dot(left, right, preferred_element_type=F32)


def wide(parts):
    return parts[0] if len(parts) == 1 else jnp.concatenate(parts, axis=1)


def after(value, *others):
    return lax.optimization_barrier((value, *others))[0]


def gate_kernel(strip, preact, left_two, act, slope, proj):
    def one(r, _):
        rows = pl.ds(pl.multiple_of(r * strip, strip), strip)
        values = preact[rows, :].astype(F32)
        normal_cdf = 0.5 * (1.0 + lax.erf(values * 0.7071067811865476))
        density = jnp.exp(-0.5 * values * values) * 0.3989422804014327
        act[rows, :] = (values * normal_cdf).astype(BF16)
        slope[rows, :] = normal_cdf + values * density
        return 0

    lax.fori_loop(0, preact.shape[0] // strip, one, 0)
    term = nn(act[...], left_two[...])

    @pl.when(pl.program_id(0) == 0)
    def _():
        proj[...] = term

    @pl.when(pl.program_id(0) > 0)
    def _():
        proj[...] += term


def gate_call(preact, left_two, size):
    _, tokens, width = preact.shape
    rank = left_two.shape[2]
    return pl.pallas_call(
        functools.partial(gate_kernel, min(64, tokens)),
        grid=(width // size,),
        in_specs=[
            pl.BlockSpec((None, tokens, size), lambda i: (0, 0, i)),
            pl.BlockSpec((None, size, rank), lambda i: (0, i, 0)),
        ],
        out_specs=[
            pl.BlockSpec((tokens, size), lambda i: (0, i)),
            pl.BlockSpec((tokens, size), lambda i: (0, i)),
            pl.BlockSpec((tokens, rank), lambda i: (0, 0)),
        ],
        out_shape=[
            jax.ShapeDtypeStruct((tokens, width), BF16),
            jax.ShapeDtypeStruct((tokens, width), F32),
            jax.ShapeDtypeStruct((tokens, rank), F32),
        ],
        name="gate",
        **params(1),
    )(preact, left_two)


def params(steps):
    return dict(
        cost_estimate=pl.CostEstimate(flops=1024, bytes_accessed=1024, transcendentals=0),
        compiler_params=pltpu.CompilerParams(
            dimension_semantics=("arbitrary",) * steps, vmem_limit_bytes=56 * 2**20
        ),
    )


def hidden_kernel(links, late, group, *refs):
    ups, refs = refs[:links], refs[links:]
    proj, refs = refs[0], refs[1:]
    seconds, refs = refs[:links], refs[links:]
    left_two, slope, right_one, refs = refs[0], refs[1], refs[2], refs[3:]
    firsts, refs = refs[:late], refs[late:]
    hidden, refs = refs[0], refs[1:]
    parts, refs = refs[: late * CHUNKS], refs[late * CHUNKS :]
    rank, up_all, hid_all = refs
    c, j = pl.program_id(0), pl.program_id(1)
    size = hidden.shape[1]

    @pl.when(j == 0)
    def _():
        for k in range(links):
            up_all[:, k * size : (k + 1) * size] = ups[k][...]
        up_all[:, links * size :] = proj[...]

    weights = wide([ref[...] for ref in seconds] + [left_two[...]])
    grad = nt(up_all[...], weights)
    hid = (grad * slope[...]).astype(BF16)
    hidden[...] = hid
    hid_all[:, pl.ds(pl.multiple_of(j * size, size), size)] = hid

    @pl.when(j == group - 1)
    def _():
        group_grad = hid_all[...]
        for n, ref in enumerate(firsts):
            part = nt(group_grad, wide([ref[g] for g in range(group)])).astype(BF16)
            for m in range(CHUNKS):
                piece = parts[n * CHUNKS + m]
                piece[...] = part[m * piece.shape[0] : (m + 1) * piece.shape[0]]
        term = nt(group_grad, right_one[...])

        @pl.when(c == 0)
        def _():
            rank[...] = term

        @pl.when(c > 0)
        def _():
            rank[...] += term


def hidden_call(ups, flips, proj, second, left_two, slope, right_one, first, late_from, chunk):
    rows = ups[-1][0].shape[0]
    _, hid_count, links, size, _ = first.shape
    count_in = ups[0][0].shape[1] // size
    group = hid_count // count_in
    rank = proj.shape[1]
    late = links - late_from
    in_specs = [
        pl.BlockSpec((rows, size), lambda c, j, flip=flip, place=place: (place, c ^ flip))
        for (_, place), flip in zip(ups, flips)
    ]
    in_specs.append(pl.BlockSpec((rows, rank), lambda c, j: (chunk, 0)))
    in_specs += [
        pl.BlockSpec((None, None, None, size, size), lambda c, j, k=k: (0, c * group + j, k, 0, 0))
        for k in range(links)
    ]
    in_specs.append(pl.BlockSpec((None, size, rank), lambda c, j: (0, c * group + j, 0)))
    in_specs.append(pl.BlockSpec((rows, size), lambda c, j: (chunk, c * group + j)))
    in_specs.append(pl.BlockSpec((None, rank, group * size), lambda c, j: (0, 0, c)))
    in_specs += [
        pl.BlockSpec((None, group, None, size, size), lambda c, j, k=k: (0, c, k, 0, 0))
        for k in range(late_from, links)
    ]
    out_specs = [pl.BlockSpec((rows, size), lambda c, j: (0, c * group + j))]
    out_specs += [pl.BlockSpec((rows // CHUNKS, size), lambda c, j: (0, c))] * (late * CHUNKS)
    out_specs.append(pl.BlockSpec((rows, rank), lambda c, j: (0, 0)))
    width = hid_count * size
    out_shape = [jax.ShapeDtypeStruct((rows, width), BF16)]
    out_shape += [
        jax.ShapeDtypeStruct((rows // CHUNKS, count_in * size), BF16)
    ] * (late * CHUNKS)
    out_shape.append(jax.ShapeDtypeStruct((rows, rank), F32))
    return pl.pallas_call(
        functools.partial(hidden_kernel, links, late, group),
        grid=(count_in, group),
        in_specs=in_specs,
        out_specs=out_specs,
        out_shape=out_shape,
        scratch_shapes=[
            pltpu.VMEM((rows, links * size + rank), BF16),
            pltpu.VMEM((rows, group * size), BF16),
        ],
        name="hidden_grad",
        **params(2),
    )(
        *[up for up, _ in ups], proj, *[second] * links, left_two, slope, right_one, *[first] * late
    )


def near_kernel(near, group, hid, *refs):
    weights, refs = refs[0], refs[1:]
    far_weights, base, far, total = refs
    kk = pl.program_id(1)
    term = nt(hid[...], wide([weights[g] for g in range(group)]))

    @pl.when(kk == 0)
    def _():
        total[...] = term
        far[...] = nt(hid[...], wide([far_weights[g] for g in range(group)])).astype(BF16)

    @pl.when(kk > 0)
    def _():
        total[...] += term

    @pl.when(kk == near - 1)
    def _():
        base[...] = total[...]


def near_call(hidden, first, count_in, near):
    rows = hidden.shape[0]
    _, hid_count, links, size, _ = first.shape
    group = hid_count // count_in

    def mate(c, kk):
        return c ^ ((1 << kk) >> 1)

    width = count_in * size
    return pl.pallas_call(
        functools.partial(near_kernel, near, group),
        grid=(count_in, near),
        in_specs=[
            pl.BlockSpec((rows, group * size), lambda c, kk: (0, mate(c, kk))),
            pl.BlockSpec(
                (None, group, None, size, size), lambda c, kk: (0, mate(c, kk), kk, 0, 0)
            ),
            pl.BlockSpec((None, group, None, size, size), lambda c, kk: (0, c, near, 0, 0)),
        ],
        out_specs=[
            pl.BlockSpec((rows, size), lambda c, kk: (0, c)),
            pl.BlockSpec((rows, size), lambda c, kk: (0, c)),
        ],
        out_shape=[
            jax.ShapeDtypeStruct((rows, width), F32),
            jax.ShapeDtypeStruct((rows, width), BF16),
        ],
        scratch_shapes=[pltpu.VMEM((rows, size), F32)],
        name="near_parts",
        **params(2),
    )(hidden, first, first)


def second_kernel(links, chunks, rows, *refs):
    ups, refs = refs[: links * chunks], refs[links * chunks :]
    proj, act, out, left_two, up_all = refs
    size = act.shape[1]

    @pl.when(pl.program_id(1) == 0)
    def _():
        for m in range(chunks):
            for k in range(links):
                up_all[m * rows : (m + 1) * rows, k * size : (k + 1) * size] = ups[m * links + k][
                    ...
                ]
        up_all[:, links * size :] = proj[...]

    grads = nn(act[...].T, up_all[...]).astype(BF16)
    for k in range(links):
        out[k] = grads[:, k * size : (k + 1) * size]
    left_two[...] = grads[:, links * size :]


def second_call(ups, flips, proj, act, shape):
    chunks = len(ups)
    tokens = act.shape[0]
    rows = tokens // chunks
    _, hid_count, links, size, _ = shape
    count_in = ups[0][0][0].shape[1] // size
    group = hid_count // count_in
    rank = proj.shape[1]
    in_specs = [
        pl.BlockSpec((rows, size), lambda c, j, flip=flip, place=place: (place, c ^ flip))
        for chunk in ups
        for (_, place), flip in zip(chunk, flips)
    ]
    in_specs.append(pl.BlockSpec((tokens, rank), lambda c, j: (0, 0)))
    in_specs.append(pl.BlockSpec((tokens, size), lambda c, j: (0, c * group + j)))
    width = hid_count * size
    return pl.pallas_call(
        functools.partial(second_kernel, links, chunks, rows),
        grid=(count_in, group),
        in_specs=in_specs,
        out_specs=[
            pl.BlockSpec(
                (None, None, links, size, size), lambda c, j: (0, c * group + j, 0, 0, 0)
            ),
            pl.BlockSpec((None, size, rank), lambda c, j: (0, c * group + j, 0)),
        ],
        out_shape=[
            jax.ShapeDtypeStruct(shape, BF16),
            jax.ShapeDtypeStruct((1, width, rank), BF16),
        ],
        scratch_shapes=[pltpu.VMEM((tokens, links * size + rank), BF16)],
        name="second_grad",
        **params(2),
    )(*[up for chunk in ups for up, _ in chunk], proj, act)


def first_kernel(links, chunks, rows, *refs):
    ins, refs = refs[: links * chunks], refs[links * chunks :]
    proj, refs = refs[0], refs[1:]
    hids, refs = refs[:1], refs[1:]
    out, right_one, in_all = refs
    size = hids[0].shape[1]

    @pl.when(pl.program_id(1) == 0)
    def _():
        for m in range(chunks):
            for k in range(links):
                in_all[k * size : (k + 1) * size, m * rows : (m + 1) * rows] = ins[m * links + k][
                    ...
                ].T
        in_all[links * size :, :] = proj[...].T

    hid = jnp.concatenate([ref[...] for ref in hids], axis=0)
    grads = nn(in_all[...], hid).astype(BF16)
    for k in range(links):
        out[k] = grads[k * size : (k + 1) * size]
    right_one[...] = grads[links * size :]


def first_call(ins, flips, proj, hids, shape):
    chunks = len(ins)
    tokens = hids[0].shape[0]
    rows = tokens // chunks
    _, hid_count, links, size, _ = shape
    count_in = ins[0][0][0].shape[1] // size
    group = hid_count // count_in
    rank = proj.shape[1]
    in_specs = [
        pl.BlockSpec((rows, size), lambda c, j, flip=flip, place=place: (place, c ^ flip))
        for chunk in ins
        for (_, place), flip in zip(chunk, flips)
    ]
    in_specs.append(pl.BlockSpec((tokens, rank), lambda c, j: (0, 0)))
    in_specs += [pl.BlockSpec((tokens, size), lambda c, j: (0, c * group + j))]
    width = hid_count * size
    return pl.pallas_call(
        functools.partial(first_kernel, links, chunks, rows),
        grid=(count_in, group),
        in_specs=in_specs,
        out_specs=[
            pl.BlockSpec(
                (None, None, links, size, size), lambda c, j: (0, c * group + j, 0, 0, 0)
            ),
            pl.BlockSpec((None, rank, size), lambda c, j: (0, 0, c * group + j)),
        ],
        out_shape=[
            jax.ShapeDtypeStruct(shape, BF16),
            jax.ShapeDtypeStruct((1, rank, width), BF16),
        ],
        scratch_shapes=[pltpu.VMEM((links * size + rank, tokens), BF16)],
        name="first_grad",
        **params(2),
    )(*[value for chunk in ins for value, _ in chunk], proj, *hids)


def body(
    inputs, preact, handoff, first_blocks, second_blocks, left_one, right_one, left_two, right_two
):
    shape = first_blocks.shape
    links, size = shape[2], shape[-1]
    tokens, feats = inputs.shape[1:]
    count_in = feats // size
    near = count_in.bit_length()
    flips = [(1 << k) >> 1 if k < near else 0 for k in range(links)]
    rows = tokens // CHUNKS
    spans = [slice(m * rows, (m + 1) * rows) for m in range(CHUNKS)]

    def sent(value):
        far = [swapped(value, bit) for bit in reversed(range(1, links - near))]
        return far[::-1]

    ranks = left_one.shape[2]
    first_half, second_half = spans

    in_core = swapped(inputs[0], 0)
    in_one = sent(inputs[0, first_half])
    act, slope, proj_act = gate_call(preact, left_two, size)
    early = jnp.concatenate([nn(inputs[0], left_one[0]), proj_act], axis=1)

    upstream = after(shifted(handoff[0]), in_core, early, *in_one)
    up_far = sent(upstream)
    up_core = swapped(upstream, 0)
    sums = tree_sum(jnp.concatenate([nt(upstream, right_two[0]), early], axis=1))
    proj_grad, proj_in, proj_act = jnp.split(sums, (ranks, 2 * ranks), axis=1)
    up_set = [(value, 0) for value in [upstream] * near + [up_core] + up_far]

    in_two = sent(after(inputs[0, second_half], sums, *up_far))
    hidden, *parts, back = hidden_call(
        up_set,
        flips,
        proj_grad,
        second_blocks,
        left_two,
        slope,
        right_one,
        first_blocks,
        near + 1,
        0,
    )

    def returned(pieces):
        return [swapped(piece, k + 1) for k, piece in reversed(list(enumerate(pieces)))]

    far_one, far_two = [returned(parts[m::CHUNKS]) for m in range(CHUNKS)]
    second_grad, lefttwo_grad = second_call([up_set], flips, after(proj_grad, back), act, shape)
    base, beside = near_call(after(hidden, second_grad), first_blocks, count_in, near)
    beside = swapped(beside, 0)
    back_rank = tree_sum(after(back, base, *in_two, *far_one))
    in_sets = [
        [(inputs[0], m)] * near + [(in_core, m)] + [(value, 0) for value in values]
        for m, values in enumerate([in_one, in_two])
    ]
    first_grad, rightone_grad = first_call(
        in_sets, flips, after(proj_in, beside), [hidden], shape
    )
    base = base + beside.astype(F32) + nt(back_rank, left_one[0])
    leftone_grad = nn(inputs[0].T, back_rank).astype(BF16)[None]
    righttwo_grad = nn(proj_act.T, upstream).astype(BF16)[None]
    total, first_grad, leftone_grad, righttwo_grad = lax.optimization_barrier(
        (base, first_grad, leftone_grad, righttwo_grad)
    )
    for pair in zip(far_one, far_two):
        total = total + jnp.concatenate(pair, axis=0).astype(F32)
    input_grad = total.astype(BF16)[None]
    return (
        input_grad,
        first_grad,
        second_grad,
        leftone_grad,
        rightone_grad,
        lefttwo_grad,
        righttwo_grad,
    )


def solution(mesh):
    by_feature = P("section", None, "tensor")
    by_block = P("section", "tensor", None, None, None)
    by_row = P("section", "tensor", None)
    in_specs = (
        by_feature,
        by_feature,
        by_feature,
        by_block,
        by_block,
        by_row,
        by_feature,
        by_row,
        by_feature,
    )
    out_specs = (
        by_feature,
        by_block,
        by_block,
        by_row,
        by_feature,
        by_row,
        by_feature,
    )
    return jax.shard_map(body, mesh=mesh, in_specs=in_specs, out_specs=out_specs, check_vma=False)
```

time: 425 us -> 367 us (0.86)
  waiting for transfers between devices: 192 us -> 168 us
  other arithmetic: 26.3 us -> 13 us
  starting transfers between devices: 37 us -> 24.1 us
  matrix products: 14.3 us -> 9.67 us
    ppermute x2 -> x1, waiting for transfers between devices: 33 us -> 0.01 us  [shifted(): lax.ppermute(value, 'section', [(i, (i - 1) % peers) for i in range(peers)])]
    pallas_call x0 -> x1, Pallas kernels: none -> 23.1 us  [gate_call(): pl.pallas_call(functools.partial(gate_kernel, min(64, tokens)), grid=(wid...]
    convert_element_type x5 -> x0, other arithmetic: 14.1 us -> none  [the longest x1 10.1 us: body(): (values * (0.5 * (1.0 + lax.erf(values * 0.7071067811865476)))).astype(BF16)]
    pallas_call x2 -> x1, Pallas kernels: 49.3 us -> 36.4 us  [hidden_call(): pl.pallas_call(functools.partial(hidden_kernel, links, late, group), grid...]
    ppermute x33 -> x23, starting transfers between devices: 32.5 us -> 20.2 us  [swapped(): return lax.ppermute(value, 'tensor', pairs)]
    pallas_call x2 -> x1, Pallas kernels: 32.2 us -> 21.5 us  [near_call(): pl.pallas_call(functools.partial(near_kernel, near, group), grid=(count_i...]
    dot_general x4 -> x3, matrix products: 13.4 us -> 4.56 us  [nn(): return jnp.dot(left, right, preferred_element_type=F32)]
    ppermute x33 -> x23, waiting for transfers between devices: 159 us -> 168 us  [swapped(): return lax.ppermute(value, 'tensor', pairs)]
  transfers between devices with their start and end apart: 35 -> 24, of which waited for: 14 -> 12; matrix products, arithmetic and copies ran while one was open for 10% -> 5% of each run, Pallas kernels for 33% -> 38%
where the time goes in v2:
time: 367 us; the launch traced here: 366 us
  waiting for transfers between devices  168 us (46%)
  Pallas kernels  141 us (38%)
  starting transfers between devices  24.1 us (7%)
  other arithmetic  13 us (4%)
  matrix products  9.67 us (3%)
  local copies, waits for them, and re-layouts  9.14 us (2%)
    ppermute x23, waiting for transfers between devices, swapped(): return lax.ppermute(value, 'tensor', pairs)  168 us
    pallas_call x1, Pallas kernels, hidden_call(): pl.pallas_call(functools.partial(hidden_kernel, links, late, group), grid...  36.4 us
    pallas_call x1, Pallas kernels, first_call(): pl.pallas_call(functools.partial(first_kernel, links, chunks, rows), grid...  31.1 us
    pallas_call x1, Pallas kernels, second_call(): pl.pallas_call(functools.partial(second_kernel, links, chunks, rows), gri...  28.4 us
    pallas_call x1, Pallas kernels, gate_call(): pl.pallas_call(functools.partial(gate_kernel, min(64, tokens)), grid=(wid...  23.1 us
    pallas_call x1, Pallas kernels, near_call(): pl.pallas_call(functools.partial(near_kernel, near, group), grid=(count_i...  21.5 us
    ppermute x23, starting transfers between devices, swapped(): return lax.ppermute(value, 'tensor', pairs)  20.2 us
  transfers between devices with their start and end apart: 24, of which 12 were waited for; matrix products, arithmetic and copies ran while one was open for 5% of the time, Pallas kernels for 38%

profile of v2, /device:TPU:0, one launch (start us, length us, event | category | flops | bytes accessed | tf_op | source)
XLA Modules:
  0.0 365.5 jit_solution(211767726148780141)
XLA Ops:
  0.6 3.9 %collective-permute-start = (bf16[1024,1024]{1,0:T(8,128)(2,1)}, bf16[1024,1024]{1,0:T(8,128)(2,1)}, u32[]{:S(2)}, u32[]{:S(2)}) collective-permute-start(bf16[1024,1024]{1,0:T(8,128)(2,1)} %bitcast.37), channel_id=1, source_target_pairs={{0,24},{8,0},{16,8},{24,16},{1,25},{9,1},{17,9},{25,17},{2,26},{10... | collective-permute-start | bytes 6291464 | tf_op jit(solution)/shard_map/ppermute | solution.py:22
  4.6 3.0 slice_bitcast_fusion
  7.6 2.6 collective-permute-start.3
  11.8 23.1 %gate.1 = (bf16[1024,4096]{1,0:T(8,128)(2,1)}, f32[1024,4096]{1,0:T(8,128)}, f32[1024,256]{1,0:T(8,128)}) custom-call(bf16[1,1024,4096]{2,1,0:T(8,128)(2,1)} %preact.1, bf16[1,4096,256]{2,1,0:T(8,128)(2,1)} %refs_13_.1), custom_call_target="tpu_custom_call" | custom-call | flops 1024 | bytes 1024 | tf_op jit(solution)/shard_map/gate/pallas_call | solution.py:86
  35.7 21.3 %collective-permute-done.3.refs_5_ = bf16[512,1024]{1,0:T(8,128)(2,1)} collective-permute-done((bf16[512,1024]{1,0:T(8,128)(2,1)}, bf16[512,1024]{1,0:T(8,128)(2,1)}, u32[]{:S(2)}, u32[]{:S(2)}) %collective-permute-start.3) | collective-permute-done | bytes 1048608 | tf_op jit(solution)/shard_map/ppermute | solution.py:17
  57.2 2.3 fusion.13
  61.6 3.5 collective-permute-done.7
  68.8 9.7 %collective-permute-done.8 = bf16[256,768]{1,0:T(8,128)(2,1)S(1)} collective-permute-done((bf16[256,768]{1,0:T(8,128)(2,1)S(1)}, bf16[256,768]{1,0:T(8,128)(2,1)S(1)}, u32[]{:S(2)}, u32[]{:S(2)}) %collective-permute-start.8) | collective-permute-done | bytes 393248 | tf_op jit(solution)/shard_map/ppermute | solution.py:17
  78.6 2.1 collective-permute-start.9
  83.0 61.3 %collective-permute-done.9 = bf16[256,768]{1,0:T(8,128)(2,1)S(1)} collective-permute-done((bf16[256,768]{1,0:T(8,128)(2,1)S(1)}, bf16[256,768]{1,0:T(8,128)(2,1)S(1)}, u32[]{:S(2)}, u32[]{:S(2)}) %collective-permute-start.9) | collective-permute-done | bytes 393248 | tf_op jit(solution)/shard_map/ppermute | solution.py:17
  146.3 50.4 %collective-permute-done.10 = bf16[256,768]{1,0:T(8,128)(2,1)} collective-permute-done((bf16[256,768]{1,0:T(8,128)(2,1)S(1)}, bf16[256,768]{1,0:T(8,128)(2,1)}, u32[]{:S(2)}, u32[]{:S(2)}) %collective-permute-start.10) | collective-permute-done | bytes 393248 | tf_op jit(solution)/shard_map/ppermute | solution.py:17
  200.1 2.6 collective-permute-start.13
  205.2 36.4 %hidden_grad.1 = (bf16[1024,4096]{1,0:T(8,128)(2,1)}, bf16[512,1024]{1,0:T(8,128)(2,1)}, bf16[512,1024]{1,0:T(8,128)(2,1)}, bf16[512,1024]{1,0:T(8,128)(2,1)}, b...) custom-call(bf16[1024,1024]{1,0:T(8,128)(2,1)} %collective-permute-done.refs_0_.refs_1_.refs_2_, ...), custom_call_target="tpu_custom_call" | custom-call | flops 1024 | bytes 1024 | tf_op jit(solution)/shard_map/hidden_grad/pallas_call | solution.py:192
  241.8 2.4 collective-permute-start.16
  244.2 28.4 %second_grad.1 = (bf16[1,16,6,256,256]{4,3,2,1,0:T(8,128)(2,1)}, bf16[1,4096,256]{2,1,0:T(8,128)(2,1)}) custom-call(bf16[1024,1024]{1,0:T(8,128)(2,1)} %collective-permute-done.refs_0_.refs_1_.refs_2_, bf16[1024,1024]{1,0:T(8,128)(2,1)} %collective-permute-done.refs_0_.refs_1_.refs_2_, bf16[1024,1024]{1,0:T(8,128)(2,1)} %collective-permute-done.refs_0_.refs_1_.refs_2_, ...), custom_call_target="tpu_custom_call" | custom-call | flops 1024 | bytes 1024 | tf_op jit(solution)/shard_map/second_grad/pallas_call | solution.py:298
  272.6 21.5 %near_parts.1 = (f32[1024,1024]{1,0:T(8,128)}, bf16[1024,1024]{1,0:T(8,128)(2,1)}) custom-call(bf16[1024,4096]{1,0:T(8,128)(2,1)} %get-tuple-element.40.hid.refs_13_, bf16[1,16,6,256,256]{4,3,2,1,0:T(8,128)(2,1)} %refs_1_.1, bf16[1,16,6,256,256]{4,3,2,1,0:T(8,128)(2,1)} %refs_1_.1), custom_call_target="tpu_custom_call" | custom-call | flops 1024 | bytes 1024 | tf_op jit(solution)/shard_map/near_parts/pallas_call | solution.py:238
  296.4 5.5 %collective-permute-done.18 = bf16[256,256]{1,0:T(8,128)(2,1)S(1)} collective-permute-done((bf16[256,256]{1,0:T(8,128)(2,1)S(1)}, bf16[256,256]{1,0:T(8,128)(2,1)S(1)}, u32[]{:S(2)}, u32[]{:S(2)}) %collective-permute-start.18) | collective-permute-done | bytes 131104 | tf_op jit(solution)/shard_map/ppermute | solution.py:17
  302.7 7.7 %collective-permute-done.19 = bf16[256,256]{1,0:T(8,128)(2,1)S(1)} collective-permute-done((bf16[256,256]{1,0:T(8,128)(2,1)S(1)}, bf16[256,256]{1,0:T(8,128)(2,1)S(1)}, u32[]{:S(2)}, u32[]{:S(2)}) %collective-permute-start.19) | collective-permute-done | bytes 131104 | tf_op jit(solution)/shard_map/ppermute | solution.py:17
  310.6 2.4 collective-permute-start.22
  313.1 5.7 %collective-permute-done.20 = bf16[256,256]{1,0:T(8,128)(2,1)S(1)} collective-permute-done((bf16[256,256]{1,0:T(8,128)(2,1)S(1)}, bf16[256,256]{1,0:T(8,128)(2,1)S(1)}, u32[]{:S(2)}, u32[]{:S(2)}) %collective-permute-start.20) | collective-permute-done | bytes 131104 | tf_op jit(solution)/shard_map/ppermute | solution.py:17
  318.9 3.1 fusion.2
  322.0 31.1 %first_grad.1 = (bf16[1,16,6,256,256]{4,3,2,1,0:T(8,128)(2,1)}, bf16[1,256,4096]{2,1,0:T(8,128)(2,1)}) custom-call(bf16[1024,1024]{1,0:T(8,128)(2,1)} %bitcast.31, bf16[1024,1024]{1,0:T(8,128)(2,1)} %bitcast.32, bf16[1024,1024]{1,0:T(8,128)(2,1)} %bitcast.33, bf16[1024,1024]{1,0:T(8,128)(2,1)} %collective-permute-done.1.refs_3_.refs_9_, ...), custom_call_target="tpu_custom_call" | custom-call | flops 1024 | bytes 1024 | tf_op jit(solution)/shard_map/first_grad/pallas_call | solution.py:357
  355.3 2.8 add_add_fusion
  361.0 4.5 %fusion = bf16[1,1024,1024]{2,1,0:T(8,128)(2,1)} fusion(f32[1024,1024]{1,0:T(8,128)} %add_add_fusion, bf16[512,1024]{1,0:T(8,128)(2,1)} %collective-permute-done.22, bf16[512,1024]{1,0:T(8,128)(2,1)S(1)} %collective-permute-done.15, bf16[512,1024]{1,0:T(8,128)(2,1)} %collective-permute-done.23, bf16[512,1024]{1,0:T(8,128)(2,1)} %copy-done.10), kind=kLoop, calls=%fused_computation.10 | loop fusion | flops 11534336 | bytes 10485760 | tf_op jit(solution)/shard_map/broadcast_in_dim | solution.py:445
  (83 shorter events, 27.0 us)
Async XLA Ops:
  0.6 56.5 %collective-permute-start = (bf16[1024,1024]{1,0:T(8,128)(2,1)}, bf16[1024,1024]{1,0:T(8,128)(2,1)}, u32[]{:S(2)}, u32[]{:S(2)}) collective-permute-start(bf16[1024,1024]{1,0:T(8,128)(2,1)} %bitcast.37), channel_id=1, source_target_pairs={{0,24},{8,0},{16,8},{24,16},{1,25},{9,1},{17,9},{25,17},{2,26},{10... | collective-permute-start | bytes 6291464 | tf_op jit(solution)/shard_map/ppermute | solution.py:22
  4.6 52.6 %collective-permute-start.1 = (bf16[1024,1024]{1,0:T(8,128)(2,1)}, bf16[1024,1024]{1,0:T(8,128)(2,1)}, u32[]{:S(2)}, u32[]{:S(2)}) collective-permute-start(bf16[1024,1024]{1,0:T(8,128)(2,1)} %bitcast.30), channel_id=1, source_target_pairs={{0,1},{1,0},{2,3},{3,2},{4,5},{5,4},{6,7},{7,6},{8,9},{9,8},{10,11... | collective-permute-start | bytes 6291464 | tf_op jit(solution)/shard_map/ppermute | solution.py:17
  7.6 49.4 %collective-permute-start.3 = (bf16[512,1024]{1,0:T(8,128)(2,1)}, bf16[512,1024]{1,0:T(8,128)(2,1)}, u32[]{:S(2)}, u32[]{:S(2)}) collective-permute-start(bf16[512,1024]{1,0:T(8,128)(2,1)} %get-tuple-element.65), channel_id=1, source_target_pairs={{0,4},{1,5},{2,6},{3,7},{4,0},{5,1},{6,2},{7,3},{8,12},{9,13},{10,... | collective-permute-start | bytes 3145736 | tf_op jit(solution)/shard_map/ppermute | solution.py:17
  10.2 47.0 %collective-permute-start.2 = (bf16[512,1024]{1,0:T(8,128)(2,1)}, bf16[512,1024]{1,0:T(8,128)(2,1)}, u32[]{:S(2)}, u32[]{:S(2)}) collective-permute-start(bf16[512,1024]{1,0:T(8,128)(2,1)} %get-tuple-element.65), channel_id=1, source_target_pairs={{0,2},{1,3},{2,0},{3,1},{4,6},{5,7},{6,4},{7,5},{8,10},{9,11},{10,... | collective-permute-start | bytes 3145736 | tf_op jit(solution)/shard_map/ppermute | solution.py:17
  61.5 3.6 collective-permute-start.7
  67.3 11.2 %collective-permute-start.8 = (bf16[256,768]{1,0:T(8,128)(2,1)S(1)}, bf16[256,768]{1,0:T(8,128)(2,1)S(1)}, u32[]{:S(2)}, u32[]{:S(2)}) collective-permute-start(bf16[256,768]{1,0:T(8,128)(2,1)S(1)} %dynamic-slice_convert_fusion), channel_id=1, source_target_pairs={{0,2},{1,3},{2,0},{3,1},{4,6},{5,7},{6,4},{7,5},{8,10},{9,11},{10,... | collective-permute-start | bytes 1179656 | tf_op jit(solution)/shard_map/ppermute | solution.py:17
  78.6 65.7 %collective-permute-start.9 = (bf16[256,768]{1,0:T(8,128)(2,1)S(1)}, bf16[256,768]{1,0:T(8,128)(2,1)S(1)}, u32[]{:S(2)}, u32[]{:S(2)}) collective-permute-start(bf16[256,768]{1,0:T(8,128)(2,1)S(1)} %fusion.15), channel_id=1, source_target_pairs={{0,4},{1,5},{2,6},{3,7},{4,0},{5,1},{6,2},{7,3},{8,12},{9,13},{10,... | collective-permute-start | bytes 1179656 | tf_op jit(solution)/shard_map/ppermute | solution.py:17
  80.7 118.2 %collective-permute-start.6 = (bf16[1024,1024]{1,0:T(8,128)(2,1)}, bf16[1024,1024]{1,0:T(8,128)(2,1)S(1)}, u32[]{:S(2)}, u32[]{:S(2)}) collective-permute-start(bf16[1024,1024]{1,0:T(8,128)(2,1)} %collective-permute-done.refs_0_.refs_1_.refs_2_), channel_id=1, source_target_pairs={{0,4},{1,5},{2,6},{3,7},{4,0},{5,1},{6,2},{7,3},{8,12},{9,13},{10,... | collective-permute-start | bytes 6291464 | tf_op jit(solution)/shard_map/ppermute | solution.py:17
  81.6 117.3 %collective-permute-start.5 = (bf16[1024,1024]{1,0:T(8,128)(2,1)}, bf16[1024,1024]{1,0:T(8,128)(2,1)}, u32[]{:S(2)}, u32[]{:S(2)}) collective-permute-start(bf16[1024,1024]{1,0:T(8,128)(2,1)} %collective-permute-done.refs_0_.refs_1_.refs_2_), channel_id=1, source_target_pairs={{0,2},{1,3},{2,0},{3,1},{4,6},{5,7},{6,4},{7,5},{8,10},{9,11},{10,... | collective-permute-start | bytes 6291464 | tf_op jit(solution)/shard_map/ppermute | solution.py:17
  83.0 122.1 %collective-permute-start.4 = (bf16[1024,1024]{1,0:T(8,128)(2,1)}, bf16[1024,1024]{1,0:T(8,128)(2,1)}, u32[]{:S(2)}, u32[]{:S(2)}) collective-permute-start(bf16[1024,1024]{1,0:T(8,128)(2,1)} %collective-permute-done.refs_0_.refs_1_.refs_2_), channel_id=1, source_target_pairs={{0,1},{1,0},{2,3},{3,2},{4,5},{5,4},{6,7},{7,6},{8,9},{9,8},{10,11... | collective-permute-start | bytes 6291464 | tf_op jit(solution)/shard_map/ppermute | solution.py:17
  145.5 51.2 %collective-permute-start.10 = (bf16[256,768]{1,0:T(8,128)(2,1)S(1)}, bf16[256,768]{1,0:T(8,128)(2,1)}, u32[]{:S(2)}, u32[]{:S(2)}) collective-permute-start(bf16[256,768]{1,0:T(8,128)(2,1)S(1)} %add_convert_fusion.1), channel_id=1, source_target_pairs={{0,2},{1,3},{2,0},{3,1},{4,6},{5,7},{6,4},{7,5},{8,10},{9,11},{10,... | collective-permute-start | bytes 1179656 | tf_op jit(solution)/shard_map/ppermute | solution.py:17
  198.8 3.9 %collective-permute-start.11 = (bf16[512,768]{1,0:T(8,128)(2,1)}, bf16[512,768]{1,0:T(8,128)(2,1)}, u32[]{:S(2)}, u32[]{:S(2)}) collective-permute-start(bf16[512,768]{1,0:T(8,128)(2,1)} %pad_maximum_fusion.2), channel_id=1, source_target_pairs={{0,1},{1,0},{2,3},{3,2},{4,5},{5,4},{6,7},{7,6},{8,9},{9,8},{10,11... | collective-permute-start | bytes 2359304 | tf_op jit(solution)/shard_map/ppermute | solution.py:17
  198.9 95.3 %collective-permute-start.14 = (bf16[512,1024]{1,0:T(8,128)(2,1)}, bf16[512,1024]{1,0:T(8,128)(2,1)S(1)}, u32[]{:S(2)}, u32[]{:S(2)}) collective-permute-start(bf16[512,1024]{1,0:T(8,128)(2,1)} %get-tuple-element.43), channel_id=1, source_target_pairs={{0,4},{1,5},{2,6},{3,7},{4,0},{5,1},{6,2},{7,3},{8,12},{9,13},{10,... | collective-permute-start | bytes 3145736 | tf_op jit(solution)/shard_map/ppermute | solution.py:17
  200.1 94.1 %collective-permute-start.13 = (bf16[512,1024]{1,0:T(8,128)(2,1)}, bf16[512,1024]{1,0:T(8,128)(2,1)S(1)}, u32[]{:S(2)}, u32[]{:S(2)}) collective-permute-start(bf16[512,1024]{1,0:T(8,128)(2,1)} %get-tuple-element.43), channel_id=1, source_target_pairs={{0,2},{1,3},{2,0},{3,1},{4,6},{5,7},{6,4},{7,5},{8,10},{9,11},{10,... | collective-permute-start | bytes 3145736 | tf_op jit(solution)/shard_map/ppermute | solution.py:17
  241.6 52.6 %collective-permute-start.15 = (bf16[512,1024]{1,0:T(8,128)(2,1)}, bf16[512,1024]{1,0:T(8,128)(2,1)S(1)}, u32[]{:S(2)}, u32[]{:S(2)}) collective-permute-start(bf16[512,1024]{1,0:T(8,128)(2,1)} %get-tuple-element.44), channel_id=1, source_target_pairs={{0,4},{1,5},{2,6},{3,7},{4,0},{5,1},{6,2},{7,3},{8,12},{9,13},{10,... | collective-permute-start | bytes 3145736 | tf_op jit(solution)/shard_map/ppermute | solution.py:17
  241.8 52.4 %collective-permute-start.16 = (bf16[512,1024]{1,0:T(8,128)(2,1)}, bf16[512,1024]{1,0:T(8,128)(2,1)S(1)}, u32[]{:S(2)}, u32[]{:S(2)}) collective-permute-start(bf16[512,1024]{1,0:T(8,128)(2,1)} %get-tuple-element.45), channel_id=1, source_target_pairs={{0,2},{1,3},{2,0},{3,1},{4,6},{5,7},{6,4},{7,5},{8,10},{9,11},{10,... | collective-permute-start | bytes 3145736 | tf_op jit(solution)/shard_map/ppermute | solution.py:17
  294.3 2.0 collective-permute-start.17
  295.6 26.5 %collective-permute-start.12 = (bf16[1024,1024]{1,0:T(8,128)(2,1)}, bf16[1024,1024]{1,0:T(8,128)(2,1)S(1)}, u32[]{:S(2)}, u32[]{:S(2)}) collective-permute-start(bf16[1024,1024]{1,0:T(8,128)(2,1)} %get-tuple-element.42), channel_id=1, source_target_pairs={{0,1},{1,0},{2,3},{3,2},{4,5},{5,4},{6,7},{7,6},{8,9},{9,8},{10,11... | collective-permute-start | bytes 6291464 | tf_op jit(solution)/shard_map/ppermute | solution.py:17
  296.3 5.6 %collective-permute-start.18 = (bf16[256,256]{1,0:T(8,128)(2,1)S(1)}, bf16[256,256]{1,0:T(8,128)(2,1)S(1)}, u32[]{:S(2)}, u32[]{:S(2)}) collective-permute-start(bf16[256,256]{1,0:T(8,128)(2,1)S(1)} %dynamic-slice_convert_fusion.1), channel_id=1, source_target_pairs={{0,2},{1,3},{2,0},{3,1},{4,6},{5,7},{6,4},{7,5},{8,10},{9,11},{10,... | collective-permute-start | bytes 393224 | tf_op jit(solution)/shard_map/ppermute | solution.py:17
  302.0 8.5 %collective-permute-start.19 = (bf16[256,256]{1,0:T(8,128)(2,1)S(1)}, bf16[256,256]{1,0:T(8,128)(2,1)S(1)}, u32[]{:S(2)}, u32[]{:S(2)}) collective-permute-start(bf16[256,256]{1,0:T(8,128)(2,1)S(1)} %fusion.16), channel_id=1, source_target_pairs={{0,4},{1,5},{2,6},{3,7},{4,0},{5,1},{6,2},{7,3},{8,12},{9,13},{10,... | collective-permute-start | bytes 393224 | tf_op jit(solution)/shard_map/ppermute | solution.py:17
  310.5 8.2 %collective-permute-start.20 = (bf16[256,256]{1,0:T(8,128)(2,1)S(1)}, bf16[256,256]{1,0:T(8,128)(2,1)S(1)}, u32[]{:S(2)}, u32[]{:S(2)}) collective-permute-start(bf16[256,256]{1,0:T(8,128)(2,1)S(1)} %add_convert_fusion.2), channel_id=1, source_target_pairs={{0,2},{1,3},{2,0},{3,1},{4,6},{5,7},{6,4},{7,5},{8,10},{9,11},{10,... | collective-permute-start | bytes 393224 | tf_op jit(solution)/shard_map/ppermute | solution.py:17
  310.6 48.9 %collective-permute-start.22 = (bf16[512,1024]{1,0:T(8,128)(2,1)}, bf16[512,1024]{1,0:T(8,128)(2,1)}, u32[]{:S(2)}, u32[]{:S(2)}) collective-permute-start(bf16[512,1024]{1,0:T(8,128)(2,1)} %get-tuple-element.50), channel_id=1, source_target_pairs={{0,4},{1,5},{2,6},{3,7},{4,0},{5,1},{6,2},{7,3},{8,12},{9,13},{10,... | collective-permute-start | bytes 3145736 | tf_op jit(solution)/shard_map/ppermute | solution.py:17
  313.0 48.0 %collective-permute-start.23 = (bf16[512,1024]{1,0:T(8,128)(2,1)}, bf16[512,1024]{1,0:T(8,128)(2,1)}, u32[]{:S(2)}, u32[]{:S(2)}) collective-permute-start(bf16[512,1024]{1,0:T(8,128)(2,1)} %get-tuple-element.51), channel_id=1, source_target_pairs={{0,2},{1,3},{2,0},{3,1},{4,6},{5,7},{6,4},{7,5},{8,10},{9,11},{10,... | collective-permute-start | bytes 3145736 | tf_op jit(solution)/shard_map/ppermute | solution.py:17
  318.8 34.3 %collective-permute-start.21 = (bf16[512,256]{1,0:T(8,128)(2,1)S(1)}, bf16[512,256]{1,0:T(8,128)(2,1)S(1)}, u32[]{:S(2)}, u32[]{:S(2)}) collective-permute-start(bf16[512,256]{1,0:T(8,128)(2,1)S(1)} %pad_maximum_fusion.6), channel_id=1, source_target_pairs={{0,1},{1,0},{2,3},{3,2},{4,5},{5,4},{6,7},{7,6},{8,9},{9,8},{10,11... | collective-permute-start | bytes 786440 | tf_op jit(solution)/shard_map/ppermute | solution.py:17
  (14 other events, 209.8 us)

commit v3 on v2

--- a/solution.py
+++ b/solution.py
@@ -22,24 +22,29 @@
     return lax.ppermute(value, "section", [(i, (i - 1) % peers) for i in range(peers)])
 
 
-def tree_sum(value):
+def tree_sum(value, halvings, before_swap=(), before_gather=()):
     bits = lax.axis_size("tensor").bit_length() - 1
     place = lax.axis_index("tensor")
-    for bit in range(bits - 1):
+    for bit in range(halvings):
         half = value.shape[0] // 2
         mine = (place >> bit) & 1
         keep = lax.dynamic_slice_in_dim(value, mine * half, half)
         give = lax.dynamic_slice_in_dim(value, (1 - mine) * half, half)
         give = give if bit == 0 else give.astype(BF16)
         value = keep + swapped(give, bit).astype(F32)
-    value = (value + swapped(value.astype(BF16), bits - 1).astype(F32)).astype(BF16)
-    for bit in reversed(range(bits - 1)):
+    value = after(value, *before_swap)
+    stages = []
+    for bit in range(halvings, bits):
+        value = value + swapped(value.astype(BF16), bit).astype(F32)
+        stages.append(value)
+    value = after(value.astype(BF16), *before_gather)
+    for bit in reversed(range(halvings)):
         mine = (place >> bit) & 1
         other = swapped(value, bit)
         first = jnp.where(mine == 0, value, other)
         second = jnp.where(mine == 0, other, value)
         value = jnp.concatenate([first, second])
-    return value
+    return value, stages[0]
 
 
 def nt(left, right):
@@ -208,14 +213,16 @@
 
 def near_kernel(near, group, hid, *refs):
     weights, refs = refs[0], refs[1:]
-    far_weights, base, far, total = refs
+    far_weights, base, *far, total = refs
     kk = pl.program_id(1)
     term = nt(hid[...], wide([weights[g] for g in range(group)]))
 
     @pl.when(kk == 0)
     def _():
         total[...] = term
-        far[...] = nt(hid[...], wide([far_weights[g] for g in range(group)])).astype(BF16)
+        other = nt(hid[...], wide([far_weights[g] for g in range(group)])).astype(BF16)
+        for m, piece in enumerate(far):
+            piece[...] = other[m * piece.shape[0] : (m + 1) * piece.shape[0]]
 
     @pl.when(kk > 0)
     def _():
@@ -247,11 +254,11 @@
         ],
         out_specs=[
             pl.BlockSpec((rows, size), lambda c, kk: (0, c)),
-            pl.BlockSpec((rows, size), lambda c, kk: (0, c)),
+            *[pl.BlockSpec((rows // CHUNKS, size), lambda c, kk: (0, c))] * CHUNKS,
         ],
         out_shape=[
             jax.ShapeDtypeStruct((rows, width), F32),
-            jax.ShapeDtypeStruct((rows, width), BF16),
+            *[jax.ShapeDtypeStruct((rows // CHUNKS, width), BF16)] * CHUNKS,
         ],
         scratch_shapes=[pltpu.VMEM((rows, size), F32)],
         name="near_parts",
@@ -259,60 +266,74 @@
     )(hidden, first, first)
 
 
-def second_kernel(links, chunks, rows, *refs):
-    ups, refs = refs[: links * chunks], refs[links * chunks :]
-    proj, act, out, left_two, up_all = refs
-    size = act.shape[1]
-
-    @pl.when(pl.program_id(1) == 0)
-    def _():
-        for m in range(chunks):
-            for k in range(links):
-                up_all[m * rows : (m + 1) * rows, k * size : (k + 1) * size] = ups[m * links + k][
-                    ...
-                ]
-        up_all[:, links * size :] = proj[...]
-
-    grads = nn(act[...].T, up_all[...]).astype(BF16)
-    for k in range(links):
-        out[k] = grads[:, k * size : (k + 1) * size]
-    left_two[...] = grads[:, links * size :]
-
-
-def second_call(ups, flips, proj, act, shape):
-    chunks = len(ups)
+def second_kernel(count, group, has_proj, *refs):
+    ups, refs = refs[:count], refs[count:]
+    if has_proj:
+        proj, act, _, out, left_two, turned = refs
+    else:
+        act, out, turned = refs
+    k = pl.program_id(1)
+    size = ups[0].shape[1]
+
+    @pl.when(k == 0)
+    def _():
+        for g in range(group):
+            turned[g * size : (g + 1) * size, :] = act[:, g * size : (g + 1) * size].T
+
+    def store(up):
+        grads = nn(turned[...], up).astype(BF16)
+        for g in range(group):
+            out[g] = grads[g * size : (g + 1) * size]
+
+    for n in range(count):
+        pl.when(k == n)(lambda n=n: store(ups[n][...]))
+
+    if has_proj:
+
+        @pl.when(k == count - 1)
+        def _():
+            left_two[...] = nn(turned[...], proj[...]).astype(BF16)
+
+
+def second_call(ups, flips, act, shape, start, proj=None, partial=None):
+    count = len(ups)
     tokens = act.shape[0]
-    rows = tokens // chunks
     _, hid_count, links, size, _ = shape
-    count_in = ups[0][0][0].shape[1] // size
+    count_in = ups[0].shape[1] // size
     group = hid_count // count_in
-    rank = proj.shape[1]
+    has_proj = proj is not None
     in_specs = [
-        pl.BlockSpec((rows, size), lambda c, j, flip=flip, place=place: (place, c ^ flip))
-        for chunk in ups
-        for (_, place), flip in zip(chunk, flips)
-    ]
-    in_specs.append(pl.BlockSpec((tokens, rank), lambda c, j: (0, 0)))
-    in_specs.append(pl.BlockSpec((tokens, size), lambda c, j: (0, c * group + j)))
-    width = hid_count * size
+        pl.BlockSpec((tokens, size), lambda c, k, flip=flip: (0, c ^ flip)) for flip in flips
+    ]
+    args = list(ups)
+    out_specs = [
+        pl.BlockSpec((None, group, None, size, size), lambda c, k: (0, c, start + k, 0, 0))
+    ]
+    out_shape = [jax.ShapeDtypeStruct(shape, BF16)]
+    aliases = {}
+    if has_proj:
+        rank = proj.shape[1]
+        in_specs.append(pl.BlockSpec((tokens, rank), lambda c, k: (0, 0)))
+        args.append(proj)
+        out_specs.append(pl.BlockSpec((None, group * size, rank), lambda c, k: (0, c, 0)))
+        out_shape.append(jax.ShapeDtypeStruct((1, hid_count * size, rank), BF16))
+    in_specs.append(pl.BlockSpec((tokens, group * size), lambda c, k: (0, c)))
+    args.append(act)
+    if has_proj:
+        in_specs.append(pl.BlockSpec(memory_space=pl.ANY))
+        args.append(partial)
+        aliases = {len(args) - 1: 0}
     return pl.pallas_call(
-        functools.partial(second_kernel, links, chunks, rows),
-        grid=(count_in, group),
+        functools.partial(second_kernel, count, group, has_proj),
+        grid=(count_in, count),
         in_specs=in_specs,
-        out_specs=[
-            pl.BlockSpec(
-                (None, None, links, size, size), lambda c, j: (0, c * group + j, 0, 0, 0)
-            ),
-            pl.BlockSpec((None, size, rank), lambda c, j: (0, c * group + j, 0)),
-        ],
-        out_shape=[
-            jax.ShapeDtypeStruct(shape, BF16),
-            jax.ShapeDtypeStruct((1, width, rank), BF16),
-        ],
-        scratch_shapes=[pltpu.VMEM((tokens, links * size + rank), BF16)],
-        name="second_grad",
+        out_specs=out_specs,
+        out_shape=out_shape,
+        scratch_shapes=[pltpu.VMEM((group * size, tokens), BF16)],
+        input_output_aliases=aliases,
+        name="second_late" if has_proj else "second_early",
         **params(2),
-    )(*[up for chunk in ups for up, _ in chunk], proj, act)
+    )(*args)
 
 
 def first_kernel(links, chunks, rows, *refs):
@@ -401,11 +422,19 @@
     upstream = after(shifted(handoff[0]), in_core, early, *in_one)
     up_far = sent(upstream)
     up_core = swapped(upstream, 0)
-    sums = tree_sum(jnp.concatenate([nt(upstream, right_two[0]), early], axis=1))
+    (second_part,) = second_call(
+        [upstream] * near + [up_core], flips[: near + 1], act, shape, 0
+    )
+    sums, _ = tree_sum(
+        jnp.concatenate([nt(upstream, right_two[0]), early], axis=1),
+        links - near - 1,
+        [second_part],
+        up_far,
+    )
     proj_grad, proj_in, proj_act = jnp.split(sums, (ranks, 2 * ranks), axis=1)
     up_set = [(value, 0) for value in [upstream] * near + [up_core] + up_far]
 
-    in_two = sent(after(inputs[0, second_half], sums, *up_far))
+    in_two = sent(after(inputs[0], *up_far)[second_half])
     hidden, *parts, back = hidden_call(
         up_set,
         flips,
@@ -422,17 +451,22 @@
     def returned(pieces):
         return [swapped(piece, k + 1) for k, piece in reversed(list(enumerate(pieces)))]
 
-    far_one, far_two = [returned(parts[m::CHUNKS]) for m in range(CHUNKS)]
-    second_grad, lefttwo_grad = second_call([up_set], flips, after(proj_grad, back), act, shape)
-    base, beside = near_call(after(hidden, second_grad), first_blocks, count_in, near)
-    beside = swapped(beside, 0)
-    back_rank = tree_sum(after(back, base, *in_two, *far_one))
+    back, *parts = lax.optimization_barrier((back, *parts, *in_two))[: 1 + len(parts)]
+    far_one = returned(parts[::CHUNKS])
+    parts = parts[1::CHUNKS]
+    far_two = returned(lax.optimization_barrier((*parts, *far_one))[: len(parts)])
+    back_rank, stage = tree_sum(back, 1)
+    base, *beside = near_call(hidden, first_blocks, count_in, near)
+    beside = jnp.concatenate([swapped(piece, 0) for piece in beside], axis=0)
+    second_grad, lefttwo_grad = second_call(
+        up_far, flips[near + 1 :], act, shape, near + 1, after(proj_grad, stage), second_part
+    )
     in_sets = [
         [(inputs[0], m)] * near + [(in_core, m)] + [(value, 0) for value in values]
         for m, values in enumerate([in_one, in_two])
     ]
     first_grad, rightone_grad = first_call(
-        in_sets, flips, after(proj_in, beside), [hidden], shape
+        in_sets, flips, after(proj_in, *far_one), [hidden], shape
     )
     base = base + beside.astype(F32) + nt(back_rank, left_one[0])
     leftone_grad = nn(inputs[0].T, back_rank).astype(BF16)[None]

time: 367 us -> 414 us (1.13)
  waiting for transfers between devices: 168 us -> 203 us
  Pallas kernels: 141 us -> 147 us
    ppermute x23, waiting for transfers between devices: 168 us -> 203 us  [swapped(): return lax.ppermute(value, 'tensor', pairs)]
    pallas_call x1 -> x2, Pallas kernels: 28.4 us -> 35.4 us  [second_call(): pl.pallas_call(functools.partial(second_kernel, count, group, has_proj),...]
  transfers between devices with their start and end apart: 24 -> 24, of which waited for: 12 -> 9; matrix products, arithmetic and copies ran while one was open for 5% -> 5% of each run, Pallas kernels for 38% -> 36%
where the time goes in v3:
time: 414 us; the launch traced here: 413 us
  waiting for transfers between devices  203 us (49%)
  Pallas kernels  147 us (36%)
  starting transfers between devices  23.5 us (6%)
  other arithmetic  13.8 us (3%)
  local copies, waits for them, and re-layouts  12.5 us (3%)
  matrix products  11.3 us (3%)
    ppermute x23, waiting for transfers between devices, swapped(): return lax.ppermute(value, 'tensor', pairs)  203 us
    pallas_call x1, Pallas kernels, hidden_call(): pl.pallas_call(functools.partial(hidden_kernel, links, late, group), grid...  36.4 us
    pallas_call x2, Pallas kernels, second_call(): pl.pallas_call(functools.partial(second_kernel, count, group, has_proj),...  35.4 us
    pallas_call x1, Pallas kernels, first_call(): pl.pallas_call(functools.partial(first_kernel, links, chunks, rows), grid...  30.9 us
    pallas_call x1, Pallas kernels, gate_call(): pl.pallas_call(functools.partial(gate_kernel, min(64, tokens)), grid=(wid...  23.1 us
    pallas_call x1, Pallas kernels, near_call(): pl.pallas_call(functools.partial(near_kernel, near, group), grid=(count_i...  21.6 us
    ppermute x23, starting transfers between devices, swapped(): return lax.ppermute(value, 'tensor', pairs)  19.9 us
  transfers between devices with their start and end apart: 24, of which 9 were waited for; matrix products, arithmetic and copies ran while one was open for 5% of the time, Pallas kernels for 36%

profile of v3, /device:TPU:0, one launch (start us, length us, event | category | flops | bytes accessed | tf_op | source)
XLA Modules:
  0.0 412.6 jit_solution(15932019976606017921)
XLA Ops:
  1.2 3.5 collective-permute-start
  4.7 2.3 slice_bitcast_fusion
  8.5 2.6 collective-permute-start.3
  11.1 23.1 %gate.1 = (bf16[1024,4096]{1,0:T(8,128)(2,1)}, f32[1024,4096]{1,0:T(8,128)}, f32[1024,256]{1,0:T(8,128)}) custom-call(bf16[1,1024,4096]{2,1,0:T(8,128)(2,1)} %preact.1, bf16[1,4096,256]{2,1,0:T(8,128)(2,1)} %refs_13_.1), custom_call_target="tpu_custom_call" | custom-call | flops 1024 | bytes 1024 | tf_op jit(solution)/shard_map/gate/pallas_call | solution.py:91
  35.0 19.9 %collective-permute-done.2.refs_4_ = bf16[512,1024]{1,0:T(8,128)(2,1)} collective-permute-done((bf16[512,1024]{1,0:T(8,128)(2,1)}, bf16[512,1024]{1,0:T(8,128)(2,1)}, u32[]{:S(2)}, u32[]{:S(2)}) %collective-permute-start.2) | collective-permute-done | bytes 1048608 | tf_op jit(solution)/shard_map/ppermute | solution.py:17
  54.8 2.4 collective-permute-done.3.refs_5_
  57.2 2.3 fusion.12
  63.6 2.6 collective-permute-start.6
  70.2 94.1 %collective-permute-done.8 = bf16[256,768]{1,0:T(8,128)(2,1)S(1)} collective-permute-done((bf16[256,768]{1,0:T(8,128)(2,1)S(1)}, bf16[256,768]{1,0:T(8,128)(2,1)S(1)}, u32[]{:S(2)}, u32[]{:S(2)}) %collective-permute-start.8) | collective-permute-done | bytes 393248 | tf_op jit(solution)/shard_map/ppermute | solution.py:17
  165.5 21.4 %second_early.1.refs_4_ = bf16[1,16,6,256,256]{4,3,2,1,0:T(8,128)(2,1)} custom-call(bf16[1024,1024]{1,0:T(8,128)(2,1)} %collective-permute-done.refs_0_.refs_1_.refs_2_, bf16[1024,1024]{1,0:T(8,128)(2,1)} %collective-permute-done.refs_0_.refs_1_.refs_2_, bf16[1024,1024]{1,0:T(8,128)(2,1)} %collective-permute-done.refs_0_.refs_1_.refs_2_, ...), custom_call_target="tpu_custom_call" | custom-call | flops 1024 | bytes 1024 | tf_op jit(solution)/shard_map/second_early/pallas_call | solution.py:326
  188.4 18.1 %collective-permute-done.9 = bf16[256,768]{1,0:T(8,128)(2,1)S(1)} collective-permute-done((bf16[256,768]{1,0:T(8,128)(2,1)S(1)}, bf16[256,768]{1,0:T(8,128)(2,1)S(1)}, u32[]{:S(2)}, u32[]{:S(2)}) %collective-permute-start.9) | collective-permute-done | bytes 393248 | tf_op jit(solution)/shard_map/ppermute | solution.py:17
  207.3 10.5 %collective-permute-done.10 = bf16[256,768]{1,0:T(8,128)(2,1)} collective-permute-done((bf16[256,768]{1,0:T(8,128)(2,1)S(1)}, bf16[256,768]{1,0:T(8,128)(2,1)}, u32[]{:S(2)}, u32[]{:S(2)}) %collective-permute-start.10) | collective-permute-done | bytes 393248 | tf_op jit(solution)/shard_map/ppermute | solution.py:17
  221.3 2.7 collective-permute-start.15
  226.5 36.4 %hidden_grad.1 = (bf16[1024,4096]{1,0:T(8,128)(2,1)}, bf16[512,1024]{1,0:T(8,128)(2,1)}, bf16[512,1024]{1,0:T(8,128)(2,1)}, bf16[512,1024]{1,0:T(8,128)(2,1)}, b...) custom-call(bf16[1024,1024]{1,0:T(8,128)(2,1)} %collective-permute-done.refs_0_.refs_1_.refs_2_, ...), custom_call_target="tpu_custom_call" | custom-call | flops 1024 | bytes 1024 | tf_op jit(solution)/shard_map/hidden_grad/pallas_call | solution.py:197
  262.9 6.1 %collective-permute-done.14.refs_10_ = bf16[512,1024]{1,0:T(8,128)(2,1)S(1)} collective-permute-done((bf16[512,1024]{1,0:T(8,128)(2,1)}, bf16[512,1024]{1,0:T(8,128)(2,1)S(1)}, u32[]{:S(2)}, u32[]{:S(2)}) %collective-permute-start.14) | collective-permute-done | bytes 1048608 | tf_op jit(solution)/shard_map/ppermute | solution.py:17
  272.1 2.7 collective-permute-start.21
  276.0 50.6 %collective-permute-done.17 = bf16[512,256]{1,0:T(8,128)(2,1)S(1)} collective-permute-done((bf16[512,256]{1,0:T(8,128)(2,1)S(1)}, bf16[512,256]{1,0:T(8,128)(2,1)S(1)}, u32[]{:S(2)}, u32[]{:S(2)}) %collective-permute-start.17) | collective-permute-done | bytes 262176 | tf_op jit(solution)/shard_map/ppermute | solution.py:17
  327.1 21.6 %near_parts.1 = (f32[1024,1024]{1,0:T(8,128)}, bf16[512,1024]{1,0:T(8,128)(2,1)}, bf16[512,1024]{1,0:T(8,128)(2,1)}) custom-call(bf16[1024,4096]{1,0:T(8,128)(2,1)} %get-tuple-element.46.hid.refs_13_, bf16[1,16,6,256,256]{4,3,2,1,0:T(8,128)(2,1)} %refs_1_.1, bf16[1,16,6,256,256]{4,3,2,1,0:T(8,128)(2,1)} %refs_1_.1), custom_call_target="tpu_custom_call" | custom-call | flops 1024 | bytes 1024 | tf_op jit(solution)/shard_map/near_parts/pallas_call | solution.py:245
  349.2 2.6 collective-permute-start.22
  352.0 3.1 fusion.2
  355.1 14.0 %second_late.1 = (bf16[1,16,6,256,256]{4,3,2,1,0:T(8,128)(2,1)}, bf16[1,4096,256]{2,1,0:T(8,128)(2,1)}) custom-call(bf16[1024,1024]{1,0:T(8,128)(2,1)} %collective-permute-done.5.refs_4_.refs_0_, bf16[1024,1024]{1,0:T(8,128)(2,1)} %collective-permute-done.6.refs_5_.refs_1_, ...), custom_call_target="tpu_custom_call", output_to_operand_aliasing={{0}: (4, {})} | custom-call | flops 1024 | bytes 1024 | tf_op jit(solution)/shard_map/second_late/pallas_call | solution.py:326
  369.1 30.9 %first_grad.1 = (bf16[1,16,6,256,256]{4,3,2,1,0:T(8,128)(2,1)}, bf16[1,256,4096]{2,1,0:T(8,128)(2,1)}) custom-call(bf16[1024,1024]{1,0:T(8,128)(2,1)} %bitcast.29, bf16[1024,1024]{1,0:T(8,128)(2,1)} %bitcast.30, bf16[1024,1024]{1,0:T(8,128)(2,1)} %bitcast.31, bf16[1024,1024]{1,0:T(8,128)(2,1)} %collective-permute-done.1.refs_3_.refs_9_, ...), custom_call_target="tpu_custom_call" | custom-call | flops 1024 | bytes 1024 | tf_op jit(solution)/shard_map/first_grad/pallas_call | solution.py:378
  402.8 4.4 %add_add_fusion = f32[1024,1024]{1,0:T(8,128)} fusion(f32[1024,1024]{1,0:T(8,128)S(1)} %copy-done.5, bf16[512,1024]{1,0:T(8,128)(2,1)} %copy-done.15, bf16[512,1024]{1,0:T(8,128)(2,1)} %copy-done.14, bf16[1,1024,256]{2,1,0:T(8,128)(2,1)S(1)} %copy-done, bf16[512,256]{1,0:T(8,128)(2,1)S(1)} %get-tuple-element.89, bf16[512,256]{1,0:T(8,128)(2,1)S(1)} %get-tuple-element.88), kind=kOutput, calls=%fused_computation.1 | convolution fusion | flops 544210944 | bytes 11534336 | tf_op jit(solution)/shard_map/dot_general | solution.py:51
  408.2 4.3 %fusion = bf16[1,1024,1024]{2,1,0:T(8,128)(2,1)} fusion(f32[1024,1024]{1,0:T(8,128)} %add_add_fusion, bf16[512,1024]{1,0:T(8,128)(2,1)} %collective-permute-done.22, bf16[512,1024]{1,0:T(8,128)(2,1)S(1)} %copy-done.10, bf16[512,1024]{1,0:T(8,128)(2,1)} %collective-permute-done.23, bf16[512,1024]{1,0:T(8,128)(2,1)S(1)} %copy-done.12), kind=kLoop, calls=%fused_computation.3 | loop fusion | flops 11534336 | bytes 10485760 | tf_op jit(solution)/shard_map/broadcast_in_dim | solution.py:479
  (90 shorter events, 29.5 us)
Async XLA Ops:
  0.6 56.6 %collective-permute-start.1 = (bf16[1024,1024]{1,0:T(8,128)(2,1)}, bf16[1024,1024]{1,0:T(8,128)(2,1)}, u32[]{:S(2)}, u32[]{:S(2)}) collective-permute-start(bf16[1024,1024]{1,0:T(8,128)(2,1)} %bitcast.28), channel_id=1, source_target_pairs={{0,1},{1,0},{2,3},{3,2},{4,5},{5,4},{6,7},{7,6},{8,9},{9,8},{10,11... | collective-permute-start | bytes 6291464 | tf_op jit(solution)/shard_map/ppermute | solution.py:17
  1.2 56.1 %collective-permute-start = (bf16[1024,1024]{1,0:T(8,128)(2,1)}, bf16[1024,1024]{1,0:T(8,128)(2,1)}, u32[]{:S(2)}, u32[]{:S(2)}) collective-permute-start(bf16[1024,1024]{1,0:T(8,128)(2,1)} %bitcast.36), channel_id=1, source_target_pairs={{0,24},{8,0},{16,8},{24,16},{1,25},{9,1},{17,9},{25,17},{2,26},{10... | collective-permute-start | bytes 6291464 | tf_op jit(solution)/shard_map/ppermute | solution.py:22
  6.9 47.9 %collective-permute-start.2 = (bf16[512,1024]{1,0:T(8,128)(2,1)}, bf16[512,1024]{1,0:T(8,128)(2,1)}, u32[]{:S(2)}, u32[]{:S(2)}) collective-permute-start(bf16[512,1024]{1,0:T(8,128)(2,1)} %slice_bitcast_fusion), channel_id=1, source_target_pairs={{0,2},{1,3},{2,0},{3,1},{4,6},{5,7},{6,4},{7,5},{8,10},{9,11},{10,... | collective-permute-start | bytes 3145736 | tf_op jit(solution)/shard_map/ppermute | solution.py:17
  8.5 48.7 %collective-permute-start.3 = (bf16[512,1024]{1,0:T(8,128)(2,1)}, bf16[512,1024]{1,0:T(8,128)(2,1)}, u32[]{:S(2)}, u32[]{:S(2)}) collective-permute-start(bf16[512,1024]{1,0:T(8,128)(2,1)} %slice_bitcast_fusion), channel_id=1, source_target_pairs={{0,4},{1,5},{2,6},{3,7},{4,0},{5,1},{6,2},{7,3},{8,12},{9,13},{10,... | collective-permute-start | bytes 3145736 | tf_op jit(solution)/shard_map/ppermute | solution.py:17
  62.7 3.8 collective-permute-start.7
  62.7 102.8 %collective-permute-start.4 = (bf16[1024,1024]{1,0:T(8,128)(2,1)}, bf16[1024,1024]{1,0:T(8,128)(2,1)}, u32[]{:S(2)}, u32[]{:S(2)}) collective-permute-start(bf16[1024,1024]{1,0:T(8,128)(2,1)} %collective-permute-done.refs_0_.refs_1_.refs_2_), channel_id=1, source_target_pairs={{0,1},{1,0},{2,3},{3,2},{4,5},{5,4},{6,7},{7,6},{8,9},{9,8},{10,11... | collective-permute-start | bytes 6291464 | tf_op jit(solution)/shard_map/ppermute | solution.py:17
  63.2 143.3 %collective-permute-start.5 = (bf16[1024,1024]{1,0:T(8,128)(2,1)}, bf16[1024,1024]{1,0:T(8,128)(2,1)}, u32[]{:S(2)}, u32[]{:S(2)}) collective-permute-start(bf16[1024,1024]{1,0:T(8,128)(2,1)} %collective-permute-done.refs_0_.refs_1_.refs_2_), channel_id=1, source_target_pairs={{0,2},{1,3},{2,0},{3,1},{4,6},{5,7},{6,4},{7,5},{8,10},{9,11},{10,... | collective-permute-start | bytes 6291464 | tf_op jit(solution)/shard_map/ppermute | solution.py:17
  63.6 142.9 %collective-permute-start.6 = (bf16[1024,1024]{1,0:T(8,128)(2,1)}, bf16[1024,1024]{1,0:T(8,128)(2,1)}, u32[]{:S(2)}, u32[]{:S(2)}) collective-permute-start(bf16[1024,1024]{1,0:T(8,128)(2,1)} %collective-permute-done.refs_0_.refs_1_.refs_2_), channel_id=1, source_target_pairs={{0,4},{1,5},{2,6},{3,7},{4,0},{5,1},{6,2},{7,3},{8,12},{9,13},{10,... | collective-permute-start | bytes 6291464 | tf_op jit(solution)/shard_map/ppermute | solution.py:17
  69.7 94.6 %collective-permute-start.8 = (bf16[256,768]{1,0:T(8,128)(2,1)S(1)}, bf16[256,768]{1,0:T(8,128)(2,1)S(1)}, u32[]{:S(2)}, u32[]{:S(2)}) collective-permute-start(bf16[256,768]{1,0:T(8,128)(2,1)S(1)} %dynamic-slice_convert_fusion), channel_id=1, source_target_pairs={{0,2},{1,3},{2,0},{3,1},{4,6},{5,7},{6,4},{7,5},{8,10},{9,11},{10,... | collective-permute-start | bytes 1179656 | tf_op jit(solution)/shard_map/ppermute | solution.py:17
  187.0 19.5 %collective-permute-start.9 = (bf16[256,768]{1,0:T(8,128)(2,1)S(1)}, bf16[256,768]{1,0:T(8,128)(2,1)S(1)}, u32[]{:S(2)}, u32[]{:S(2)}) collective-permute-start(bf16[256,768]{1,0:T(8,128)(2,1)S(1)} %convert_element_type.53), channel_id=1, source_target_pairs={{0,4},{1,5},{2,6},{3,7},{4,0},{5,1},{6,2},{7,3},{8,12},{9,13},{10,... | collective-permute-start | bytes 1179656 | tf_op jit(solution)/shard_map/ppermute | solution.py:17
  206.6 11.2 %collective-permute-start.10 = (bf16[256,768]{1,0:T(8,128)(2,1)S(1)}, bf16[256,768]{1,0:T(8,128)(2,1)}, u32[]{:S(2)}, u32[]{:S(2)}) collective-permute-start(bf16[256,768]{1,0:T(8,128)(2,1)S(1)} %add_convert_fusion.1), channel_id=1, source_target_pairs={{0,2},{1,3},{2,0},{3,1},{4,6},{5,7},{6,4},{7,5},{8,10},{9,11},{10,... | collective-permute-start | bytes 1179656 | tf_op jit(solution)/shard_map/ppermute | solution.py:17
  219.9 4.1 collective-permute-start.11
  221.0 48.0 %collective-permute-start.14 = (bf16[512,1024]{1,0:T(8,128)(2,1)}, bf16[512,1024]{1,0:T(8,128)(2,1)S(1)}, u32[]{:S(2)}, u32[]{:S(2)}) collective-permute-start(bf16[512,1024]{1,0:T(8,128)(2,1)} %slice.7), channel_id=1, source_target_pairs={{0,2},{1,3},{2,0},{3,1},{4,6},{5,7},{6,4},{7,5},{8,10},{9,11},{10,... | collective-permute-start | bytes 3145736 | tf_op jit(solution)/shard_map/ppermute | solution.py:17
  221.3 49.1 %collective-permute-start.15 = (bf16[512,1024]{1,0:T(8,128)(2,1)}, bf16[512,1024]{1,0:T(8,128)(2,1)S(1)}, u32[]{:S(2)}, u32[]{:S(2)}) collective-permute-start(bf16[512,1024]{1,0:T(8,128)(2,1)} %slice.7), channel_id=1, source_target_pairs={{0,4},{1,5},{2,6},{3,7},{4,0},{5,1},{6,2},{7,3},{8,12},{9,13},{10,... | collective-permute-start | bytes 3145736 | tf_op jit(solution)/shard_map/ppermute | solution.py:17
  271.7 3.0 collective-permute-start.16
  271.8 77.4 %collective-permute-start.20 = (bf16[512,1024]{1,0:T(8,128)(2,1)}, bf16[512,1024]{1,0:T(8,128)(2,1)S(1)}, u32[]{:S(2)}, u32[]{:S(2)}) collective-permute-start(bf16[512,1024]{1,0:T(8,128)(2,1)} %get-tuple-element.57), channel_id=1, source_target_pairs={{0,4},{1,5},{2,6},{3,7},{4,0},{5,1},{6,2},{7,3},{8,12},{9,13},{10,... | collective-permute-start | bytes 3145736 | tf_op jit(solution)/shard_map/ppermute | solution.py:17
  272.1 77.1 %collective-permute-start.21 = (bf16[512,1024]{1,0:T(8,128)(2,1)}, bf16[512,1024]{1,0:T(8,128)(2,1)S(1)}, u32[]{:S(2)}, u32[]{:S(2)}) collective-permute-start(bf16[512,1024]{1,0:T(8,128)(2,1)} %get-tuple-element.58), channel_id=1, source_target_pairs={{0,2},{1,3},{2,0},{3,1},{4,6},{5,7},{6,4},{7,5},{8,10},{9,11},{10,... | collective-permute-start | bytes 3145736 | tf_op jit(solution)/shard_map/ppermute | solution.py:17
  275.9 50.6 %collective-permute-start.17 = (bf16[512,256]{1,0:T(8,128)(2,1)S(1)}, bf16[512,256]{1,0:T(8,128)(2,1)S(1)}, u32[]{:S(2)}, u32[]{:S(2)}) collective-permute-start(bf16[512,256]{1,0:T(8,128)(2,1)S(1)} %convert_element_type.57), channel_id=1, source_target_pairs={{0,2},{1,3},{2,0},{3,1},{4,6},{5,7},{6,4},{7,5},{8,10},{9,11},{10,... | collective-permute-start | bytes 786440 | tf_op jit(solution)/shard_map/ppermute | solution.py:17
  326.7 25.2 %collective-permute-start.18 = (bf16[512,256]{1,0:T(8,128)(2,1)S(1)}, bf16[512,256]{1,0:T(8,128)(2,1)S(1)}, u32[]{:S(2)}, u32[]{:S(2)}) collective-permute-start(bf16[512,256]{1,0:T(8,128)(2,1)S(1)} %get-tuple-element.80), channel_id=1, source_target_pairs={{0,4},{1,5},{2,6},{3,7},{4,0},{5,1},{6,2},{7,3},{8,12},{9,13},{10,... | collective-permute-start | bytes 786440 | tf_op jit(solution)/shard_map/ppermute | solution.py:17
  348.7 52.1 %collective-permute-start.12 = (bf16[512,1024]{1,0:T(8,128)(2,1)}, bf16[512,1024]{1,0:T(8,128)(2,1)S(1)}, u32[]{:S(2)}, u32[]{:S(2)}) collective-permute-start(bf16[512,1024]{1,0:T(8,128)(2,1)} %get-tuple-element.48), channel_id=1, source_target_pairs={{0,1},{1,0},{2,3},{3,2},{4,5},{5,4},{6,7},{7,6},{8,9},{9,8},{10,11... | collective-permute-start | bytes 3145736 | tf_op jit(solution)/shard_map/ppermute | solution.py:17
  348.7 52.1 %collective-permute-start.13 = (bf16[512,1024]{1,0:T(8,128)(2,1)}, bf16[512,1024]{1,0:T(8,128)(2,1)S(1)}, u32[]{:S(2)}, u32[]{:S(2)}) collective-permute-start(bf16[512,1024]{1,0:T(8,128)(2,1)} %get-tuple-element.49), channel_id=1, source_target_pairs={{0,1},{1,0},{2,3},{3,2},{4,5},{5,4},{6,7},{7,6},{8,9},{9,8},{10,11... | collective-permute-start | bytes 3145736 | tf_op jit(solution)/shard_map/ppermute | solution.py:17
  349.2 59.0 %collective-permute-start.22 = (bf16[512,1024]{1,0:T(8,128)(2,1)}, bf16[512,1024]{1,0:T(8,128)(2,1)}, u32[]{:S(2)}, u32[]{:S(2)}) collective-permute-start(bf16[512,1024]{1,0:T(8,128)(2,1)} %get-tuple-element.64), channel_id=1, source_target_pairs={{0,4},{1,5},{2,6},{3,7},{4,0},{5,1},{6,2},{7,3},{8,12},{9,13},{10,... | collective-permute-start | bytes 3145736 | tf_op jit(solution)/shard_map/ppermute | solution.py:17
  351.8 56.4 %collective-permute-start.23 = (bf16[512,1024]{1,0:T(8,128)(2,1)}, bf16[512,1024]{1,0:T(8,128)(2,1)}, u32[]{:S(2)}, u32[]{:S(2)}) collective-permute-start(bf16[512,1024]{1,0:T(8,128)(2,1)} %get-tuple-element.65), channel_id=1, source_target_pairs={{0,2},{1,3},{2,0},{3,1},{4,6},{5,7},{6,4},{7,5},{8,10},{9,11},{10,... | collective-permute-start | bytes 3145736 | tf_op jit(solution)/shard_map/ppermute | solution.py:17
  351.9 48.1 %collective-permute-start.19 = (bf16[512,256]{1,0:T(8,128)(2,1)S(1)}, bf16[512,256]{1,0:T(8,128)(2,1)S(1)}, u32[]{:S(2)}, u32[]{:S(2)}) collective-permute-start(bf16[512,256]{1,0:T(8,128)(2,1)S(1)} %add_convert_fusion.2), channel_id=1, source_target_pairs={{0,1},{1,0},{2,3},{3,2},{4,5},{5,4},{6,7},{7,6},{8,9},{9,8},{10,11... | collective-permute-start | bytes 786440 | tf_op jit(solution)/shard_map/ppermute | solution.py:17
  (17 other events, 284.5 us)

commit v4 on v3

--- a/solution.py
+++ b/solution.py
@@ -7,7 +7,8 @@
 from jax.experimental.pallas import tpu as pltpu
 from jax.sharding import PartitionSpec as P
 
-CHUNKS = 2
+UP_SHARES = ((3, 0, 5), (4, 4, 0))
+BACK_SHARES = ((2, 4, 2), (7, 1, 0))
 BF16 = jnp.bfloat16
 F32 = jnp.float32
 
@@ -22,29 +23,61 @@
     return lax.ppermute(value, "section", [(i, (i - 1) % peers) for i in range(peers)])
 
 
-def tree_sum(value, halvings, before_swap=(), before_gather=()):
-    bits = lax.axis_size("tensor").bit_length() - 1
-    place = lax.axis_index("tensor")
-    for bit in range(halvings):
-        half = value.shape[0] // 2
-        mine = (place >> bit) & 1
-        keep = lax.dynamic_slice_in_dim(value, mine * half, half)
-        give = lax.dynamic_slice_in_dim(value, (1 - mine) * half, half)
-        give = give if bit == 0 else give.astype(BF16)
-        value = keep + swapped(give, bit).astype(F32)
-    value = after(value, *before_swap)
-    stages = []
-    for bit in range(halvings, bits):
-        value = value + swapped(value.astype(BF16), bit).astype(F32)
-        stages.append(value)
-    value = after(value.astype(BF16), *before_gather)
-    for bit in reversed(range(halvings)):
-        mine = (place >> bit) & 1
-        other = swapped(value, bit)
-        first = jnp.where(mine == 0, value, other)
-        second = jnp.where(mine == 0, other, value)
-        value = jnp.concatenate([first, second])
-    return value, stages[0]
+def halved(value, bit, work=()):
+    half = value.shape[0] // 2
+    mine = (lax.axis_index("tensor") >> bit) & 1
+    keep = lax.dynamic_slice_in_dim(value, mine * half, half)
+    give = lax.dynamic_slice_in_dim(value, (1 - mine) * half, half)
+    give = give if bit == 0 else give.astype(BF16)
+    return keep + after(swapped(give, bit), *work).astype(F32)
+
+
+def gathered(value, bit):
+    mine = (lax.axis_index("tensor") >> bit) & 1
+    other = swapped(value, bit)
+    first = jnp.where(mine == 0, value, other)
+    second = jnp.where(mine == 0, other, value)
+    return jnp.concatenate([first, second])
+
+
+def shares_of(shares, count):
+    return [shares[0]] * (count - 1) + [shares[1]]
+
+
+def cut(value, shares):
+    pieces, start = [], 0
+    for share in shares:
+        stop = start + value.shape[0] * share // 8
+        pieces.append(value[start:stop] if share else None)
+        start = stop
+    return pieces
+
+
+def sent(piece, bit, *others):
+    return None if piece is None else swapped(after(piece, *others), bit)
+
+
+def kept(pieces):
+    return [piece for piece in pieces if piece is not None]
+
+
+def relay(links, value, work):
+    last = len(links)
+    firsts = [sent(link[0], bit) for bit, link in enumerate(links, 1)]
+    value = halved(value, 0)
+    done = work(value)
+    seconds = [sent(link[1], bit, value) for bit, link in enumerate(links[:-1], 1)]
+    for bit in range(1, last):
+        value = halved(value, bit, done if bit == 1 else ())
+    value = after(value, *firsts)
+    seconds.append(sent(links[-1][1], last, value))
+    value = (value + swapped(value.astype(BF16), last).astype(F32)).astype(BF16)
+    thirds = [sent(link[2], bit, value) for bit, link in enumerate(links, 1)]
+    value = after(value, *kept(seconds[:-1]))
+    for bit in reversed(range(1, last)):
+        value = gathered(value, bit)
+    value = gathered(after(value, seconds[-1]), 0)
+    return value, [kept(link) for link in zip(firsts, seconds, thirds)]
 
 
 def nt(left, right):
@@ -119,14 +152,23 @@
     )
 
 
-def hidden_kernel(links, late, group, *refs):
-    ups, refs = refs[:links], refs[links:]
+def taken(refs, counts):
+    groups = []
+    for count in counts:
+        groups.append(refs[:count])
+        refs = refs[count:]
+    return groups, refs
+
+
+def hidden_kernel(counts, part_counts, group, *refs):
+    links, late = len(counts), len(part_counts)
+    ups, refs = taken(refs, counts)
     proj, refs = refs[0], refs[1:]
     seconds, refs = refs[:links], refs[links:]
     left_two, slope, right_one, refs = refs[0], refs[1], refs[2], refs[3:]
     firsts, refs = refs[:late], refs[late:]
     hidden, refs = refs[0], refs[1:]
-    parts, refs = refs[: late * CHUNKS], refs[late * CHUNKS :]
+    parts, refs = taken(refs, part_counts)
     rank, up_all, hid_all = refs
     c, j = pl.program_id(0), pl.program_id(1)
     size = hidden.shape[1]
@@ -134,7 +176,11 @@
     @pl.when(j == 0)
     def _():
         for k in range(links):
-            up_all[:, k * size : (k + 1) * size] = ups[k][...]
+            start = 0
+            for piece in ups[k]:
+                stop = start + piece.shape[0]
+                up_all[start:stop, k * size : (k + 1) * size] = piece[...]
+                start = stop
         up_all[:, links * size :] = proj[...]
 
     weights = wide([ref[...] for ref in seconds] + [left_two[...]])
@@ -148,9 +194,11 @@
         group_grad = hid_all[...]
         for n, ref in enumerate(firsts):
             part = nt(group_grad, wide([ref[g] for g in range(group)])).astype(BF16)
-            for m in range(CHUNKS):
-                piece = parts[n * CHUNKS + m]
-                piece[...] = part[m * piece.shape[0] : (m + 1) * piece.shape[0]]
+            start = 0
+            for piece in parts[n]:
+                stop = start + piece.shape[0]
+                piece[...] = part[start:stop]
+                start = stop
         term = nt(group_grad, right_one[...])
 
         @pl.when(c == 0)
@@ -162,40 +210,46 @@
             rank[...] += term
 
 
-def hidden_call(ups, flips, proj, second, left_two, slope, right_one, first, late_from, chunk):
-    rows = ups[-1][0].shape[0]
+def piece_specs(sets, flips, size):
+    return [
+        pl.BlockSpec((piece.shape[0], size), lambda c, j, flip=flip: (0, c ^ flip))
+        for pieces, flip in zip(sets, flips)
+        for piece in pieces
+    ]
+
+
+def hidden_call(ups, flips, proj, second, left_two, slope, right_one, first, late_from):
+    rows, width = slope.shape
     _, hid_count, links, size, _ = first.shape
     count_in = ups[0][0].shape[1] // size
     group = hid_count // count_in
     rank = proj.shape[1]
     late = links - late_from
-    in_specs = [
-        pl.BlockSpec((rows, size), lambda c, j, flip=flip, place=place: (place, c ^ flip))
-        for (_, place), flip in zip(ups, flips)
-    ]
-    in_specs.append(pl.BlockSpec((rows, rank), lambda c, j: (chunk, 0)))
+    shares = [[rows * n // 8 for n in link if n] for link in shares_of(BACK_SHARES, late)]
+    pieces = [n for link in shares for n in link]
+    in_specs = piece_specs(ups, flips, size)
+    in_specs.append(pl.BlockSpec((rows, rank), lambda c, j: (0, 0)))
     in_specs += [
         pl.BlockSpec((None, None, None, size, size), lambda c, j, k=k: (0, c * group + j, k, 0, 0))
         for k in range(links)
     ]
     in_specs.append(pl.BlockSpec((None, size, rank), lambda c, j: (0, c * group + j, 0)))
-    in_specs.append(pl.BlockSpec((rows, size), lambda c, j: (chunk, c * group + j)))
+    in_specs.append(pl.BlockSpec((rows, size), lambda c, j: (0, c * group + j)))
     in_specs.append(pl.BlockSpec((None, rank, group * size), lambda c, j: (0, 0, c)))
     in_specs += [
         pl.BlockSpec((None, group, None, size, size), lambda c, j, k=k: (0, c, k, 0, 0))
         for k in range(late_from, links)
     ]
     out_specs = [pl.BlockSpec((rows, size), lambda c, j: (0, c * group + j))]
-    out_specs += [pl.BlockSpec((rows // CHUNKS, size), lambda c, j: (0, c))] * (late * CHUNKS)
+    out_specs += [pl.BlockSpec((n, size), lambda c, j: (0, c)) for n in pieces]
     out_specs.append(pl.BlockSpec((rows, rank), lambda c, j: (0, 0)))
-    width = hid_count * size
     out_shape = [jax.ShapeDtypeStruct((rows, width), BF16)]
-    out_shape += [
-        jax.ShapeDtypeStruct((rows // CHUNKS, count_in * size), BF16)
-    ] * (late * CHUNKS)
+    out_shape += [jax.ShapeDtypeStruct((n, count_in * size), BF16) for n in pieces]
     out_shape.append(jax.ShapeDtypeStruct((rows, rank), F32))
     return pl.pallas_call(
-        functools.partial(hidden_kernel, links, late, group),
+        functools.partial(
+            hidden_kernel, [len(link) for link in ups], [len(link) for link in shares], group
+        ),
         grid=(count_in, group),
         in_specs=in_specs,
         out_specs=out_specs,
@@ -207,7 +261,7 @@
         name="hidden_grad",
         **params(2),
     )(
-        *[up for up, _ in ups], proj, *[second] * links, left_two, slope, right_one, *[first] * late
+        *[piece for link in ups for piece in link], proj, *[second] * links, left_two, slope, right_one, *[first] * late
     )
 
 
@@ -254,11 +308,11 @@
         ],
         out_specs=[
             pl.BlockSpec((rows, size), lambda c, kk: (0, c)),
-            *[pl.BlockSpec((rows // CHUNKS, size), lambda c, kk: (0, c))] * CHUNKS,
+            *[pl.BlockSpec((rows // 2, size), lambda c, kk: (0, c))] * 2,
         ],
         out_shape=[
             jax.ShapeDtypeStruct((rows, width), F32),
-            *[jax.ShapeDtypeStruct((rows // CHUNKS, width), BF16)] * CHUNKS,
+            *[jax.ShapeDtypeStruct((rows // 2, width), BF16)] * 2,
         ],
         scratch_shapes=[pltpu.VMEM((rows, size), F32)],
         name="near_parts",
@@ -266,27 +320,29 @@
     )(hidden, first, first)
 
 
-def second_kernel(count, group, has_proj, *refs):
-    ups, refs = refs[:count], refs[count:]
+def second_kernel(counts, group, has_proj, *refs):
+    count = len(counts)
+    ups, refs = taken(refs, counts)
     if has_proj:
         proj, act, _, out, left_two, turned = refs
     else:
         act, out, turned = refs
     k = pl.program_id(1)
-    size = ups[0].shape[1]
+    size = ups[0][0].shape[1]
 
     @pl.when(k == 0)
     def _():
         for g in range(group):
             turned[g * size : (g + 1) * size, :] = act[:, g * size : (g + 1) * size].T
 
-    def store(up):
+    def store(pieces):
+        up = jnp.concatenate([piece[...] for piece in pieces], axis=0)
         grads = nn(turned[...], up).astype(BF16)
         for g in range(group):
             out[g] = grads[g * size : (g + 1) * size]
 
     for n in range(count):
-        pl.when(k == n)(lambda n=n: store(ups[n][...]))
+        pl.when(k == n)(lambda n=n: store(ups[n]))
 
     if has_proj:
 
@@ -299,13 +355,11 @@
     count = len(ups)
     tokens = act.shape[0]
     _, hid_count, links, size, _ = shape
-    count_in = ups[0].shape[1] // size
+    count_in = ups[0][0].shape[1] // size
     group = hid_count // count_in
     has_proj = proj is not None
-    in_specs = [
-        pl.BlockSpec((tokens, size), lambda c, k, flip=flip: (0, c ^ flip)) for flip in flips
-    ]
-    args = list(ups)
+    in_specs = piece_specs(ups, flips, size)
+    args = [piece for link in ups for piece in link]
     out_specs = [
         pl.BlockSpec((None, group, None, size, size), lambda c, k: (0, c, start + k, 0, 0))
     ]
@@ -324,7 +378,7 @@
         args.append(partial)
         aliases = {len(args) - 1: 0}
     return pl.pallas_call(
-        functools.partial(second_kernel, count, group, has_proj),
+        functools.partial(second_kernel, [len(link) for link in ups], group, has_proj),
         grid=(count_in, count),
         in_specs=in_specs,
         out_specs=out_specs,
@@ -336,47 +390,39 @@
     )(*args)
 
 
-def first_kernel(links, chunks, rows, *refs):
-    ins, refs = refs[: links * chunks], refs[links * chunks :]
-    proj, refs = refs[0], refs[1:]
-    hids, refs = refs[:1], refs[1:]
-    out, right_one, in_all = refs
-    size = hids[0].shape[1]
+def first_kernel(counts, *refs):
+    links = len(counts)
+    ins, refs = taken(refs, counts)
+    proj, hid, out, right_one, in_all = refs
+    size = hid.shape[1]
 
     @pl.when(pl.program_id(1) == 0)
     def _():
-        for m in range(chunks):
-            for k in range(links):
-                in_all[k * size : (k + 1) * size, m * rows : (m + 1) * rows] = ins[m * links + k][
-                    ...
-                ].T
+        for k in range(links):
+            start = 0
+            for piece in ins[k]:
+                stop = start + piece.shape[0]
+                in_all[k * size : (k + 1) * size, start:stop] = piece[...].T
+                start = stop
         in_all[links * size :, :] = proj[...].T
 
-    hid = jnp.concatenate([ref[...] for ref in hids], axis=0)
-    grads = nn(in_all[...], hid).astype(BF16)
+    grads = nn(in_all[...], hid[...]).astype(BF16)
     for k in range(links):
         out[k] = grads[k * size : (k + 1) * size]
     right_one[...] = grads[links * size :]
 
 
-def first_call(ins, flips, proj, hids, shape):
-    chunks = len(ins)
-    tokens = hids[0].shape[0]
-    rows = tokens // chunks
+def first_call(ins, flips, proj, hidden, shape):
+    tokens, width = hidden.shape
     _, hid_count, links, size, _ = shape
-    count_in = ins[0][0][0].shape[1] // size
+    count_in = ins[0][0].shape[1] // size
     group = hid_count // count_in
     rank = proj.shape[1]
-    in_specs = [
-        pl.BlockSpec((rows, size), lambda c, j, flip=flip, place=place: (place, c ^ flip))
-        for chunk in ins
-        for (_, place), flip in zip(chunk, flips)
-    ]
+    in_specs = piece_specs(ins, flips, size)
     in_specs.append(pl.BlockSpec((tokens, rank), lambda c, j: (0, 0)))
-    in_specs += [pl.BlockSpec((tokens, size), lambda c, j: (0, c * group + j))]
-    width = hid_count * size
+    in_specs.append(pl.BlockSpec((tokens, size), lambda c, j: (0, c * group + j)))
     return pl.pallas_call(
-        functools.partial(first_kernel, links, chunks, rows),
+        functools.partial(first_kernel, [len(link) for link in ins]),
         grid=(count_in, group),
         in_specs=in_specs,
         out_specs=[
@@ -392,7 +438,7 @@
         scratch_shapes=[pltpu.VMEM((links * size + rank, tokens), BF16)],
         name="first_grad",
         **params(2),
-    )(*[value for chunk in ins for value, _ in chunk], proj, *hids)
+    )(*[piece for link in ins for piece in link], proj, hidden)
 
 
 def body(
@@ -404,39 +450,36 @@
     count_in = feats // size
     near = count_in.bit_length()
     flips = [(1 << k) >> 1 if k < near else 0 for k in range(links)]
-    rows = tokens // CHUNKS
-    spans = [slice(m * rows, (m + 1) * rows) for m in range(CHUNKS)]
-
-    def sent(value):
-        far = [swapped(value, bit) for bit in reversed(range(1, links - near))]
-        return far[::-1]
+    spans = [slice(0, tokens // 2), slice(tokens // 2, tokens)]
+
+    far_count = links - near - 1
+
+    def half_sent(value):
+        return [swapped(value, bit) for bit in reversed(range(1, far_count + 1))][::-1]
 
     ranks = left_one.shape[2]
     first_half, second_half = spans
 
     in_core = swapped(inputs[0], 0)
-    in_one = sent(inputs[0, first_half])
+    in_one = half_sent(inputs[0, first_half])
     act, slope, proj_act = gate_call(preact, left_two, size)
     early = jnp.concatenate([nn(inputs[0], left_one[0]), proj_act], axis=1)
 
     upstream = after(shifted(handoff[0]), in_core, early, *in_one)
-    up_far = sent(upstream)
     up_core = swapped(upstream, 0)
-    (second_part,) = second_call(
-        [upstream] * near + [up_core], flips[: near + 1], act, shape, 0
-    )
-    sums, _ = tree_sum(
+    near_ups = [[upstream]] * near + [[up_core]]
+    (second_part,) = second_call(near_ups, flips[: near + 1], act, shape, 0)
+    up_shares = shares_of(UP_SHARES, far_count)
+    sums, far_ups = relay(
+        [cut(upstream, shares) for shares in up_shares],
         jnp.concatenate([nt(upstream, right_two[0]), early], axis=1),
-        links - near - 1,
-        [second_part],
-        up_far,
+        lambda stage: [second_part],
     )
     proj_grad, proj_in, proj_act = jnp.split(sums, (ranks, 2 * ranks), axis=1)
-    up_set = [(value, 0) for value in [upstream] * near + [up_core] + up_far]
-
-    in_two = sent(after(inputs[0], *up_far)[second_half])
+
+    in_two = half_sent(after(inputs[0], far_ups[-1][1])[second_half])
     hidden, *parts, back = hidden_call(
-        up_set,
+        near_ups + far_ups,
         flips,
         proj_grad,
         second_blocks,
@@ -445,37 +488,40 @@
         right_one,
         first_blocks,
         near + 1,
-        0,
-    )
-
-    def returned(pieces):
-        return [swapped(piece, k + 1) for k, piece in reversed(list(enumerate(pieces)))]
-
+    )
+    in_sets = [[inputs[0]]] * near + [[in_core]] + [list(link) for link in zip(in_one, in_two)]
     back, *parts = lax.optimization_barrier((back, *parts, *in_two))[: 1 + len(parts)]
-    far_one = returned(parts[::CHUNKS])
-    parts = parts[1::CHUNKS]
-    far_two = returned(lax.optimization_barrier((*parts, *far_one))[: len(parts)])
-    back_rank, stage = tree_sum(back, 1)
-    base, *beside = near_call(hidden, first_blocks, count_in, near)
-    beside = jnp.concatenate([swapped(piece, 0) for piece in beside], axis=0)
-    second_grad, lefttwo_grad = second_call(
-        up_far, flips[near + 1 :], act, shape, near + 1, after(proj_grad, stage), second_part
-    )
-    in_sets = [
-        [(inputs[0], m)] * near + [(in_core, m)] + [(value, 0) for value in values]
-        for m, values in enumerate([in_one, in_two])
+    found = []
+
+    def work(stage):
+        base, *beside = near_call(after(hidden, stage), first_blocks, count_in, near)
+        second_grad, lefttwo_grad = second_call(
+            far_ups, flips[near + 1 :], act, shape, near + 1, after(proj_grad, stage), second_part
+        )
+        first_grad, rightone_grad = first_call(
+            in_sets, flips, after(proj_in, stage), hidden, shape
+        )
+        beside = jnp.concatenate([swapped(piece, 0) for piece in beside], axis=0)
+        found.extend(
+            [base, beside, first_grad, second_grad, rightone_grad, lefttwo_grad]
+        )
+        return [base, lefttwo_grad, rightone_grad]
+
+    parts = iter(parts)
+    back_links = [
+        [next(parts) if share else None for share in shares]
+        for shares in shares_of(BACK_SHARES, far_count)
     ]
-    first_grad, rightone_grad = first_call(
-        in_sets, flips, after(proj_in, *far_one), [hidden], shape
-    )
+    back_rank, far = relay(back_links, back, work)
+    base, beside, first_grad, second_grad, rightone_grad, lefttwo_grad = found
     base = base + beside.astype(F32) + nt(back_rank, left_one[0])
     leftone_grad = nn(inputs[0].T, back_rank).astype(BF16)[None]
     righttwo_grad = nn(proj_act.T, upstream).astype(BF16)[None]
-    total, first_grad, leftone_grad, righttwo_grad = lax.optimization_barrier(
-        (base, first_grad, leftone_grad, righttwo_grad)
-    )
-    for pair in zip(far_one, far_two):
-        total = total + jnp.concatenate(pair, axis=0).astype(F32)
+    total, leftone_grad, righttwo_grad = lax.optimization_barrier(
+        (base, leftone_grad, righttwo_grad)
+    )
+    for link in far:
+        total = total + jnp.concatenate(link, axis=0).astype(F32)
     input_grad = total.astype(BF16)[None]
     return (
         input_grad,

time: 414 us -> 388 us (0.937)
  waiting for transfers between devices: 203 us -> 174 us
  starting transfers between devices: 23.5 us -> 28.8 us
    ppermute x23 -> x27, waiting for transfers between devices: 203 us -> 174 us  [swapped(): return lax.ppermute(value, 'tensor', pairs)]
    ppermute x23 -> x27, starting transfers between devices: 19.9 us -> 24.9 us  [swapped(): return lax.ppermute(value, 'tensor', pairs)]
  transfers between devices with their start and end apart: 24 -> 28, of which waited for: 9 -> 14; matrix products, arithmetic and copies ran while one was open for 5% -> 6% of each run, Pallas kernels for 36% -> 38%
where the time goes in v4:
time: 388 us; the launch traced here: 387 us
  waiting for transfers between devices  174 us (45%)
  Pallas kernels  147 us (38%)
  starting transfers between devices  28.8 us (7%)
  local copies, waits for them, and re-layouts  15.5 us (4%)
  other arithmetic  11.7 us (3%)
  matrix products  8.1 us (2%)
    ppermute x27, waiting for transfers between devices, swapped(): return lax.ppermute(value, 'tensor', pairs)  174 us
    pallas_call x1, Pallas kernels, hidden_call(): pl.pallas_call(functools.partial(hidden_kernel, [len(link) for link in up...  36.4 us
    pallas_call x2, Pallas kernels, second_call(): pl.pallas_call(functools.partial(second_kernel, [len(link) for link in up...  35.5 us
    pallas_call x1, Pallas kernels, first_call(): pl.pallas_call(functools.partial(first_kernel, [len(link) for link in ins...  30.7 us
    ppermute x27, starting transfers between devices, swapped(): return lax.ppermute(value, 'tensor', pairs)  24.9 us
    pallas_call x1, Pallas kernels, gate_call(): pl.pallas_call(functools.partial(gate_kernel, min(64, tokens)), grid=(wid...  23.1 us
    pallas_call x1, Pallas kernels, near_call(): pl.pallas_call(functools.partial(near_kernel, near, group), grid=(count_i...  21.5 us
  transfers between devices with their start and end apart: 28, of which 14 were waited for; matrix products, arithmetic and copies ran while one was open for 6% of the time, Pallas kernels for 38%

profile of v4, /device:TPU:0, one launch (start us, length us, event | category | flops | bytes accessed | tf_op | source)
XLA Modules:
  0.0 386.6 jit_solution(13769045513289630812)
XLA Ops:
  0.6 3.9 %collective-permute-start = (bf16[1024,1024]{1,0:T(8,128)(2,1)}, bf16[1024,1024]{1,0:T(8,128)(2,1)S(1)}, u32[]{:S(2)}, u32[]{:S(2)}) collective-permute-start(bf16[1024,1024]{1,0:T(8,128)(2,1)} %bitcast.33), channel_id=1, source_target_pairs={{0,24},{8,0},{16,8},{24,16},{1,25},{9,1},{17,9},{25,17},{2,26},{10... | collective-permute-start | bytes 6291464 | tf_op jit(solution)/shard_map/ppermute | solution.py:23
  6.9 2.6 collective-permute-start.3
  11.0 23.1 %gate.1 = (bf16[1024,4096]{1,0:T(8,128)(2,1)}, f32[1024,4096]{1,0:T(8,128)}, f32[1024,256]{1,0:T(8,128)}) custom-call(bf16[1,1024,4096]{2,1,0:T(8,128)(2,1)} %preact.1, bf16[1,4096,256]{2,1,0:T(8,128)(2,1)} %refs_15_.1), custom_call_target="tpu_custom_call" | custom-call | flops 1024 | bytes 1024 | tf_op jit(solution)/shard_map/gate/pallas_call | solution.py:124
  36.5 19.7 %collective-permute-done.3.refs_6_ = bf16[512,1024]{1,0:T(8,128)(2,1)} collective-permute-done((bf16[512,1024]{1,0:T(8,128)(2,1)}, bf16[512,1024]{1,0:T(8,128)(2,1)}, u32[]{:S(2)}, u32[]{:S(2)}) %collective-permute-start.3) | collective-permute-done | bytes 1048608 | tf_op jit(solution)/shard_map/ppermute | solution.py:18
  70.6 21.5 %second_early.1.refs_6_ = bf16[1,16,6,256,256]{4,3,2,1,0:T(8,128)(2,1)} custom-call(bf16[1024,1024]{1,0:T(8,128)(2,1)} %copy-done.1, bf16[1024,1024]{1,0:T(8,128)(2,1)} %copy-done.1, bf16[1024,1024]{1,0:T(8,128)(2,1)} %copy-done.1, bf16[1024,1024]{1,0:T(8,128)(2,1)} %collective-permute-done.4.refs_3_, bf16[1024,4096]{1,0:T(8,128)(2,1)} %get-tuple-element.52.refs_4_.refs_5_), custom_call_target="tpu_custom_call" | custom-call | flops 1024 | bytes 1024 | tf_op jit(solution)/shard_map/second_early/pallas_call | solution.py:380
  92.1 18.6 %collective-permute-done.7 = bf16[256,768]{1,0:T(8,128)(2,1)} collective-permute-done((bf16[256,768]{1,0:T(8,128)(2,1)}, bf16[256,768]{1,0:T(8,128)(2,1)}, u32[]{:S(2)}, u32[]{:S(2)}) %collective-permute-start.7) | collective-permute-done | bytes 393248 | tf_op jit(solution)/shard_map/ppermute | solution.py:18
  112.5 2.5 collective-permute-start.9
  115.5 40.4 %collective-permute-done.9 = bf16[256,768]{1,0:T(8,128)(2,1)S(1)} collective-permute-done((bf16[256,768]{1,0:T(8,128)(2,1)S(1)}, bf16[256,768]{1,0:T(8,128)(2,1)S(1)}, u32[]{:S(2)}, u32[]{:S(2)}) %collective-permute-start.9) | collective-permute-done | bytes 393248 | tf_op jit(solution)/shard_map/ppermute | solution.py:18
  159.9 25.9 %collective-permute-done.12 = bf16[256,768]{1,0:T(8,128)(2,1)} collective-permute-done((bf16[256,768]{1,0:T(8,128)(2,1)}, bf16[256,768]{1,0:T(8,128)(2,1)}, u32[]{:S(2)}, u32[]{:S(2)}) %collective-permute-start.12) | collective-permute-done | bytes 393248 | tf_op jit(solution)/shard_map/ppermute | solution.py:18
  192.0 24.2 %collective-permute-done.10.refs_5_.refs_1_ = bf16[640,1024]{1,0:T(8,128)(2,1)S(1)} collective-permute-done((bf16[640,1024]{1,0:T(8,128)(2,1)}, bf16[640,1024]{1,0:T(8,128)(2,1)S(1)}, u32[]{:S(2)}, u32[]{:S(2)}) %collective-permute-start.10) | collective-permute-done | bytes 1310752 | tf_op jit(solution)/shard_map/ppermute | solution.py:18
  217.3 36.4 %hidden_grad.1 = (bf16[1024,4096]{1,0:T(8,128)(2,1)}, bf16[256,1024]{1,0:T(8,128)(2,1)}, bf16[512,1024]{1,0:T(8,128)(2,1)}, bf16[256,1024]{1,0:T(8,128)(2,1)}, b...) custom-call(bf16[1024,1024]{1,0:T(8,128)(2,1)} %copy-done.1, ...), custom_call_target="tpu_custom_call" | custom-call | flops 1024 | bytes 1024 | tf_op jit(solution)/shard_map/hidden_grad/pallas_call | solution.py:249
  253.7 5.1 %collective-permute-done.14.refs_5_ = bf16[512,1024]{1,0:T(8,128)(2,1)} collective-permute-done((bf16[512,1024]{1,0:T(8,128)(2,1)}, bf16[512,1024]{1,0:T(8,128)(2,1)}, u32[]{:S(2)}, u32[]{:S(2)}) %collective-permute-start.14) | collective-permute-done | bytes 1048608 | tf_op jit(solution)/shard_map/ppermute | solution.py:18
  263.1 2.5 collective-permute-start.23
  267.7 21.5 %near_parts.1 = (f32[1024,1024]{1,0:T(8,128)}, bf16[512,1024]{1,0:T(8,128)(2,1)}, bf16[512,1024]{1,0:T(8,128)(2,1)}) custom-call(bf16[1024,4096]{1,0:T(8,128)(2,1)} %get-tuple-element.68.hid.refs_9_, bf16[1,16,6,256,256]{4,3,2,1,0:T(8,128)(2,1)} %refs_1_.1, bf16[1,16,6,256,256]{4,3,2,1,0:T(8,128)(2,1)} %refs_1_.1), custom_call_target="tpu_custom_call" | custom-call | flops 1024 | bytes 1024 | tf_op jit(solution)/shard_map/near_parts/pallas_call | solution.py:299
  289.2 14.0 %second_late.1 = (bf16[1,16,6,256,256]{4,3,2,1,0:T(8,128)(2,1)}, bf16[1,4096,256]{2,1,0:T(8,128)(2,1)}) custom-call(bf16[384,1024]{1,0:T(8,128)(2,1)} %copy-done.12, bf16[640,1024]{1,0:T(8,128)(2,1)} %copy-done.8, bf16[512,1024]{1,0:T(8,128)(2,1)} %collective-permute-done.8.refs_6_.refs_2_, ...), custom_call_target="tpu_custom_call", output_to_operand_aliasing={{0}: (6, {})} | custom-call | flops 1024 | bytes 1024 | tf_op jit(solution)/shard_map/second_late/pallas_call | solution.py:380
  303.2 30.7 %first_grad.1 = (bf16[1,16,6,256,256]{4,3,2,1,0:T(8,128)(2,1)}, bf16[1,256,4096]{2,1,0:T(8,128)(2,1)}) custom-call(bf16[1024,1024]{1,0:T(8,128)(2,1)} %bitcast.29, bf16[1024,1024]{1,0:T(8,128)(2,1)} %bitcast.30, bf16[1024,1024]{1,0:T(8,128)(2,1)} %bitcast.31, bf16[1024,1024]{1,0:T(8,128)(2,1)} %collective-permute-done.1.refs_3_, ...), custom_call_target="tpu_custom_call" | custom-call | flops 1024 | bytes 1024 | tf_op jit(solution)/shard_map/first_grad/pallas_call | solution.py:424
  333.9 8.6 %collective-permute-done.19 = bf16[256,256]{1,0:T(8,128)(2,1)S(1)} collective-permute-done((bf16[256,256]{1,0:T(8,128)(2,1)S(1)}, bf16[256,256]{1,0:T(8,128)(2,1)S(1)}, u32[]{:S(2)}, u32[]{:S(2)}) %collective-permute-start.19) | collective-permute-done | bytes 131104 | tf_op jit(solution)/shard_map/ppermute | solution.py:18
  342.7 7.9 %collective-permute-done.22 = bf16[256,256]{1,0:T(8,128)(2,1)S(1)} collective-permute-done((bf16[256,256]{1,0:T(8,128)(2,1)S(1)}, bf16[256,256]{1,0:T(8,128)(2,1)S(1)}, u32[]{:S(2)}, u32[]{:S(2)}) %collective-permute-start.22) | collective-permute-done | bytes 131104 | tf_op jit(solution)/shard_map/ppermute | solution.py:18
  351.3 2.5 collective-permute-start.25
  353.8 3.9 %collective-permute-done.24 = bf16[256,256]{1,0:T(8,128)(2,1)S(1)} collective-permute-done((bf16[256,256]{1,0:T(8,128)(2,1)S(1)}, bf16[256,256]{1,0:T(8,128)(2,1)S(1)}, u32[]{:S(2)}, u32[]{:S(2)}) %collective-permute-start.24) | collective-permute-done | bytes 131104 | tf_op jit(solution)/shard_map/ppermute | solution.py:18
  357.8 8.4 %collective-permute-done.25 = bf16[128,1024]{1,0:T(8,128)(2,1)S(1)} collective-permute-done((bf16[128,1024]{1,0:T(8,128)(2,1)S(1)}, bf16[128,1024]{1,0:T(8,128)(2,1)S(1)}, u32[]{:S(2)}, u32[]{:S(2)}) %collective-permute-start.25) | collective-permute-done | bytes 262176 | tf_op jit(solution)/shard_map/ppermute | solution.py:18
  369.9 2.7 add_add_fusion
  373.6 8.7 %collective-permute-done.27 = bf16[256,1024]{1,0:T(8,128)(2,1)} collective-permute-done((bf16[256,1024]{1,0:T(8,128)(2,1)}, bf16[256,1024]{1,0:T(8,128)(2,1)}, u32[]{:S(2)}, u32[]{:S(2)}) %collective-permute-start.27) | collective-permute-done | bytes 524320 | tf_op jit(solution)/shard_map/ppermute | solution.py:18
  382.3 4.3 %fusion = bf16[1,1024,1024]{2,1,0:T(8,128)(2,1)} fusion(f32[1024,1024]{1,0:T(8,128)} %add_add_fusion, bf16[256,1024]{1,0:T(8,128)(2,1)} %collective-permute-done.27, bf16[512,1024]{1,0:T(8,128)(2,1)} %copy-done.13, bf16[256,1024]{1,0:T(8,128)(2,1)} %collective-permute-done.20, bf16[128,1024]{1,0:T(8,128)(2,1)S(1)} %copy-done.16, ...), kind=kLoop, calls=%fused_computation.3 | loop fusion | flops 13631488 | bytes 10485760 | tf_op jit(solution)/shard_map/broadcast_in_dim | solution.py:525
  (108 shorter events, 45.8 us)
Async XLA Ops:
  0.6 55.8 %collective-permute-start = (bf16[1024,1024]{1,0:T(8,128)(2,1)}, bf16[1024,1024]{1,0:T(8,128)(2,1)S(1)}, u32[]{:S(2)}, u32[]{:S(2)}) collective-permute-start(bf16[1024,1024]{1,0:T(8,128)(2,1)} %bitcast.33), channel_id=1, source_target_pairs={{0,24},{8,0},{16,8},{24,16},{1,25},{9,1},{17,9},{25,17},{2,26},{10... | collective-permute-start | bytes 6291464 | tf_op jit(solution)/shard_map/ppermute | solution.py:23
  4.6 51.8 %collective-permute-start.1 = (bf16[1024,1024]{1,0:T(8,128)(2,1)}, bf16[1024,1024]{1,0:T(8,128)(2,1)}, u32[]{:S(2)}, u32[]{:S(2)}) collective-permute-start(bf16[1024,1024]{1,0:T(8,128)(2,1)} %bitcast.28), channel_id=1, source_target_pairs={{0,1},{1,0},{2,3},{3,2},{4,5},{5,4},{6,7},{7,6},{8,9},{9,8},{10,11... | collective-permute-start | bytes 6291464 | tf_op jit(solution)/shard_map/ppermute | solution.py:18
  6.9 49.4 %collective-permute-start.3 = (bf16[512,1024]{1,0:T(8,128)(2,1)}, bf16[512,1024]{1,0:T(8,128)(2,1)}, u32[]{:S(2)}, u32[]{:S(2)}) collective-permute-start(bf16[512,1024]{1,0:T(8,128)(2,1)} %slice_bitcast_fusion), channel_id=1, source_target_pairs={{0,4},{1,5},{2,6},{3,7},{4,0},{5,1},{6,2},{7,3},{8,12},{9,13},{10,... | collective-permute-start | bytes 3145736 | tf_op jit(solution)/shard_map/ppermute | solution.py:18
  9.4 47.0 %collective-permute-start.2 = (bf16[512,1024]{1,0:T(8,128)(2,1)}, bf16[512,1024]{1,0:T(8,128)(2,1)}, u32[]{:S(2)}, u32[]{:S(2)}) collective-permute-start(bf16[512,1024]{1,0:T(8,128)(2,1)} %slice_bitcast_fusion), channel_id=1, source_target_pairs={{0,2},{1,3},{2,0},{3,1},{4,6},{5,7},{6,4},{7,5},{8,10},{9,11},{10,... | collective-permute-start | bytes 3145736 | tf_op jit(solution)/shard_map/ppermute | solution.py:18
  59.6 11.1 %collective-permute-start.4 = (bf16[1024,1024]{1,0:T(8,128)(2,1)S(1)}, bf16[1024,1024]{1,0:T(8,128)(2,1)}, u32[]{:S(2)}, u32[]{:S(2)}) collective-permute-start(bf16[1024,1024]{1,0:T(8,128)(2,1)S(1)} %collective-permute-done.refs_0_.refs_1_.refs_2_), channel_id=1, source_target_pairs={{0,1},{1,0},{2,3},{3,2},{4,5},{5,4},{6,7},{7,6},{8,9},{9,8},{10,11... | collective-permute-start | bytes 6291464 | tf_op jit(solution)/shard_map/ppermute | solution.py:18
  61.0 50.7 %collective-permute-start.5 = (bf16[384,1024]{1,0:T(8,128)(2,1)}, bf16[384,1024]{1,0:T(8,128)(2,1)S(1)}, u32[]{:S(2)}, u32[]{:S(2)}) collective-permute-start(bf16[384,1024]{1,0:T(8,128)(2,1)} %slice.19), channel_id=1, source_target_pairs={{0,2},{1,3},{2,0},{3,1},{4,6},{5,7},{6,4},{7,5},{8,10},{9,11},{10,... | collective-permute-start | bytes 2359304 | tf_op jit(solution)/shard_map/ppermute | solution.py:18
  63.9 48.5 %collective-permute-start.8 = (bf16[512,1024]{1,0:T(8,128)(2,1)}, bf16[512,1024]{1,0:T(8,128)(2,1)}, u32[]{:S(2)}, u32[]{:S(2)}) collective-permute-start(bf16[512,1024]{1,0:T(8,128)(2,1)} %get-tuple-element.101), channel_id=1, source_target_pairs={{0,4},{1,5},{2,6},{3,7},{4,0},{5,1},{6,2},{7,3},{8,12},{9,13},{10,... | collective-permute-start | bytes 3145736 | tf_op jit(solution)/shard_map/ppermute | solution.py:18
  69.9 40.8 %collective-permute-start.7 = (bf16[256,768]{1,0:T(8,128)(2,1)}, bf16[256,768]{1,0:T(8,128)(2,1)}, u32[]{:S(2)}, u32[]{:S(2)}) collective-permute-start(bf16[256,768]{1,0:T(8,128)(2,1)} %dynamic-slice_convert_fusion), channel_id=1, source_target_pairs={{0,2},{1,3},{2,0},{3,1},{4,6},{5,7},{6,4},{7,5},{8,10},{9,11},{10,... | collective-permute-start | bytes 1179656 | tf_op jit(solution)/shard_map/ppermute | solution.py:18
  112.5 43.4 %collective-permute-start.9 = (bf16[256,768]{1,0:T(8,128)(2,1)S(1)}, bf16[256,768]{1,0:T(8,128)(2,1)S(1)}, u32[]{:S(2)}, u32[]{:S(2)}) collective-permute-start(bf16[256,768]{1,0:T(8,128)(2,1)S(1)} %convert_element_type.53), channel_id=1, source_target_pairs={{0,4},{1,5},{2,6},{3,7},{4,0},{5,1},{6,2},{7,3},{8,12},{9,13},{10,... | collective-permute-start | bytes 1179656 | tf_op jit(solution)/shard_map/ppermute | solution.py:18
  115.0 72.1 %collective-permute-start.11 = (bf16[512,1024]{1,0:T(8,128)(2,1)}, bf16[512,1024]{1,0:T(8,128)(2,1)}, u32[]{:S(2)}, u32[]{:S(2)}) collective-permute-start(bf16[512,1024]{1,0:T(8,128)(2,1)} %get-tuple-element.56), channel_id=1, source_target_pairs={{0,4},{1,5},{2,6},{3,7},{4,0},{5,1},{6,2},{7,3},{8,12},{9,13},{10,... | collective-permute-start | bytes 3145736 | tf_op jit(solution)/shard_map/ppermute | solution.py:18
  156.8 29.1 %collective-permute-start.12 = (bf16[256,768]{1,0:T(8,128)(2,1)}, bf16[256,768]{1,0:T(8,128)(2,1)}, u32[]{:S(2)}, u32[]{:S(2)}) collective-permute-start(bf16[256,768]{1,0:T(8,128)(2,1)} %add_convert_fusion.1), channel_id=1, source_target_pairs={{0,2},{1,3},{2,0},{3,1},{4,6},{5,7},{6,4},{7,5},{8,10},{9,11},{10,... | collective-permute-start | bytes 1179656 | tf_op jit(solution)/shard_map/ppermute | solution.py:18
  157.9 58.3 %collective-permute-start.10 = (bf16[640,1024]{1,0:T(8,128)(2,1)}, bf16[640,1024]{1,0:T(8,128)(2,1)S(1)}, u32[]{:S(2)}, u32[]{:S(2)}) collective-permute-start(bf16[640,1024]{1,0:T(8,128)(2,1)} %slice.20), channel_id=1, source_target_pairs={{0,2},{1,3},{2,0},{3,1},{4,6},{5,7},{6,4},{7,5},{8,10},{9,11},{10,... | collective-permute-start | bytes 3932168 | tf_op jit(solution)/shard_map/ppermute | solution.py:18
  188.2 65.5 %collective-permute-start.15 = (bf16[512,1024]{1,0:T(8,128)(2,1)}, bf16[512,1024]{1,0:T(8,128)(2,1)}, u32[]{:S(2)}, u32[]{:S(2)}) collective-permute-start(bf16[512,1024]{1,0:T(8,128)(2,1)} %slice.23), channel_id=1, source_target_pairs={{0,4},{1,5},{2,6},{3,7},{4,0},{5,1},{6,2},{7,3},{8,12},{9,13},{10,... | collective-permute-start | bytes 3145736 | tf_op jit(solution)/shard_map/ppermute | solution.py:18
  188.4 70.4 %collective-permute-start.14 = (bf16[512,1024]{1,0:T(8,128)(2,1)}, bf16[512,1024]{1,0:T(8,128)(2,1)}, u32[]{:S(2)}, u32[]{:S(2)}) collective-permute-start(bf16[512,1024]{1,0:T(8,128)(2,1)} %slice.23), channel_id=1, source_target_pairs={{0,2},{1,3},{2,0},{3,1},{4,6},{5,7},{6,4},{7,5},{8,10},{9,11},{10,... | collective-permute-start | bytes 3145736 | tf_op jit(solution)/shard_map/ppermute | solution.py:18
  258.8 83.8 %collective-permute-start.21 = (bf16[896,1024]{1,0:T(8,128)(2,1)}, bf16[896,1024]{1,0:T(8,128)(2,1)S(1)}, u32[]{:S(2)}, u32[]{:S(2)}) collective-permute-start(bf16[896,1024]{1,0:T(8,128)(2,1)} %get-tuple-element.78), channel_id=1, source_target_pairs={{0,4},{1,5},{2,6},{3,7},{4,0},{5,1},{6,2},{7,3},{8,12},{9,13},{10,... | collective-permute-start | bytes 5505032 | tf_op jit(solution)/shard_map/ppermute | solution.py:18
  263.1 87.6 %collective-permute-start.23 = (bf16[512,1024]{1,0:T(8,128)(2,1)}, bf16[512,1024]{1,0:T(8,128)(2,1)S(1)}, u32[]{:S(2)}, u32[]{:S(2)}) collective-permute-start(bf16[512,1024]{1,0:T(8,128)(2,1)} %get-tuple-element.81), channel_id=1, source_target_pairs={{0,2},{1,3},{2,0},{3,1},{4,6},{5,7},{6,4},{7,5},{8,10},{9,11},{10,... | collective-permute-start | bytes 3145736 | tf_op jit(solution)/shard_map/ppermute | solution.py:18
  265.6 77.0 %collective-permute-start.20 = (bf16[256,1024]{1,0:T(8,128)(2,1)}, bf16[256,1024]{1,0:T(8,128)(2,1)}, u32[]{:S(2)}, u32[]{:S(2)}) collective-permute-start(bf16[256,1024]{1,0:T(8,128)(2,1)} %get-tuple-element.77), channel_id=1, source_target_pairs={{0,2},{1,3},{2,0},{3,1},{4,6},{5,7},{6,4},{7,5},{8,10},{9,11},{10,... | collective-permute-start | bytes 1572872 | tf_op jit(solution)/shard_map/ppermute | solution.py:18
  265.7 76.8 %collective-permute-start.19 = (bf16[256,256]{1,0:T(8,128)(2,1)S(1)}, bf16[256,256]{1,0:T(8,128)(2,1)S(1)}, u32[]{:S(2)}, u32[]{:S(2)}) collective-permute-start(bf16[256,256]{1,0:T(8,128)(2,1)S(1)} %dynamic-slice_convert_fusion.1), channel_id=1, source_target_pairs={{0,2},{1,3},{2,0},{3,1},{4,6},{5,7},{6,4},{7,5},{8,10},{9,11},{10,... | collective-permute-start | bytes 393224 | tf_op jit(solution)/shard_map/ppermute | solution.py:18
  342.6 8.0 %collective-permute-start.22 = (bf16[256,256]{1,0:T(8,128)(2,1)S(1)}, bf16[256,256]{1,0:T(8,128)(2,1)S(1)}, u32[]{:S(2)}, u32[]{:S(2)}) collective-permute-start(bf16[256,256]{1,0:T(8,128)(2,1)S(1)} %convert_element_type.59), channel_id=1, source_target_pairs={{0,4},{1,5},{2,6},{3,7},{4,0},{5,1},{6,2},{7,3},{8,12},{9,13},{10,... | collective-permute-start | bytes 393224 | tf_op jit(solution)/shard_map/ppermute | solution.py:18
  350.6 7.1 %collective-permute-start.24 = (bf16[256,256]{1,0:T(8,128)(2,1)S(1)}, bf16[256,256]{1,0:T(8,128)(2,1)S(1)}, u32[]{:S(2)}, u32[]{:S(2)}) collective-permute-start(bf16[256,256]{1,0:T(8,128)(2,1)S(1)} %add_convert_fusion.2), channel_id=1, source_target_pairs={{0,2},{1,3},{2,0},{3,1},{4,6},{5,7},{6,4},{7,5},{8,10},{9,11},{10,... | collective-permute-start | bytes 393224 | tf_op jit(solution)/shard_map/ppermute | solution.py:18
  350.7 17.8 %collective-permute-start.17 = (bf16[512,1024]{1,0:T(8,128)(2,1)}, bf16[512,1024]{1,0:T(8,128)(2,1)S(1)}, u32[]{:S(2)}, u32[]{:S(2)}) collective-permute-start(bf16[512,1024]{1,0:T(8,128)(2,1)} %get-tuple-element.70), channel_id=1, source_target_pairs={{0,1},{1,0},{2,3},{3,2},{4,5},{5,4},{6,7},{7,6},{8,9},{9,8},{10,11... | collective-permute-start | bytes 3145736 | tf_op jit(solution)/shard_map/ppermute | solution.py:18
  350.8 17.7 %collective-permute-start.18 = (bf16[512,1024]{1,0:T(8,128)(2,1)}, bf16[512,1024]{1,0:T(8,128)(2,1)S(1)}, u32[]{:S(2)}, u32[]{:S(2)}) collective-permute-start(bf16[512,1024]{1,0:T(8,128)(2,1)} %get-tuple-element.71), channel_id=1, source_target_pairs={{0,1},{1,0},{2,3},{3,2},{4,5},{5,4},{6,7},{7,6},{8,9},{9,8},{10,11... | collective-permute-start | bytes 3145736 | tf_op jit(solution)/shard_map/ppermute | solution.py:18
  351.3 14.9 %collective-permute-start.25 = (bf16[128,1024]{1,0:T(8,128)(2,1)S(1)}, bf16[128,1024]{1,0:T(8,128)(2,1)S(1)}, u32[]{:S(2)}, u32[]{:S(2)}) collective-permute-start(bf16[128,1024]{1,0:T(8,128)(2,1)S(1)} %copy-done.18), channel_id=1, source_target_pairs={{0,4},{1,5},{2,6},{3,7},{4,0},{5,1},{6,2},{7,3},{8,12},{9,13},{10,... | collective-permute-start | bytes 786440 | tf_op jit(solution)/shard_map/ppermute | solution.py:18
  367.7 14.6 %collective-permute-start.27 = (bf16[256,1024]{1,0:T(8,128)(2,1)}, bf16[256,1024]{1,0:T(8,128)(2,1)}, u32[]{:S(2)}, u32[]{:S(2)}) collective-permute-start(bf16[256,1024]{1,0:T(8,128)(2,1)} %get-tuple-element.88), channel_id=1, source_target_pairs={{0,2},{1,3},{2,0},{3,1},{4,6},{5,7},{6,4},{7,5},{8,10},{9,11},{10,... | collective-permute-start | bytes 1572872 | tf_op jit(solution)/shard_map/ppermute | solution.py:18
  (23 other events, 411.2 us)

commit v5 on v4

--- a/solution.py
+++ b/solution.py
@@ -7,8 +7,8 @@
 from jax.experimental.pallas import tpu as pltpu
 from jax.sharding import PartitionSpec as P
 
-UP_SHARES = ((3, 0, 5), (4, 4, 0))
-BACK_SHARES = ((2, 4, 2), (7, 1, 0))
+UP_SHARES = ((2, 6, 0), (5, 3, 0))
+BACK_SHARES = ((3, 5, 0), (7, 1, 0))
 BF16 = jnp.bfloat16
 F32 = jnp.float32
 
@@ -23,13 +23,17 @@
     return lax.ppermute(value, "section", [(i, (i - 1) % peers) for i in range(peers)])
 
 
-def halved(value, bit, work=()):
+def halves(value, bit):
     half = value.shape[0] // 2
     mine = (lax.axis_index("tensor") >> bit) & 1
     keep = lax.dynamic_slice_in_dim(value, mine * half, half)
-    give = lax.dynamic_slice_in_dim(value, (1 - mine) * half, half)
+    return keep, lax.dynamic_slice_in_dim(value, (1 - mine) * half, half)
+
+
+def halved(value, bit):
+    keep, give = halves(value, bit)
     give = give if bit == 0 else give.astype(BF16)
-    return keep + after(swapped(give, bit), *work).astype(F32)
+    return keep + swapped(give, bit).astype(F32)
 
 
 def gathered(value, bit):
@@ -63,12 +67,23 @@
 
 def relay(links, value, work):
     last = len(links)
-    firsts = [sent(link[0], bit) for bit, link in enumerate(links, 1)]
     value = halved(value, 0)
     done = work(value)
-    seconds = [sent(link[1], bit, value) for bit, link in enumerate(links[:-1], 1)]
-    for bit in range(1, last):
-        value = halved(value, bit, done if bit == 1 else ())
+    seconds = [sent(link[1], bit, done[0]) for bit, link in enumerate(links[:-1], 1)]
+    if last > 1:
+        keep, give = halves(value, 1)
+        rows, width = links[0][0].shape
+        give = give.astype(BF16)
+        both = jnp.concatenate([links[0][0], give.reshape(-1, width)], axis=0)
+        both = swapped(both, 1)
+        firsts = [both[:rows]]
+        value = keep + after(both[rows:].reshape(give.shape), *done).astype(F32)
+    else:
+        firsts = [sent(links[0][0], 1)]
+        value = after(value, *done)
+    firsts += [sent(link[0], bit) for bit, link in enumerate(links[1:], 2)]
+    for bit in range(2, last):
+        value = halved(value, bit)
     value = after(value, *firsts)
     seconds.append(sent(links[-1][1], last, value))
     value = (value + swapped(value.astype(BF16), last).astype(F32)).astype(BF16)

time: 388 us -> 384 us (0.990)
  waiting for transfers between devices: 174 us -> 156 us
  local copies, waits for them, and re-layouts: 15.5 us -> 24 us
    ppermute x27 -> x24, waiting for transfers between devices: 174 us -> 156 us  [swapped(): return lax.ppermute(value, 'tensor', pairs)]
    reshape x0 -> x4, local copies, waits for them, and re-layouts: none -> 4.27 us  [the longest x2 2.3 us: relay(): both = jnp.concatenate([links[0][0], give.reshape(-1, width)], axis=0)]
    ppermute x27 -> x24, starting transfers between devices: 24.9 us -> 26.2 us  [swapped(): return lax.ppermute(value, 'tensor', pairs)]
  transfers between devices with their start and end apart: 28 -> 25, of which waited for: 14 -> 17; matrix products, arithmetic and copies ran while one was open for 6% -> 8% of each run, Pallas kernels for 38% -> 38%
where the time goes in v5:
time: 384 us; the launch traced here: 382 us
  waiting for transfers between devices  156 us (41%)
  Pallas kernels  147 us (38%)
  starting transfers between devices  30.2 us (8%)
  local copies, waits for them, and re-layouts  24 us (6%)
  other arithmetic  15.4 us (4%)
  matrix products  8.09 us (2%)
    ppermute x24, waiting for transfers between devices, swapped(): return lax.ppermute(value, 'tensor', pairs)  156 us
    pallas_call x1, Pallas kernels, hidden_call(): pl.pallas_call(functools.partial(hidden_kernel, [len(link) for link in up...  36.4 us
    pallas_call x2, Pallas kernels, second_call(): pl.pallas_call(functools.partial(second_kernel, [len(link) for link in up...  35.3 us
    pallas_call x1, Pallas kernels, first_call(): pl.pallas_call(functools.partial(first_kernel, [len(link) for link in ins...  30.7 us
    ppermute x24, starting transfers between devices, swapped(): return lax.ppermute(value, 'tensor', pairs)  26.2 us
    pallas_call x1, Pallas kernels, gate_call(): pl.pallas_call(functools.partial(gate_kernel, min(64, tokens)), grid=(wid...  23.1 us
    pallas_call x1, Pallas kernels, near_call(): pl.pallas_call(functools.partial(near_kernel, near, group), grid=(count_i...  21.5 us
  transfers between devices with their start and end apart: 25, of which 17 were waited for; matrix products, arithmetic and copies ran while one was open for 8% of the time, Pallas kernels for 38%

profile of v5, /device:TPU:0, one launch (start us, length us, event | category | flops | bytes accessed | tf_op | source)
XLA Modules:
  0.0 382.0 jit_solution(13018965711842252625)
XLA Ops:
  0.6 3.9 %collective-permute-start = (bf16[1024,1024]{1,0:T(8,128)(2,1)}, bf16[1024,1024]{1,0:T(8,128)(2,1)S(1)}, u32[]{:S(2)}, u32[]{:S(2)}) collective-permute-start(bf16[1024,1024]{1,0:T(8,128)(2,1)} %bitcast.33), channel_id=1, source_target_pairs={{0,24},{8,0},{16,8},{24,16},{1,25},{9,1},{17,9},{25,17},{2,26},{10... | collective-permute-start | bytes 6291464 | tf_op jit(solution)/shard_map/ppermute | solution.py:23
  11.0 23.1 %gate.1 = (bf16[1024,4096]{1,0:T(8,128)(2,1)}, f32[1024,4096]{1,0:T(8,128)}, f32[1024,256]{1,0:T(8,128)}) custom-call(bf16[1,1024,4096]{2,1,0:T(8,128)(2,1)} %preact.1, bf16[1,4096,256]{2,1,0:T(8,128)(2,1)} %refs_15_.1), custom_call_target="tpu_custom_call" | custom-call | flops 1024 | bytes 1024 | tf_op jit(solution)/shard_map/gate/pallas_call | solution.py:139
  36.5 19.7 %collective-permute-done.3.refs_6_ = bf16[512,1024]{1,0:T(8,128)(2,1)} collective-permute-done((bf16[512,1024]{1,0:T(8,128)(2,1)}, bf16[512,1024]{1,0:T(8,128)(2,1)}, u32[]{:S(2)}, u32[]{:S(2)}) %collective-permute-start.3) | collective-permute-done | bytes 1048608 | tf_op jit(solution)/shard_map/ppermute | solution.py:18
  62.6 2.9 collective-permute-done.5
  74.1 21.4 %second_early.1.refs_6_ = bf16[1,16,6,256,256]{4,3,2,1,0:T(8,128)(2,1)} custom-call(bf16[1024,1024]{1,0:T(8,128)(2,1)} %copy-done.1, bf16[1024,1024]{1,0:T(8,128)(2,1)} %copy-done.1, bf16[1024,1024]{1,0:T(8,128)(2,1)} %copy-done.1, bf16[1024,1024]{1,0:T(8,128)(2,1)} %collective-permute-done.4.refs_3_, bf16[1024,4096]{1,0:T(8,128)(2,1)} %get-tuple-element.50.refs_4_.refs_5_), custom_call_target="tpu_custom_call" | custom-call | flops 1024 | bytes 1024 | tf_op jit(solution)/shard_map/second_early/pallas_call | solution.py:395
  96.1 15.7 %collective-permute-done.6 = bf16[448,1024]{1,0:T(8,128)(2,1)S(1)} collective-permute-done((bf16[448,1024]{1,0:T(8,128)(2,1)}, bf16[448,1024]{1,0:T(8,128)(2,1)S(1)}, u32[]{:S(2)}, u32[]{:S(2)}) %collective-permute-start.6) | collective-permute-done | bytes 917536 | tf_op jit(solution)/shard_map/ppermute | solution.py:18
  115.0 6.3 %collective-permute-done.8.refs_6_.refs_2_ = bf16[640,1024]{1,0:T(8,128)(2,1)} collective-permute-done((bf16[640,1024]{1,0:T(8,128)(2,1)}, bf16[640,1024]{1,0:T(8,128)(2,1)}, u32[]{:S(2)}, u32[]{:S(2)}) %collective-permute-start.8) | collective-permute-done | bytes 1310752 | tf_op jit(solution)/shard_map/ppermute | solution.py:18
  121.4 5.5 %collective-permute-start.10 = (bf16[256,768]{1,0:T(8,128)(2,1)S(1)}, bf16[256,768]{1,0:T(8,128)(2,1)S(1)}, u32[]{:S(2)}, u32[]{:S(2)}) collective-permute-start(bf16[256,768]{1,0:T(8,128)(2,1)S(1)} %convert_element_type.53), channel_id=1, source_target_pairs={{0,4},{1,5},{2,6},{3,7},{4,0},{5,1},{6,2},{7,3},{8,12},{9,13},{10,... | collective-permute-start | bytes 1179656 | tf_op jit(solution)/shard_map/ppermute | solution.py:18
  126.9 26.0 %collective-permute-done.10 = bf16[256,768]{1,0:T(8,128)(2,1)S(1)} collective-permute-done((bf16[256,768]{1,0:T(8,128)(2,1)S(1)}, bf16[256,768]{1,0:T(8,128)(2,1)S(1)}, u32[]{:S(2)}, u32[]{:S(2)}) %collective-permute-start.10) | collective-permute-done | bytes 393248 | tf_op jit(solution)/shard_map/ppermute | solution.py:18
  153.7 9.7 %collective-permute-done.7.refs_5_.refs_1_ = bf16[768,1024]{1,0:T(8,128)(2,1)} collective-permute-done((bf16[768,1024]{1,0:T(8,128)(2,1)}, bf16[768,1024]{1,0:T(8,128)(2,1)}, u32[]{:S(2)}, u32[]{:S(2)}) %collective-permute-start.7) | collective-permute-done | bytes 1572896 | tf_op jit(solution)/shard_map/ppermute | solution.py:18
  165.4 3.9 %collective-permute-start.9 = (bf16[384,1024]{1,0:T(8,128)(2,1)}, bf16[384,1024]{1,0:T(8,128)(2,1)S(1)}, u32[]{:S(2)}, u32[]{:S(2)}) collective-permute-start(bf16[384,1024]{1,0:T(8,128)(2,1)} %slice.35), channel_id=1, source_target_pairs={{0,4},{1,5},{2,6},{3,7},{4,0},{5,1},{6,2},{7,3},{8,12},{9,13},{10,... | collective-permute-start | bytes 2359304 | tf_op jit(solution)/shard_map/ppermute | solution.py:18
  169.4 11.5 %collective-permute-done.11 = bf16[256,768]{1,0:T(8,128)(2,1)} collective-permute-done((bf16[256,768]{1,0:T(8,128)(2,1)}, bf16[256,768]{1,0:T(8,128)(2,1)}, u32[]{:S(2)}, u32[]{:S(2)}) %collective-permute-start.11) | collective-permute-done | bytes 393248 | tf_op jit(solution)/shard_map/ppermute | solution.py:18
  183.0 20.2 %collective-permute-done.9.refs_7_.refs_3_ = bf16[384,1024]{1,0:T(8,128)(2,1)S(1)} collective-permute-done((bf16[384,1024]{1,0:T(8,128)(2,1)}, bf16[384,1024]{1,0:T(8,128)(2,1)S(1)}, u32[]{:S(2)}, u32[]{:S(2)}) %collective-permute-start.9) | collective-permute-done | bytes 786464 | tf_op jit(solution)/shard_map/ppermute | solution.py:18
  209.8 36.4 %hidden_grad.1 = (bf16[1024,4096]{1,0:T(8,128)(2,1)}, bf16[384,1024]{1,0:T(8,128)(2,1)}, bf16[640,1024]{1,0:T(8,128)(2,1)}, bf16[896,1024]{1,0:T(8,128)(2,1)}, b...) custom-call(bf16[1024,1024]{1,0:T(8,128)(2,1)} %copy-done.1, bf16[1024,1024]{1,0:T(8,128)(2,1)} %copy-done.1, ...), custom_call_target="tpu_custom_call" | custom-call | flops 1024 | bytes 1024 | tf_op jit(solution)/shard_map/hidden_grad/pallas_call | solution.py:264
  246.2 7.1 %collective-permute-done.14.refs_7_ = bf16[512,1024]{1,0:T(8,128)(2,1)} collective-permute-done((bf16[512,1024]{1,0:T(8,128)(2,1)}, bf16[512,1024]{1,0:T(8,128)(2,1)}, u32[]{:S(2)}, u32[]{:S(2)}) %collective-permute-start.14) | collective-permute-done | bytes 1048608 | tf_op jit(solution)/shard_map/ppermute | solution.py:18
  259.7 21.5 %near_parts.1 = (f32[1024,1024]{1,0:T(8,128)}, bf16[512,1024]{1,0:T(8,128)(2,1)}, bf16[512,1024]{1,0:T(8,128)(2,1)}) custom-call(bf16[1024,4096]{1,0:T(8,128)(2,1)} %get-tuple-element.66.hid.refs_9_, bf16[1,16,6,256,256]{4,3,2,1,0:T(8,128)(2,1)} %refs_1_.1, bf16[1,16,6,256,256]{4,3,2,1,0:T(8,128)(2,1)} %refs_1_.1), custom_call_target="tpu_custom_call" | custom-call | flops 1024 | bytes 1024 | tf_op jit(solution)/shard_map/near_parts/pallas_call | solution.py:314
  283.1 13.9 %second_late.1 = (bf16[1,16,6,256,256]{4,3,2,1,0:T(8,128)(2,1)}, bf16[1,4096,256]{2,1,0:T(8,128)(2,1)}) custom-call(bf16[256,1024]{1,0:T(8,128)(2,1)} %slice.40.refs_4_.refs_0_, bf16[768,1024]{1,0:T(8,128)(2,1)} %collective-permute-done.7.refs_5_.refs_1_, bf16[640,1024]{1,0:T(8,128)(2,1)} %collective-permute-done.8.refs_6_.refs_2_, ...), custom_call_target="tpu_custom_call", output_to_operand_aliasing={{0}: (6, {})} | custom-call | flops 1024 | bytes 1024 | tf_op jit(solution)/shard_map/second_late/pallas_call | solution.py:395
  297.1 30.7 %first_grad.1 = (bf16[1,16,6,256,256]{4,3,2,1,0:T(8,128)(2,1)}, bf16[1,256,4096]{2,1,0:T(8,128)(2,1)}) custom-call(bf16[1024,1024]{1,0:T(8,128)(2,1)} %bitcast.29, bf16[1024,1024]{1,0:T(8,128)(2,1)} %bitcast.30, bf16[1024,1024]{1,0:T(8,128)(2,1)} %bitcast.31, bf16[1024,1024]{1,0:T(8,128)(2,1)} %collective-permute-done.1.refs_3_, ...), custom_call_target="tpu_custom_call" | custom-call | flops 1024 | bytes 1024 | tf_op jit(solution)/shard_map/first_grad/pallas_call | solution.py:439
  331.2 5.6 %collective-permute-done.19 = bf16[896,1024]{1,0:T(8,128)(2,1)} collective-permute-done((bf16[896,1024]{1,0:T(8,128)(2,1)}, bf16[896,1024]{1,0:T(8,128)(2,1)}, u32[]{:S(2)}, u32[]{:S(2)}) %collective-permute-start.19) | collective-permute-done | bytes 1835040 | tf_op jit(solution)/shard_map/ppermute | solution.py:18
  336.9 8.9 %collective-permute-done.20 = bf16[256,256]{1,0:T(8,128)(2,1)S(1)} collective-permute-done((bf16[256,256]{1,0:T(8,128)(2,1)S(1)}, bf16[256,256]{1,0:T(8,128)(2,1)S(1)}, u32[]{:S(2)}, u32[]{:S(2)}) %collective-permute-start.20) | collective-permute-done | bytes 131104 | tf_op jit(solution)/shard_map/ppermute | solution.py:18
  345.8 8.5 %collective-permute-done.21 = bf16[640,1024]{1,0:T(8,128)(2,1)} collective-permute-done((bf16[640,1024]{1,0:T(8,128)(2,1)}, bf16[640,1024]{1,0:T(8,128)(2,1)}, u32[]{:S(2)}, u32[]{:S(2)}) %collective-permute-start.21) | collective-permute-done | bytes 1310752 | tf_op jit(solution)/shard_map/ppermute | solution.py:18
  357.6 3.0 collective-permute-done.22
  360.7 9.3 %collective-permute-done.23 = bf16[128,1024]{1,0:T(8,128)(2,1)S(1)} collective-permute-done((bf16[128,1024]{1,0:T(8,128)(2,1)}, bf16[128,1024]{1,0:T(8,128)(2,1)S(1)}, u32[]{:S(2)}, u32[]{:S(2)}) %collective-permute-start.23) | collective-permute-done | bytes 262176 | tf_op jit(solution)/shard_map/ppermute | solution.py:18
  377.5 4.5 %fusion = bf16[1,1024,1024]{2,1,0:T(8,128)(2,1)} fusion(f32[1024,1024]{1,0:T(8,128)} %add_add_fusion, bf16[640,1024]{1,0:T(8,128)(2,1)} %collective-permute-done.21, bf16[384,1024]{1,0:T(8,128)(2,1)S(1)} %slice-done, bf16[128,1024]{1,0:T(8,128)(2,1)S(1)} %collective-permute-done.23, bf16[896,1024]{1,0:T(8,128)(2,1)} %collective-permute-done.19), kind=kLoop, calls=%fused_computation.3 | loop fusion | flops 11534336 | bytes 10485760 | tf_op jit(solution)/shard_map/broadcast_in_dim | solution.py:540
  (112 shorter events, 61.7 us)
Async XLA Ops:
  0.6 55.8 %collective-permute-start = (bf16[1024,1024]{1,0:T(8,128)(2,1)}, bf16[1024,1024]{1,0:T(8,128)(2,1)S(1)}, u32[]{:S(2)}, u32[]{:S(2)}) collective-permute-start(bf16[1024,1024]{1,0:T(8,128)(2,1)} %bitcast.33), channel_id=1, source_target_pairs={{0,24},{8,0},{16,8},{24,16},{1,25},{9,1},{17,9},{25,17},{2,26},{10... | collective-permute-start | bytes 6291464 | tf_op jit(solution)/shard_map/ppermute | solution.py:23
  4.6 51.8 %collective-permute-start.1 = (bf16[1024,1024]{1,0:T(8,128)(2,1)}, bf16[1024,1024]{1,0:T(8,128)(2,1)}, u32[]{:S(2)}, u32[]{:S(2)}) collective-permute-start(bf16[1024,1024]{1,0:T(8,128)(2,1)} %bitcast.28), channel_id=1, source_target_pairs={{0,1},{1,0},{2,3},{3,2},{4,5},{5,4},{6,7},{7,6},{8,9},{9,8},{10,11... | collective-permute-start | bytes 6291464 | tf_op jit(solution)/shard_map/ppermute | solution.py:18
  6.9 49.4 %collective-permute-start.3 = (bf16[512,1024]{1,0:T(8,128)(2,1)}, bf16[512,1024]{1,0:T(8,128)(2,1)}, u32[]{:S(2)}, u32[]{:S(2)}) collective-permute-start(bf16[512,1024]{1,0:T(8,128)(2,1)} %slice_bitcast_fusion), channel_id=1, source_target_pairs={{0,4},{1,5},{2,6},{3,7},{4,0},{5,1},{6,2},{7,3},{8,12},{9,13},{10,... | collective-permute-start | bytes 3145736 | tf_op jit(solution)/shard_map/ppermute | solution.py:18
  9.4 47.0 %collective-permute-start.2 = (bf16[512,1024]{1,0:T(8,128)(2,1)}, bf16[512,1024]{1,0:T(8,128)(2,1)}, u32[]{:S(2)}, u32[]{:S(2)}) collective-permute-start(bf16[512,1024]{1,0:T(8,128)(2,1)} %slice_bitcast_fusion), channel_id=1, source_target_pairs={{0,2},{1,3},{2,0},{3,1},{4,6},{5,7},{6,4},{7,5},{8,10},{9,11},{10,... | collective-permute-start | bytes 3145736 | tf_op jit(solution)/shard_map/ppermute | solution.py:18
  59.5 6.0 %collective-permute-start.5 = (f32[512,768]{1,0:T(8,128)}, f32[512,768]{1,0:T(8,128)}, u32[]{:S(2)}, u32[]{:S(2)}) collective-permute-start(f32[512,768]{1,0:T(8,128)} %constant_dynamic-slice_fusion.1), channel_id=1, source_target_pairs={{0,1},{1,0},{2,3},{3,2},{4,5},{5,4},{6,7},{7,6},{8,9},{9,8},{10,11... | collective-permute-start | bytes 4718600 | tf_op jit(solution)/shard_map/ppermute | solution.py:18
  59.6 14.5 %collective-permute-start.4 = (bf16[1024,1024]{1,0:T(8,128)(2,1)S(1)}, bf16[1024,1024]{1,0:T(8,128)(2,1)}, u32[]{:S(2)}, u32[]{:S(2)}) collective-permute-start(bf16[1024,1024]{1,0:T(8,128)(2,1)S(1)} %collective-permute-done.refs_0_.refs_1_.refs_2_), channel_id=1, source_target_pairs={{0,1},{1,0},{2,3},{3,2},{4,5},{5,4},{6,7},{7,6},{8,9},{9,8},{10,11... | collective-permute-start | bytes 6291464 | tf_op jit(solution)/shard_map/ppermute | solution.py:18
  61.3 60.1 %collective-permute-start.8 = (bf16[640,1024]{1,0:T(8,128)(2,1)}, bf16[640,1024]{1,0:T(8,128)(2,1)}, u32[]{:S(2)}, u32[]{:S(2)}) collective-permute-start(bf16[640,1024]{1,0:T(8,128)(2,1)} %slice.34), channel_id=1, source_target_pairs={{0,4},{1,5},{2,6},{3,7},{4,0},{5,1},{6,2},{7,3},{8,12},{9,13},{10,... | collective-permute-start | bytes 3932168 | tf_op jit(solution)/shard_map/ppermute | solution.py:18
  71.4 40.4 %collective-permute-start.6 = (bf16[448,1024]{1,0:T(8,128)(2,1)}, bf16[448,1024]{1,0:T(8,128)(2,1)S(1)}, u32[]{:S(2)}, u32[]{:S(2)}) collective-permute-start(bf16[448,1024]{1,0:T(8,128)(2,1)} %pad_maximum_fusion.1), channel_id=1, source_target_pairs={{0,2},{1,3},{2,0},{3,1},{4,6},{5,7},{6,4},{7,5},{8,10},{9,11},{10,... | collective-permute-start | bytes 2752520 | tf_op jit(solution)/shard_map/ppermute | solution.py:18
  95.5 67.9 %collective-permute-start.7 = (bf16[768,1024]{1,0:T(8,128)(2,1)}, bf16[768,1024]{1,0:T(8,128)(2,1)}, u32[]{:S(2)}, u32[]{:S(2)}) collective-permute-start(bf16[768,1024]{1,0:T(8,128)(2,1)} %slice.33), channel_id=1, source_target_pairs={{0,2},{1,3},{2,0},{3,1},{4,6},{5,7},{6,4},{7,5},{8,10},{9,11},{10,... | collective-permute-start | bytes 4718600 | tf_op jit(solution)/shard_map/ppermute | solution.py:18
  121.4 31.4 %collective-permute-start.10 = (bf16[256,768]{1,0:T(8,128)(2,1)S(1)}, bf16[256,768]{1,0:T(8,128)(2,1)S(1)}, u32[]{:S(2)}, u32[]{:S(2)}) collective-permute-start(bf16[256,768]{1,0:T(8,128)(2,1)S(1)} %convert_element_type.53), channel_id=1, source_target_pairs={{0,4},{1,5},{2,6},{3,7},{4,0},{5,1},{6,2},{7,3},{8,12},{9,13},{10,... | collective-permute-start | bytes 1179656 | tf_op jit(solution)/shard_map/ppermute | solution.py:18
  163.4 17.5 %collective-permute-start.11 = (bf16[256,768]{1,0:T(8,128)(2,1)}, bf16[256,768]{1,0:T(8,128)(2,1)}, u32[]{:S(2)}, u32[]{:S(2)}) collective-permute-start(bf16[256,768]{1,0:T(8,128)(2,1)} %add_convert_fusion.1), channel_id=1, source_target_pairs={{0,2},{1,3},{2,0},{3,1},{4,6},{5,7},{6,4},{7,5},{8,10},{9,11},{10,... | collective-permute-start | bytes 1179656 | tf_op jit(solution)/shard_map/ppermute | solution.py:18
  165.4 37.8 %collective-permute-start.9 = (bf16[384,1024]{1,0:T(8,128)(2,1)}, bf16[384,1024]{1,0:T(8,128)(2,1)S(1)}, u32[]{:S(2)}, u32[]{:S(2)}) collective-permute-start(bf16[384,1024]{1,0:T(8,128)(2,1)} %slice.35), channel_id=1, source_target_pairs={{0,4},{1,5},{2,6},{3,7},{4,0},{5,1},{6,2},{7,3},{8,12},{9,13},{10,... | collective-permute-start | bytes 2359304 | tf_op jit(solution)/shard_map/ppermute | solution.py:18
  203.2 4.1 %collective-permute-start.12 = (bf16[512,768]{1,0:T(8,128)(2,1)}, bf16[512,768]{1,0:T(8,128)(2,1)}, u32[]{:S(2)}, u32[]{:S(2)}) collective-permute-start(bf16[512,768]{1,0:T(8,128)(2,1)} %pad_maximum_fusion.3), channel_id=1, source_target_pairs={{0,1},{1,0},{2,3},{3,2},{4,5},{5,4},{6,7},{7,6},{8,9},{9,8},{10,11... | collective-permute-start | bytes 2359304 | tf_op jit(solution)/shard_map/ppermute | solution.py:18
  204.3 49.0 %collective-permute-start.14 = (bf16[512,1024]{1,0:T(8,128)(2,1)}, bf16[512,1024]{1,0:T(8,128)(2,1)}, u32[]{:S(2)}, u32[]{:S(2)}) collective-permute-start(bf16[512,1024]{1,0:T(8,128)(2,1)} %slice.37), channel_id=1, source_target_pairs={{0,4},{1,5},{2,6},{3,7},{4,0},{5,1},{6,2},{7,3},{8,12},{9,13},{10,... | collective-permute-start | bytes 3145736 | tf_op jit(solution)/shard_map/ppermute | solution.py:18
  204.3 49.2 %collective-permute-start.13 = (bf16[512,1024]{1,0:T(8,128)(2,1)}, bf16[512,1024]{1,0:T(8,128)(2,1)}, u32[]{:S(2)}, u32[]{:S(2)}) collective-permute-start(bf16[512,1024]{1,0:T(8,128)(2,1)} %slice.37), channel_id=1, source_target_pairs={{0,2},{1,3},{2,0},{3,1},{4,6},{5,7},{6,4},{7,5},{8,10},{9,11},{10,... | collective-permute-start | bytes 3145736 | tf_op jit(solution)/shard_map/ppermute | solution.py:18
  254.6 2.0 collective-permute-start.15
  254.7 82.1 %collective-permute-start.19 = (bf16[896,1024]{1,0:T(8,128)(2,1)}, bf16[896,1024]{1,0:T(8,128)(2,1)}, u32[]{:S(2)}, u32[]{:S(2)}) collective-permute-start(bf16[896,1024]{1,0:T(8,128)(2,1)} %get-tuple-element.76), channel_id=1, source_target_pairs={{0,4},{1,5},{2,6},{3,7},{4,0},{5,1},{6,2},{7,3},{8,12},{9,13},{10,... | collective-permute-start | bytes 5505032 | tf_op jit(solution)/shard_map/ppermute | solution.py:18
  259.5 68.3 %collective-permute-start.18 = (bf16[448,1024]{1,0:T(8,128)(2,1)S(1)}, bf16[448,1024]{1,0:T(8,128)(2,1)S(1)}, u32[]{:S(2)}, u32[]{:S(2)}) collective-permute-start(bf16[448,1024]{1,0:T(8,128)(2,1)S(1)} %pad_maximum_fusion.2), channel_id=1, source_target_pairs={{0,2},{1,3},{2,0},{3,1},{4,6},{5,7},{6,4},{7,5},{8,10},{9,11},{10,... | collective-permute-start | bytes 2752520 | tf_op jit(solution)/shard_map/ppermute | solution.py:18
  281.3 73.0 %collective-permute-start.21 = (bf16[640,1024]{1,0:T(8,128)(2,1)}, bf16[640,1024]{1,0:T(8,128)(2,1)}, u32[]{:S(2)}, u32[]{:S(2)}) collective-permute-start(bf16[640,1024]{1,0:T(8,128)(2,1)} %get-tuple-element.79), channel_id=1, source_target_pairs={{0,2},{1,3},{2,0},{3,1},{4,6},{5,7},{6,4},{7,5},{8,10},{9,11},{10,... | collective-permute-start | bytes 3932168 | tf_op jit(solution)/shard_map/ppermute | solution.py:18
  336.8 8.9 %collective-permute-start.20 = (bf16[256,256]{1,0:T(8,128)(2,1)S(1)}, bf16[256,256]{1,0:T(8,128)(2,1)S(1)}, u32[]{:S(2)}, u32[]{:S(2)}) collective-permute-start(bf16[256,256]{1,0:T(8,128)(2,1)S(1)} %convert_element_type.59), channel_id=1, source_target_pairs={{0,4},{1,5},{2,6},{3,7},{4,0},{5,1},{6,2},{7,3},{8,12},{9,13},{10,... | collective-permute-start | bytes 393224 | tf_op jit(solution)/shard_map/ppermute | solution.py:18
  354.3 6.3 %collective-permute-start.22 = (bf16[256,256]{1,0:T(8,128)(2,1)S(1)}, bf16[256,256]{1,0:T(8,128)(2,1)S(1)}, u32[]{:S(2)}, u32[]{:S(2)}) collective-permute-start(bf16[256,256]{1,0:T(8,128)(2,1)S(1)} %add_convert_fusion.2), channel_id=1, source_target_pairs={{0,2},{1,3},{2,0},{3,1},{4,6},{5,7},{6,4},{7,5},{8,10},{9,11},{10,... | collective-permute-start | bytes 393224 | tf_op jit(solution)/shard_map/ppermute | solution.py:18
  354.3 18.1 %collective-permute-start.16 = (bf16[512,1024]{1,0:T(8,128)(2,1)S(1)}, bf16[512,1024]{1,0:T(8,128)(2,1)S(1)}, u32[]{:S(2)}, u32[]{:S(2)}) collective-permute-start(bf16[512,1024]{1,0:T(8,128)(2,1)S(1)} %copy-done.16), channel_id=1, source_target_pairs={{0,1},{1,0},{2,3},{3,2},{4,5},{5,4},{6,7},{7,6},{8,9},{9,8},{10,11... | collective-permute-start | bytes 3145736 | tf_op jit(solution)/shard_map/ppermute | solution.py:18
  354.3 18.1 %collective-permute-start.17 = (bf16[512,1024]{1,0:T(8,128)(2,1)S(1)}, bf16[512,1024]{1,0:T(8,128)(2,1)S(1)}, u32[]{:S(2)}, u32[]{:S(2)}) collective-permute-start(bf16[512,1024]{1,0:T(8,128)(2,1)S(1)} %copy-done.15), channel_id=1, source_target_pairs={{0,1},{1,0},{2,3},{3,2},{4,5},{5,4},{6,7},{7,6},{8,9},{9,8},{10,11... | collective-permute-start | bytes 3145736 | tf_op jit(solution)/shard_map/ppermute | solution.py:18
  354.8 15.2 %collective-permute-start.23 = (bf16[128,1024]{1,0:T(8,128)(2,1)}, bf16[128,1024]{1,0:T(8,128)(2,1)S(1)}, u32[]{:S(2)}, u32[]{:S(2)}) collective-permute-start(bf16[128,1024]{1,0:T(8,128)(2,1)} %get-tuple-element.82), channel_id=1, source_target_pairs={{0,4},{1,5},{2,6},{3,7},{4,0},{5,1},{6,2},{7,3},{8,12},{9,13},{10,... | collective-permute-start | bytes 786440 | tf_op jit(solution)/shard_map/ppermute | solution.py:18
  (20 other events, 331.2 us)

commit v6 on v5

--- a/solution.py
+++ b/solution.py
@@ -88,11 +88,10 @@
     seconds.append(sent(links[-1][1], last, value))
     value = (value + swapped(value.astype(BF16), last).astype(F32)).astype(BF16)
     thirds = [sent(link[2], bit, value) for bit, link in enumerate(links, 1)]
-    value = after(value, *kept(seconds[:-1]))
+    value = after(value, *kept(seconds))
     for bit in reversed(range(1, last)):
         value = gathered(value, bit)
-    value = gathered(after(value, seconds[-1]), 0)
-    return value, [kept(link) for link in zip(firsts, seconds, thirds)]
+    return gathered(value, 0), value, [kept(link) for link in zip(firsts, seconds, thirds)]
 
 
 def nt(left, right):
@@ -485,14 +484,17 @@
     near_ups = [[upstream]] * near + [[up_core]]
     (second_part,) = second_call(near_ups, flips[: near + 1], act, shape, 0)
     up_shares = shares_of(UP_SHARES, far_count)
-    sums, far_ups = relay(
+    sums, stage, far_ups = relay(
         [cut(upstream, shares) for shares in up_shares],
         jnp.concatenate([nt(upstream, right_two[0]), early], axis=1),
         lambda stage: [second_part],
     )
     proj_grad, proj_in, proj_act = jnp.split(sums, (ranks, 2 * ranks), axis=1)
 
-    in_two = half_sent(after(inputs[0], far_ups[-1][1])[second_half])
+    in_two = [
+        swapped(after(inputs[0], far_ups[-1][1] if bit == far_count else stage)[second_half], bit)
+        for bit in range(1, far_count + 1)
+    ]
     hidden, *parts, back = hidden_call(
         near_ups + far_ups,
         flips,
@@ -527,7 +529,7 @@
         [next(parts) if share else None for share in shares]
         for shares in shares_of(BACK_SHARES, far_count)
     ]
-    back_rank, far = relay(back_links, back, work)
+    back_rank, _, far = relay(back_links, back, work)
     base, beside, first_grad, second_grad, rightone_grad, lefttwo_grad = found
     base = base + beside.astype(F32) + nt(back_rank, left_one[0])
     leftone_grad = nn(inputs[0].T, back_rank).astype(BF16)[None]

time: 384 us -> 371 us (0.966)
  waiting for transfers between devices: 156 us -> 146 us
    ppermute x24, waiting for transfers between devices: 156 us -> 146 us  [swapped(): return lax.ppermute(value, 'tensor', pairs)]
  transfers between devices with their start and end apart: 25 -> 25, of which waited for: 17 -> 15; matrix products, arithmetic and copies ran while one was open for 8% -> 8% of each run, Pallas kernels for 38% -> 40%
where the time goes in v6:
time: 371 us; the launch traced here: 369 us
  Pallas kernels  147 us (40%)
  waiting for transfers between devices  146 us (39%)
  starting transfers between devices  26.7 us (7%)
  local copies, waits for them, and re-layouts  25.1 us (7%)
  other arithmetic  14.5 us (4%)
  matrix products  8.08 us (2%)
    ppermute x24, waiting for transfers between devices, swapped(): return lax.ppermute(value, 'tensor', pairs)  146 us
    pallas_call x1, Pallas kernels, hidden_call(): pl.pallas_call(functools.partial(hidden_kernel, [len(link) for link in up...  36.4 us
    pallas_call x2, Pallas kernels, second_call(): pl.pallas_call(functools.partial(second_kernel, [len(link) for link in up...  35.3 us
    pallas_call x1, Pallas kernels, first_call(): pl.pallas_call(functools.partial(first_kernel, [len(link) for link in ins...  30.7 us
    pallas_call x1, Pallas kernels, gate_call(): pl.pallas_call(functools.partial(gate_kernel, min(64, tokens)), grid=(wid...  23.1 us
    ppermute x24, starting transfers between devices, swapped(): return lax.ppermute(value, 'tensor', pairs)  22.7 us
    pallas_call x1, Pallas kernels, near_call(): pl.pallas_call(functools.partial(near_kernel, near, group), grid=(count_i...  21.5 us
  transfers between devices with their start and end apart: 25, of which 15 were waited for; matrix products, arithmetic and copies ran while one was open for 8% of the time, Pallas kernels for 40%

profile of v6, /device:TPU:0, one launch (start us, length us, event | category | flops | bytes accessed | tf_op | source)
XLA Modules:
  0.0 368.7 jit_solution(7541493926160442916)
XLA Ops:
  0.6 3.9 %collective-permute-start = (bf16[1024,1024]{1,0:T(8,128)(2,1)}, bf16[1024,1024]{1,0:T(8,128)(2,1)S(1)}, u32[]{:S(2)}, u32[]{:S(2)}) collective-permute-start(bf16[1024,1024]{1,0:T(8,128)(2,1)} %bitcast.34), channel_id=1, source_target_pairs={{0,24},{8,0},{16,8},{24,16},{1,25},{9,1},{17,9},{25,17},{2,26},{10... | collective-permute-start | bytes 6291464 | tf_op jit(solution)/shard_map/ppermute | solution.py:23
  6.9 2.6 collective-permute-start.3
  11.0 23.1 %gate.1 = (bf16[1024,4096]{1,0:T(8,128)(2,1)}, f32[1024,4096]{1,0:T(8,128)}, f32[1024,256]{1,0:T(8,128)}) custom-call(bf16[1,1024,4096]{2,1,0:T(8,128)(2,1)} %preact.1, bf16[1,4096,256]{2,1,0:T(8,128)(2,1)} %refs_15_.1), custom_call_target="tpu_custom_call" | custom-call | flops 1024 | bytes 1024 | tf_op jit(solution)/shard_map/gate/pallas_call | solution.py:138
  36.5 19.7 %collective-permute-done.3.refs_6_ = bf16[512,1024]{1,0:T(8,128)(2,1)} collective-permute-done((bf16[512,1024]{1,0:T(8,128)(2,1)}, bf16[512,1024]{1,0:T(8,128)(2,1)}, u32[]{:S(2)}, u32[]{:S(2)}) %collective-permute-start.3) | collective-permute-done | bytes 1048608 | tf_op jit(solution)/shard_map/ppermute | solution.py:18
  62.6 2.9 collective-permute-done.5
  74.1 21.4 %second_early.1.refs_6_ = bf16[1,16,6,256,256]{4,3,2,1,0:T(8,128)(2,1)} custom-call(bf16[1024,1024]{1,0:T(8,128)(2,1)} %copy-done.1, bf16[1024,1024]{1,0:T(8,128)(2,1)} %copy-done.1, bf16[1024,1024]{1,0:T(8,128)(2,1)} %copy-done.1, bf16[1024,1024]{1,0:T(8,128)(2,1)} %collective-permute-done.4.refs_3_, bf16[1024,4096]{1,0:T(8,128)(2,1)} %get-tuple-element.49.refs_4_.refs_5_), custom_call_target="tpu_custom_call" | custom-call | flops 1024 | bytes 1024 | tf_op jit(solution)/shard_map/second_early/pallas_call | solution.py:394
  98.3 13.5 %collective-permute-done.6 = bf16[448,1024]{1,0:T(8,128)(2,1)S(1)} collective-permute-done((bf16[448,1024]{1,0:T(8,128)(2,1)}, bf16[448,1024]{1,0:T(8,128)(2,1)S(1)}, u32[]{:S(2)}, u32[]{:S(2)}) %collective-permute-start.6) | collective-permute-done | bytes 917536 | tf_op jit(solution)/shard_map/ppermute | solution.py:18
  115.1 6.3 %collective-permute-done.8.refs_6_.refs_2_ = bf16[640,1024]{1,0:T(8,128)(2,1)} collective-permute-done((bf16[640,1024]{1,0:T(8,128)(2,1)}, bf16[640,1024]{1,0:T(8,128)(2,1)}, u32[]{:S(2)}, u32[]{:S(2)}) %collective-permute-start.8) | collective-permute-done | bytes 1310752 | tf_op jit(solution)/shard_map/ppermute | solution.py:18
  121.4 5.5 %collective-permute-start.9 = (bf16[384,1024]{1,0:T(8,128)(2,1)S(1)}, bf16[384,1024]{1,0:T(8,128)(2,1)}, u32[]{:S(2)}, u32[]{:S(2)}) collective-permute-start(bf16[384,1024]{1,0:T(8,128)(2,1)S(1)} %copy-done.15), channel_id=1, source_target_pairs={{0,4},{1,5},{2,6},{3,7},{4,0},{5,1},{6,2},{7,3},{8,12},{9,13},{10,... | collective-permute-start | bytes 2359304 | tf_op jit(solution)/shard_map/ppermute | solution.py:18
  127.0 47.6 %collective-permute-done.10 = bf16[256,768]{1,0:T(8,128)(2,1)S(1)} collective-permute-done((bf16[256,768]{1,0:T(8,128)(2,1)S(1)}, bf16[256,768]{1,0:T(8,128)(2,1)S(1)}, u32[]{:S(2)}, u32[]{:S(2)}) %collective-permute-start.10) | collective-permute-done | bytes 393248 | tf_op jit(solution)/shard_map/ppermute | solution.py:18
  174.8 5.5 %collective-permute-done.7.refs_5_.refs_1_ = bf16[768,1024]{1,0:T(8,128)(2,1)} collective-permute-done((bf16[768,1024]{1,0:T(8,128)(2,1)}, bf16[768,1024]{1,0:T(8,128)(2,1)}, u32[]{:S(2)}, u32[]{:S(2)}) %collective-permute-start.7) | collective-permute-done | bytes 1572896 | tf_op jit(solution)/shard_map/ppermute | solution.py:18
  180.2 11.1 %collective-permute-done.11 = bf16[256,768]{1,0:T(8,128)(2,1)} collective-permute-done((bf16[256,768]{1,0:T(8,128)(2,1)S(1)}, bf16[256,768]{1,0:T(8,128)(2,1)}, u32[]{:S(2)}, u32[]{:S(2)}) %collective-permute-start.11) | collective-permute-done | bytes 393248 | tf_op jit(solution)/shard_map/ppermute | solution.py:18
  201.2 36.4 %hidden_grad.1 = (bf16[1024,4096]{1,0:T(8,128)(2,1)}, bf16[384,1024]{1,0:T(8,128)(2,1)}, bf16[640,1024]{1,0:T(8,128)(2,1)}, bf16[896,1024]{1,0:T(8,128)(2,1)}, b...) custom-call(bf16[1024,1024]{1,0:T(8,128)(2,1)} %copy-done.1, bf16[1024,1024]{1,0:T(8,128)(2,1)} %copy-done.1, ...), custom_call_target="tpu_custom_call" | custom-call | flops 1024 | bytes 1024 | tf_op jit(solution)/shard_map/hidden_grad/pallas_call | solution.py:263
  237.7 6.2 %collective-permute-done.14.refs_7_ = bf16[512,1024]{1,0:T(8,128)(2,1)} collective-permute-done((bf16[512,1024]{1,0:T(8,128)(2,1)}, bf16[512,1024]{1,0:T(8,128)(2,1)}, u32[]{:S(2)}, u32[]{:S(2)}) %collective-permute-start.14) | collective-permute-done | bytes 1048608 | tf_op jit(solution)/shard_map/ppermute | solution.py:18
  251.3 21.5 %near_parts.1 = (f32[1024,1024]{1,0:T(8,128)}, bf16[512,1024]{1,0:T(8,128)(2,1)}, bf16[512,1024]{1,0:T(8,128)(2,1)}) custom-call(bf16[1024,4096]{1,0:T(8,128)(2,1)} %get-tuple-element.65.hid.refs_9_, bf16[1,16,6,256,256]{4,3,2,1,0:T(8,128)(2,1)} %refs_1_.1, bf16[1,16,6,256,256]{4,3,2,1,0:T(8,128)(2,1)} %refs_1_.1), custom_call_target="tpu_custom_call" | custom-call | flops 1024 | bytes 1024 | tf_op jit(solution)/shard_map/near_parts/pallas_call | solution.py:313
  274.5 13.9 %second_late.1 = (bf16[1,16,6,256,256]{4,3,2,1,0:T(8,128)(2,1)}, bf16[1,4096,256]{2,1,0:T(8,128)(2,1)}) custom-call(bf16[256,1024]{1,0:T(8,128)(2,1)} %slice.44.refs_4_.refs_0_, bf16[768,1024]{1,0:T(8,128)(2,1)} %collective-permute-done.7.refs_5_.refs_1_, bf16[640,1024]{1,0:T(8,128)(2,1)} %collective-permute-done.8.refs_6_.refs_2_, ...), custom_call_target="tpu_custom_call", output_to_operand_aliasing={{0}: (6, {})} | custom-call | flops 1024 | bytes 1024 | tf_op jit(solution)/shard_map/second_late/pallas_call | solution.py:394
  288.5 30.7 %first_grad.1 = (bf16[1,16,6,256,256]{4,3,2,1,0:T(8,128)(2,1)}, bf16[1,256,4096]{2,1,0:T(8,128)(2,1)}) custom-call(bf16[1024,1024]{1,0:T(8,128)(2,1)} %bitcast.29, bf16[1024,1024]{1,0:T(8,128)(2,1)} %bitcast.30, bf16[1024,1024]{1,0:T(8,128)(2,1)} %bitcast.31, bf16[1024,1024]{1,0:T(8,128)(2,1)} %collective-permute-done.1.refs_3_, ...), custom_call_target="tpu_custom_call" | custom-call | flops 1024 | bytes 1024 | tf_op jit(solution)/shard_map/first_grad/pallas_call | solution.py:438
  322.7 5.5 %collective-permute-done.19 = bf16[896,1024]{1,0:T(8,128)(2,1)} collective-permute-done((bf16[896,1024]{1,0:T(8,128)(2,1)}, bf16[896,1024]{1,0:T(8,128)(2,1)}, u32[]{:S(2)}, u32[]{:S(2)}) %collective-permute-start.19) | collective-permute-done | bytes 1835040 | tf_op jit(solution)/shard_map/ppermute | solution.py:18
  328.3 2.9 collective-permute-start.22
  331.2 6.3 %collective-permute-done.20 = bf16[256,256]{1,0:T(8,128)(2,1)S(1)} collective-permute-done((bf16[256,256]{1,0:T(8,128)(2,1)S(1)}, bf16[256,256]{1,0:T(8,128)(2,1)S(1)}, u32[]{:S(2)}, u32[]{:S(2)}) %collective-permute-start.20) | collective-permute-done | bytes 131104 | tf_op jit(solution)/shard_map/ppermute | solution.py:18
  337.5 14.0 %collective-permute-done.21 = bf16[640,1024]{1,0:T(8,128)(2,1)} collective-permute-done((bf16[640,1024]{1,0:T(8,128)(2,1)}, bf16[640,1024]{1,0:T(8,128)(2,1)}, u32[]{:S(2)}, u32[]{:S(2)}) %collective-permute-start.21) | collective-permute-done | bytes 1310752 | tf_op jit(solution)/shard_map/ppermute | solution.py:18
  352.1 4.4 %collective-permute-done.23 = bf16[256,256]{1,0:T(8,128)(2,1)S(1)} collective-permute-done((bf16[256,256]{1,0:T(8,128)(2,1)S(1)}, bf16[256,256]{1,0:T(8,128)(2,1)S(1)}, u32[]{:S(2)}, u32[]{:S(2)}) %collective-permute-start.23) | collective-permute-done | bytes 131104 | tf_op jit(solution)/shard_map/ppermute | solution.py:18
  360.4 2.7 add_add_fusion
  364.1 4.5 %fusion = bf16[1,1024,1024]{2,1,0:T(8,128)(2,1)} fusion(f32[1024,1024]{1,0:T(8,128)} %add_add_fusion, bf16[640,1024]{1,0:T(8,128)(2,1)} %collective-permute-done.21, bf16[384,1024]{1,0:T(8,128)(2,1)S(1)} %slice-done, bf16[128,1024]{1,0:T(8,128)(2,1)S(1)} %collective-permute-done.22, bf16[896,1024]{1,0:T(8,128)(2,1)} %collective-permute-done.19), kind=kLoop, calls=%fused_computation.3 | loop fusion | flops 11534336 | bytes 10485760 | tf_op jit(solution)/shard_map/broadcast_in_dim | solution.py:542
  (115 shorter events, 55.3 us)
Async XLA Ops:
  0.6 55.8 %collective-permute-start = (bf16[1024,1024]{1,0:T(8,128)(2,1)}, bf16[1024,1024]{1,0:T(8,128)(2,1)S(1)}, u32[]{:S(2)}, u32[]{:S(2)}) collective-permute-start(bf16[1024,1024]{1,0:T(8,128)(2,1)} %bitcast.34), channel_id=1, source_target_pairs={{0,24},{8,0},{16,8},{24,16},{1,25},{9,1},{17,9},{25,17},{2,26},{10... | collective-permute-start | bytes 6291464 | tf_op jit(solution)/shard_map/ppermute | solution.py:23
  4.6 51.8 %collective-permute-start.1 = (bf16[1024,1024]{1,0:T(8,128)(2,1)}, bf16[1024,1024]{1,0:T(8,128)(2,1)}, u32[]{:S(2)}, u32[]{:S(2)}) collective-permute-start(bf16[1024,1024]{1,0:T(8,128)(2,1)} %bitcast.28), channel_id=1, source_target_pairs={{0,1},{1,0},{2,3},{3,2},{4,5},{5,4},{6,7},{7,6},{8,9},{9,8},{10,11... | collective-permute-start | bytes 6291464 | tf_op jit(solution)/shard_map/ppermute | solution.py:18
  6.9 49.4 %collective-permute-start.3 = (bf16[512,1024]{1,0:T(8,128)(2,1)}, bf16[512,1024]{1,0:T(8,128)(2,1)}, u32[]{:S(2)}, u32[]{:S(2)}) collective-permute-start(bf16[512,1024]{1,0:T(8,128)(2,1)} %slice_bitcast_fusion), channel_id=1, source_target_pairs={{0,4},{1,5},{2,6},{3,7},{4,0},{5,1},{6,2},{7,3},{8,12},{9,13},{10,... | collective-permute-start | bytes 3145736 | tf_op jit(solution)/shard_map/ppermute | solution.py:18
  9.4 47.0 %collective-permute-start.2 = (bf16[512,1024]{1,0:T(8,128)(2,1)}, bf16[512,1024]{1,0:T(8,128)(2,1)}, u32[]{:S(2)}, u32[]{:S(2)}) collective-permute-start(bf16[512,1024]{1,0:T(8,128)(2,1)} %slice_bitcast_fusion), channel_id=1, source_target_pairs={{0,2},{1,3},{2,0},{3,1},{4,6},{5,7},{6,4},{7,5},{8,10},{9,11},{10,... | collective-permute-start | bytes 3145736 | tf_op jit(solution)/shard_map/ppermute | solution.py:18
  59.5 6.0 %collective-permute-start.5 = (f32[512,768]{1,0:T(8,128)}, f32[512,768]{1,0:T(8,128)}, u32[]{:S(2)}, u32[]{:S(2)}) collective-permute-start(f32[512,768]{1,0:T(8,128)} %constant_dynamic-slice_fusion.1), channel_id=1, source_target_pairs={{0,1},{1,0},{2,3},{3,2},{4,5},{5,4},{6,7},{7,6},{8,9},{9,8},{10,11... | collective-permute-start | bytes 4718600 | tf_op jit(solution)/shard_map/ppermute | solution.py:18
  59.6 14.5 %collective-permute-start.4 = (bf16[1024,1024]{1,0:T(8,128)(2,1)S(1)}, bf16[1024,1024]{1,0:T(8,128)(2,1)}, u32[]{:S(2)}, u32[]{:S(2)}) collective-permute-start(bf16[1024,1024]{1,0:T(8,128)(2,1)S(1)} %collective-permute-done.refs_0_.refs_1_.refs_2_), channel_id=1, source_target_pairs={{0,1},{1,0},{2,3},{3,2},{4,5},{5,4},{6,7},{7,6},{8,9},{9,8},{10,11... | collective-permute-start | bytes 6291464 | tf_op jit(solution)/shard_map/ppermute | solution.py:18
  61.3 60.1 %collective-permute-start.8 = (bf16[640,1024]{1,0:T(8,128)(2,1)}, bf16[640,1024]{1,0:T(8,128)(2,1)}, u32[]{:S(2)}, u32[]{:S(2)}) collective-permute-start(bf16[640,1024]{1,0:T(8,128)(2,1)} %slice.37), channel_id=1, source_target_pairs={{0,4},{1,5},{2,6},{3,7},{4,0},{5,1},{6,2},{7,3},{8,12},{9,13},{10,... | collective-permute-start | bytes 3932168 | tf_op jit(solution)/shard_map/ppermute | solution.py:18
  71.4 40.4 %collective-permute-start.6 = (bf16[448,1024]{1,0:T(8,128)(2,1)}, bf16[448,1024]{1,0:T(8,128)(2,1)S(1)}, u32[]{:S(2)}, u32[]{:S(2)}) collective-permute-start(bf16[448,1024]{1,0:T(8,128)(2,1)} %pad_maximum_fusion.1), channel_id=1, source_target_pairs={{0,2},{1,3},{2,0},{3,1},{4,6},{5,7},{6,4},{7,5},{8,10},{9,11},{10,... | collective-permute-start | bytes 2752520 | tf_op jit(solution)/shard_map/ppermute | solution.py:18
  95.5 84.8 %collective-permute-start.7 = (bf16[768,1024]{1,0:T(8,128)(2,1)}, bf16[768,1024]{1,0:T(8,128)(2,1)}, u32[]{:S(2)}, u32[]{:S(2)}) collective-permute-start(bf16[768,1024]{1,0:T(8,128)(2,1)} %slice.36), channel_id=1, source_target_pairs={{0,2},{1,3},{2,0},{3,1},{4,6},{5,7},{6,4},{7,5},{8,10},{9,11},{10,... | collective-permute-start | bytes 4718600 | tf_op jit(solution)/shard_map/ppermute | solution.py:18
  121.4 53.4 %collective-permute-start.9 = (bf16[384,1024]{1,0:T(8,128)(2,1)S(1)}, bf16[384,1024]{1,0:T(8,128)(2,1)}, u32[]{:S(2)}, u32[]{:S(2)}) collective-permute-start(bf16[384,1024]{1,0:T(8,128)(2,1)S(1)} %copy-done.15), channel_id=1, source_target_pairs={{0,4},{1,5},{2,6},{3,7},{4,0},{5,1},{6,2},{7,3},{8,12},{9,13},{10,... | collective-permute-start | bytes 2359304 | tf_op jit(solution)/shard_map/ppermute | solution.py:18
  126.9 47.7 %collective-permute-start.10 = (bf16[256,768]{1,0:T(8,128)(2,1)S(1)}, bf16[256,768]{1,0:T(8,128)(2,1)S(1)}, u32[]{:S(2)}, u32[]{:S(2)}) collective-permute-start(bf16[256,768]{1,0:T(8,128)(2,1)S(1)} %convert_element_type.53), channel_id=1, source_target_pairs={{0,4},{1,5},{2,6},{3,7},{4,0},{5,1},{6,2},{7,3},{8,12},{9,13},{10,... | collective-permute-start | bytes 1179656 | tf_op jit(solution)/shard_map/ppermute | solution.py:18
  180.2 11.1 %collective-permute-start.11 = (bf16[256,768]{1,0:T(8,128)(2,1)S(1)}, bf16[256,768]{1,0:T(8,128)(2,1)}, u32[]{:S(2)}, u32[]{:S(2)}) collective-permute-start(bf16[256,768]{1,0:T(8,128)(2,1)S(1)} %add_convert_fusion.1), channel_id=1, source_target_pairs={{0,2},{1,3},{2,0},{3,1},{4,6},{5,7},{6,4},{7,5},{8,10},{9,11},{10,... | collective-permute-start | bytes 1179656 | tf_op jit(solution)/shard_map/ppermute | solution.py:18
  193.5 5.3 %collective-permute-start.12 = (bf16[512,768]{1,0:T(8,128)(2,1)}, bf16[512,768]{1,0:T(8,128)(2,1)}, u32[]{:S(2)}, u32[]{:S(2)}) collective-permute-start(bf16[512,768]{1,0:T(8,128)(2,1)} %pad_maximum_fusion.3), channel_id=1, source_target_pairs={{0,1},{1,0},{2,3},{3,2},{4,5},{5,4},{6,7},{7,6},{8,9},{9,8},{10,11... | collective-permute-start | bytes 2359304 | tf_op jit(solution)/shard_map/ppermute | solution.py:18
  194.5 49.4 %collective-permute-start.14 = (bf16[512,1024]{1,0:T(8,128)(2,1)}, bf16[512,1024]{1,0:T(8,128)(2,1)}, u32[]{:S(2)}, u32[]{:S(2)}) collective-permute-start(bf16[512,1024]{1,0:T(8,128)(2,1)} %slice.41), channel_id=1, source_target_pairs={{0,4},{1,5},{2,6},{3,7},{4,0},{5,1},{6,2},{7,3},{8,12},{9,13},{10,... | collective-permute-start | bytes 3145736 | tf_op jit(solution)/shard_map/ppermute | solution.py:18
  197.0 48.0 %collective-permute-start.13 = (bf16[512,1024]{1,0:T(8,128)(2,1)}, bf16[512,1024]{1,0:T(8,128)(2,1)}, u32[]{:S(2)}, u32[]{:S(2)}) collective-permute-start(bf16[512,1024]{1,0:T(8,128)(2,1)} %slice.40), channel_id=1, source_target_pairs={{0,2},{1,3},{2,0},{3,1},{4,6},{5,7},{6,4},{7,5},{8,10},{9,11},{10,... | collective-permute-start | bytes 3145736 | tf_op jit(solution)/shard_map/ppermute | solution.py:18
  246.1 2.0 collective-permute-start.15
  246.2 82.1 %collective-permute-start.19 = (bf16[896,1024]{1,0:T(8,128)(2,1)}, bf16[896,1024]{1,0:T(8,128)(2,1)}, u32[]{:S(2)}, u32[]{:S(2)}) collective-permute-start(bf16[896,1024]{1,0:T(8,128)(2,1)} %get-tuple-element.75), channel_id=1, source_target_pairs={{0,4},{1,5},{2,6},{3,7},{4,0},{5,1},{6,2},{7,3},{8,12},{9,13},{10,... | collective-permute-start | bytes 5505032 | tf_op jit(solution)/shard_map/ppermute | solution.py:18
  250.9 68.3 %collective-permute-start.18 = (bf16[448,1024]{1,0:T(8,128)(2,1)S(1)}, bf16[448,1024]{1,0:T(8,128)(2,1)S(1)}, u32[]{:S(2)}, u32[]{:S(2)}) collective-permute-start(bf16[448,1024]{1,0:T(8,128)(2,1)S(1)} %pad_maximum_fusion.2), channel_id=1, source_target_pairs={{0,2},{1,3},{2,0},{3,1},{4,6},{5,7},{6,4},{7,5},{8,10},{9,11},{10,... | collective-permute-start | bytes 2752520 | tf_op jit(solution)/shard_map/ppermute | solution.py:18
  272.8 78.7 %collective-permute-start.21 = (bf16[640,1024]{1,0:T(8,128)(2,1)}, bf16[640,1024]{1,0:T(8,128)(2,1)}, u32[]{:S(2)}, u32[]{:S(2)}) collective-permute-start(bf16[640,1024]{1,0:T(8,128)(2,1)} %get-tuple-element.78), channel_id=1, source_target_pairs={{0,2},{1,3},{2,0},{3,1},{4,6},{5,7},{6,4},{7,5},{8,10},{9,11},{10,... | collective-permute-start | bytes 3932168 | tf_op jit(solution)/shard_map/ppermute | solution.py:18
  328.2 9.3 %collective-permute-start.20 = (bf16[256,256]{1,0:T(8,128)(2,1)S(1)}, bf16[256,256]{1,0:T(8,128)(2,1)S(1)}, u32[]{:S(2)}, u32[]{:S(2)}) collective-permute-start(bf16[256,256]{1,0:T(8,128)(2,1)S(1)} %convert_element_type.59), channel_id=1, source_target_pairs={{0,4},{1,5},{2,6},{3,7},{4,0},{5,1},{6,2},{7,3},{8,12},{9,13},{10,... | collective-permute-start | bytes 393224 | tf_op jit(solution)/shard_map/ppermute | solution.py:18
  328.3 23.2 %collective-permute-start.22 = (bf16[128,1024]{1,0:T(8,128)(2,1)}, bf16[128,1024]{1,0:T(8,128)(2,1)S(1)}, u32[]{:S(2)}, u32[]{:S(2)}) collective-permute-start(bf16[128,1024]{1,0:T(8,128)(2,1)} %get-tuple-element.80), channel_id=1, source_target_pairs={{0,4},{1,5},{2,6},{3,7},{4,0},{5,1},{6,2},{7,3},{8,12},{9,13},{10,... | collective-permute-start | bytes 786440 | tf_op jit(solution)/shard_map/ppermute | solution.py:18
  351.5 5.0 %collective-permute-start.23 = (bf16[256,256]{1,0:T(8,128)(2,1)S(1)}, bf16[256,256]{1,0:T(8,128)(2,1)S(1)}, u32[]{:S(2)}, u32[]{:S(2)}) collective-permute-start(bf16[256,256]{1,0:T(8,128)(2,1)S(1)} %add_convert_fusion.2), channel_id=1, source_target_pairs={{0,2},{1,3},{2,0},{3,1},{4,6},{5,7},{6,4},{7,5},{8,10},{9,11},{10,... | collective-permute-start | bytes 393224 | tf_op jit(solution)/shard_map/ppermute | solution.py:18
  351.5 7.5 %collective-permute-start.16 = (bf16[512,1024]{1,0:T(8,128)(2,1)S(1)}, bf16[512,1024]{1,0:T(8,128)(2,1)S(1)}, u32[]{:S(2)}, u32[]{:S(2)}) collective-permute-start(bf16[512,1024]{1,0:T(8,128)(2,1)S(1)} %copy-done.17), channel_id=1, source_target_pairs={{0,1},{1,0},{2,3},{3,2},{4,5},{5,4},{6,7},{7,6},{8,9},{9,8},{10,11... | collective-permute-start | bytes 3145736 | tf_op jit(solution)/shard_map/ppermute | solution.py:18
  351.6 7.4 %collective-permute-start.17 = (bf16[512,1024]{1,0:T(8,128)(2,1)S(1)}, bf16[512,1024]{1,0:T(8,128)(2,1)S(1)}, u32[]{:S(2)}, u32[]{:S(2)}) collective-permute-start(bf16[512,1024]{1,0:T(8,128)(2,1)S(1)} %copy-done.16), channel_id=1, source_target_pairs={{0,1},{1,0},{2,3},{3,2},{4,5},{5,4},{6,7},{7,6},{8,9},{9,8},{10,11... | collective-permute-start | bytes 3145736 | tf_op jit(solution)/shard_map/ppermute | solution.py:18
  (21 other events, 358.0 us)

commit v7 on v6

--- a/solution.py
+++ b/solution.py
@@ -8,7 +8,7 @@
 from jax.sharding import PartitionSpec as P
 
 UP_SHARES = ((2, 6, 0), (5, 3, 0))
-BACK_SHARES = ((3, 5, 0), (7, 1, 0))
+BACK_SHARES = ((3, 4, 1), (7, 1, 0))
 BF16 = jnp.bfloat16
 F32 = jnp.float32
 

time: 371 us -> 370 us (level)
    ppermute x24 -> x25, waiting for transfers between devices: 146 us -> 147 us  [swapped(): return lax.ppermute(value, 'tensor', pairs)]
    ppermute x24 -> x25, starting transfers between devices: 22.7 us -> 23 us  [swapped(): return lax.ppermute(value, 'tensor', pairs)]
  transfers between devices with their start and end apart: 25 -> 26, of which waited for: 15 -> 16; matrix products, arithmetic and copies ran while one was open for 8% -> 9% of each run, Pallas kernels for 40% -> 40%
where the time goes in v7:
time: 370 us; the launch traced here: 369 us
  Pallas kernels  147 us (40%)
  waiting for transfers between devices  147 us (40%)
  starting transfers between devices  26.9 us (7%)
  local copies, waits for them, and re-layouts  24.2 us (7%)
  other arithmetic  14.5 us (4%)
  matrix products  8.1 us (2%)
    ppermute x25, waiting for transfers between devices, swapped(): return lax.ppermute(value, 'tensor', pairs)  147 us
    pallas_call x1, Pallas kernels, hidden_call(): pl.pallas_call(functools.partial(hidden_kernel, [len(link) for link in up...  36.4 us
    pallas_call x2, Pallas kernels, second_call(): pl.pallas_call(functools.partial(second_kernel, [len(link) for link in up...  35.3 us
    pallas_call x1, Pallas kernels, first_call(): pl.pallas_call(functools.partial(first_kernel, [len(link) for link in ins...  30.7 us
    pallas_call x1, Pallas kernels, gate_call(): pl.pallas_call(functools.partial(gate_kernel, min(64, tokens)), grid=(wid...  23.1 us
    ppermute x25, starting transfers between devices, swapped(): return lax.ppermute(value, 'tensor', pairs)  23 us
    pallas_call x1, Pallas kernels, near_call(): pl.pallas_call(functools.partial(near_kernel, near, group), grid=(count_i...  21.5 us
  transfers between devices with their start and end apart: 26, of which 16 were waited for; matrix products, arithmetic and copies ran while one was open for 9% of the time, Pallas kernels for 40%

profile of v7, /device:TPU:0, one launch (start us, length us, event | category | flops | bytes accessed | tf_op | source)
XLA Modules:
  0.0 368.5 jit_solution(8237464888745354753)
XLA Ops:
  0.6 3.9 %collective-permute-start = (bf16[1024,1024]{1,0:T(8,128)(2,1)}, bf16[1024,1024]{1,0:T(8,128)(2,1)S(1)}, u32[]{:S(2)}, u32[]{:S(2)}) collective-permute-start(bf16[1024,1024]{1,0:T(8,128)(2,1)} %bitcast.34), channel_id=1, source_target_pairs={{0,24},{8,0},{16,8},{24,16},{1,25},{9,1},{17,9},{25,17},{2,26},{10... | collective-permute-start | bytes 6291464 | tf_op jit(solution)/shard_map/ppermute | solution.py:23
  11.0 23.1 %gate.1 = (bf16[1024,4096]{1,0:T(8,128)(2,1)}, f32[1024,4096]{1,0:T(8,128)}, f32[1024,256]{1,0:T(8,128)}) custom-call(bf16[1,1024,4096]{2,1,0:T(8,128)(2,1)} %preact.1, bf16[1,4096,256]{2,1,0:T(8,128)(2,1)} %refs_15_.1), custom_call_target="tpu_custom_call" | custom-call | flops 1024 | bytes 1024 | tf_op jit(solution)/shard_map/gate/pallas_call | solution.py:138
  36.5 19.7 %collective-permute-done.3.refs_6_ = bf16[512,1024]{1,0:T(8,128)(2,1)} collective-permute-done((bf16[512,1024]{1,0:T(8,128)(2,1)}, bf16[512,1024]{1,0:T(8,128)(2,1)}, u32[]{:S(2)}, u32[]{:S(2)}) %collective-permute-start.3) | collective-permute-done | bytes 1048608 | tf_op jit(solution)/shard_map/ppermute | solution.py:18
  62.6 2.9 collective-permute-done.5
  74.1 21.4 %second_early.1.refs_6_ = bf16[1,16,6,256,256]{4,3,2,1,0:T(8,128)(2,1)} custom-call(bf16[1024,1024]{1,0:T(8,128)(2,1)} %copy-done.1, bf16[1024,1024]{1,0:T(8,128)(2,1)} %copy-done.1, bf16[1024,1024]{1,0:T(8,128)(2,1)} %copy-done.1, bf16[1024,1024]{1,0:T(8,128)(2,1)} %collective-permute-done.4.refs_3_, bf16[1024,4096]{1,0:T(8,128)(2,1)} %get-tuple-element.52.refs_4_.refs_5_), custom_call_target="tpu_custom_call" | custom-call | flops 1024 | bytes 1024 | tf_op jit(solution)/shard_map/second_early/pallas_call | solution.py:394
  98.3 13.5 %collective-permute-done.6 = bf16[448,1024]{1,0:T(8,128)(2,1)S(1)} collective-permute-done((bf16[448,1024]{1,0:T(8,128)(2,1)}, bf16[448,1024]{1,0:T(8,128)(2,1)S(1)}, u32[]{:S(2)}, u32[]{:S(2)}) %collective-permute-start.6) | collective-permute-done | bytes 917536 | tf_op jit(solution)/shard_map/ppermute | solution.py:18
  115.1 6.2 %collective-permute-done.8.refs_6_.refs_2_ = bf16[640,1024]{1,0:T(8,128)(2,1)} collective-permute-done((bf16[640,1024]{1,0:T(8,128)(2,1)}, bf16[640,1024]{1,0:T(8,128)(2,1)}, u32[]{:S(2)}, u32[]{:S(2)}) %collective-permute-start.8) | collective-permute-done | bytes 1310752 | tf_op jit(solution)/shard_map/ppermute | solution.py:18
  121.3 5.6 %collective-permute-start.9 = (bf16[384,1024]{1,0:T(8,128)(2,1)S(1)}, bf16[384,1024]{1,0:T(8,128)(2,1)}, u32[]{:S(2)}, u32[]{:S(2)}) collective-permute-start(bf16[384,1024]{1,0:T(8,128)(2,1)S(1)} %copy-done.15), channel_id=1, source_target_pairs={{0,4},{1,5},{2,6},{3,7},{4,0},{5,1},{6,2},{7,3},{8,12},{9,13},{10,... | collective-permute-start | bytes 2359304 | tf_op jit(solution)/shard_map/ppermute | solution.py:18
  127.1 47.6 %collective-permute-done.10 = bf16[256,768]{1,0:T(8,128)(2,1)S(1)} collective-permute-done((bf16[256,768]{1,0:T(8,128)(2,1)S(1)}, bf16[256,768]{1,0:T(8,128)(2,1)S(1)}, u32[]{:S(2)}, u32[]{:S(2)}) %collective-permute-start.10) | collective-permute-done | bytes 393248 | tf_op jit(solution)/shard_map/ppermute | solution.py:18
  174.7 5.5 %collective-permute-done.7.refs_5_.refs_1_ = bf16[768,1024]{1,0:T(8,128)(2,1)} collective-permute-done((bf16[768,1024]{1,0:T(8,128)(2,1)}, bf16[768,1024]{1,0:T(8,128)(2,1)}, u32[]{:S(2)}, u32[]{:S(2)}) %collective-permute-start.7) | collective-permute-done | bytes 1572896 | tf_op jit(solution)/shard_map/ppermute | solution.py:18
  180.2 11.1 %collective-permute-done.11 = bf16[256,768]{1,0:T(8,128)(2,1)} collective-permute-done((bf16[256,768]{1,0:T(8,128)(2,1)S(1)}, bf16[256,768]{1,0:T(8,128)(2,1)}, u32[]{:S(2)}, u32[]{:S(2)}) %collective-permute-start.11) | collective-permute-done | bytes 393248 | tf_op jit(solution)/shard_map/ppermute | solution.py:18
  201.3 36.4 %hidden_grad.1 = (bf16[1024,4096]{1,0:T(8,128)(2,1)}, bf16[384,1024]{1,0:T(8,128)(2,1)}, bf16[512,1024]{1,0:T(8,128)(2,1)}, bf16[128,1024]{1,0:T(8,128)(2,1)}, b...) custom-call(bf16[1024,1024]{1,0:T(8,128)(2,1)} %copy-done.1, ...), custom_call_target="tpu_custom_call" | custom-call | flops 1024 | bytes 1024 | tf_op jit(solution)/shard_map/hidden_grad/pallas_call | solution.py:263
  237.7 6.2 %collective-permute-done.14.refs_7_ = bf16[512,1024]{1,0:T(8,128)(2,1)} collective-permute-done((bf16[512,1024]{1,0:T(8,128)(2,1)}, bf16[512,1024]{1,0:T(8,128)(2,1)}, u32[]{:S(2)}, u32[]{:S(2)}) %collective-permute-start.14) | collective-permute-done | bytes 1048608 | tf_op jit(solution)/shard_map/ppermute | solution.py:18
  251.3 21.5 %near_parts.1 = (f32[1024,1024]{1,0:T(8,128)}, bf16[512,1024]{1,0:T(8,128)(2,1)}, bf16[512,1024]{1,0:T(8,128)(2,1)}) custom-call(bf16[1024,4096]{1,0:T(8,128)(2,1)} %get-tuple-element.69.hid.refs_9_, bf16[1,16,6,256,256]{4,3,2,1,0:T(8,128)(2,1)} %refs_1_.1, bf16[1,16,6,256,256]{4,3,2,1,0:T(8,128)(2,1)} %refs_1_.1), custom_call_target="tpu_custom_call" | custom-call | flops 1024 | bytes 1024 | tf_op jit(solution)/shard_map/near_parts/pallas_call | solution.py:313
  274.5 13.9 %second_late.1 = (bf16[1,16,6,256,256]{4,3,2,1,0:T(8,128)(2,1)}, bf16[1,4096,256]{2,1,0:T(8,128)(2,1)}) custom-call(bf16[256,1024]{1,0:T(8,128)(2,1)} %slice.44.refs_4_.refs_0_, bf16[768,1024]{1,0:T(8,128)(2,1)} %collective-permute-done.7.refs_5_.refs_1_, bf16[640,1024]{1,0:T(8,128)(2,1)} %collective-permute-done.8.refs_6_.refs_2_, ...), custom_call_target="tpu_custom_call", output_to_operand_aliasing={{0}: (6, {})} | custom-call | flops 1024 | bytes 1024 | tf_op jit(solution)/shard_map/second_late/pallas_call | solution.py:394
  288.4 30.7 %first_grad.1 = (bf16[1,16,6,256,256]{4,3,2,1,0:T(8,128)(2,1)}, bf16[1,256,4096]{2,1,0:T(8,128)(2,1)}) custom-call(bf16[1024,1024]{1,0:T(8,128)(2,1)} %bitcast.29, bf16[1024,1024]{1,0:T(8,128)(2,1)} %bitcast.30, bf16[1024,1024]{1,0:T(8,128)(2,1)} %bitcast.31, bf16[1024,1024]{1,0:T(8,128)(2,1)} %collective-permute-done.1.refs_3_, ...), custom_call_target="tpu_custom_call" | custom-call | flops 1024 | bytes 1024 | tf_op jit(solution)/shard_map/first_grad/pallas_call | solution.py:438
  322.6 5.6 %collective-permute-done.19 = bf16[896,1024]{1,0:T(8,128)(2,1)} collective-permute-done((bf16[896,1024]{1,0:T(8,128)(2,1)}, bf16[896,1024]{1,0:T(8,128)(2,1)}, u32[]{:S(2)}, u32[]{:S(2)}) %collective-permute-start.19) | collective-permute-done | bytes 1835040 | tf_op jit(solution)/shard_map/ppermute | solution.py:18
  328.3 2.9 collective-permute-start.22
  331.8 10.9 %collective-permute-done.20 = bf16[256,256]{1,0:T(8,128)(2,1)S(1)} collective-permute-done((bf16[256,256]{1,0:T(8,128)(2,1)S(1)}, bf16[256,256]{1,0:T(8,128)(2,1)S(1)}, u32[]{:S(2)}, u32[]{:S(2)}) %collective-permute-start.20) | collective-permute-done | bytes 131104 | tf_op jit(solution)/shard_map/ppermute | solution.py:18
  342.7 5.5 %collective-permute-done.22 = bf16[128,1024]{1,0:T(8,128)(2,1)S(1)} collective-permute-done((bf16[128,1024]{1,0:T(8,128)(2,1)}, bf16[128,1024]{1,0:T(8,128)(2,1)S(1)}, u32[]{:S(2)}, u32[]{:S(2)}) %collective-permute-start.22) | collective-permute-done | bytes 262176 | tf_op jit(solution)/shard_map/ppermute | solution.py:18
  348.2 5.4 %collective-permute-done.23 = bf16[256,256]{1,0:T(8,128)(2,1)S(1)} collective-permute-done((bf16[256,256]{1,0:T(8,128)(2,1)S(1)}, bf16[256,256]{1,0:T(8,128)(2,1)S(1)}, u32[]{:S(2)}, u32[]{:S(2)}) %collective-permute-start.23) | collective-permute-done | bytes 131104 | tf_op jit(solution)/shard_map/ppermute | solution.py:18
  356.2 2.7 add_add_fusion
  360.6 3.4 collective-permute-done.25
  364.0 4.5 %fusion = bf16[1,1024,1024]{2,1,0:T(8,128)(2,1)} fusion(f32[1024,1024]{1,0:T(8,128)} %add_add_fusion, bf16[128,1024]{1,0:T(8,128)(2,1)S(1)} %collective-permute-done.25, bf16[512,1024]{1,0:T(8,128)(2,1)} %collective-permute-done.21, bf16[384,1024]{1,0:T(8,128)(2,1)S(1)} %slice-done, bf16[128,1024]{1,0:T(8,128)(2,1)S(1)} %collective-permute-done.22, ...), kind=kLoop, calls=%fused_computation.3 | loop fusion | flops 13631488 | bytes 10485760 | tf_op jit(solution)/shard_map/broadcast_in_dim | solution.py:542
  (119 shorter events, 57.2 us)
Async XLA Ops:
  0.6 55.8 %collective-permute-start = (bf16[1024,1024]{1,0:T(8,128)(2,1)}, bf16[1024,1024]{1,0:T(8,128)(2,1)S(1)}, u32[]{:S(2)}, u32[]{:S(2)}) collective-permute-start(bf16[1024,1024]{1,0:T(8,128)(2,1)} %bitcast.34), channel_id=1, source_target_pairs={{0,24},{8,0},{16,8},{24,16},{1,25},{9,1},{17,9},{25,17},{2,26},{10... | collective-permute-start | bytes 6291464 | tf_op jit(solution)/shard_map/ppermute | solution.py:23
  4.6 51.8 %collective-permute-start.1 = (bf16[1024,1024]{1,0:T(8,128)(2,1)}, bf16[1024,1024]{1,0:T(8,128)(2,1)}, u32[]{:S(2)}, u32[]{:S(2)}) collective-permute-start(bf16[1024,1024]{1,0:T(8,128)(2,1)} %bitcast.28), channel_id=1, source_target_pairs={{0,1},{1,0},{2,3},{3,2},{4,5},{5,4},{6,7},{7,6},{8,9},{9,8},{10,11... | collective-permute-start | bytes 6291464 | tf_op jit(solution)/shard_map/ppermute | solution.py:18
  6.9 49.4 %collective-permute-start.3 = (bf16[512,1024]{1,0:T(8,128)(2,1)}, bf16[512,1024]{1,0:T(8,128)(2,1)}, u32[]{:S(2)}, u32[]{:S(2)}) collective-permute-start(bf16[512,1024]{1,0:T(8,128)(2,1)} %slice_bitcast_fusion), channel_id=1, source_target_pairs={{0,4},{1,5},{2,6},{3,7},{4,0},{5,1},{6,2},{7,3},{8,12},{9,13},{10,... | collective-permute-start | bytes 3145736 | tf_op jit(solution)/shard_map/ppermute | solution.py:18
  9.4 47.0 %collective-permute-start.2 = (bf16[512,1024]{1,0:T(8,128)(2,1)}, bf16[512,1024]{1,0:T(8,128)(2,1)}, u32[]{:S(2)}, u32[]{:S(2)}) collective-permute-start(bf16[512,1024]{1,0:T(8,128)(2,1)} %slice_bitcast_fusion), channel_id=1, source_target_pairs={{0,2},{1,3},{2,0},{3,1},{4,6},{5,7},{6,4},{7,5},{8,10},{9,11},{10,... | collective-permute-start | bytes 3145736 | tf_op jit(solution)/shard_map/ppermute | solution.py:18
  59.5 6.0 %collective-permute-start.5 = (f32[512,768]{1,0:T(8,128)}, f32[512,768]{1,0:T(8,128)}, u32[]{:S(2)}, u32[]{:S(2)}) collective-permute-start(f32[512,768]{1,0:T(8,128)} %constant_dynamic-slice_fusion.1), channel_id=1, source_target_pairs={{0,1},{1,0},{2,3},{3,2},{4,5},{5,4},{6,7},{7,6},{8,9},{9,8},{10,11... | collective-permute-start | bytes 4718600 | tf_op jit(solution)/shard_map/ppermute | solution.py:18
  59.6 14.6 %collective-permute-start.4 = (bf16[1024,1024]{1,0:T(8,128)(2,1)S(1)}, bf16[1024,1024]{1,0:T(8,128)(2,1)}, u32[]{:S(2)}, u32[]{:S(2)}) collective-permute-start(bf16[1024,1024]{1,0:T(8,128)(2,1)S(1)} %collective-permute-done.refs_0_.refs_1_.refs_2_), channel_id=1, source_target_pairs={{0,1},{1,0},{2,3},{3,2},{4,5},{5,4},{6,7},{7,6},{8,9},{9,8},{10,11... | collective-permute-start | bytes 6291464 | tf_op jit(solution)/shard_map/ppermute | solution.py:18
  61.3 60.1 %collective-permute-start.8 = (bf16[640,1024]{1,0:T(8,128)(2,1)}, bf16[640,1024]{1,0:T(8,128)(2,1)}, u32[]{:S(2)}, u32[]{:S(2)}) collective-permute-start(bf16[640,1024]{1,0:T(8,128)(2,1)} %slice.37), channel_id=1, source_target_pairs={{0,4},{1,5},{2,6},{3,7},{4,0},{5,1},{6,2},{7,3},{8,12},{9,13},{10,... | collective-permute-start | bytes 3932168 | tf_op jit(solution)/shard_map/ppermute | solution.py:18
  71.4 40.4 %collective-permute-start.6 = (bf16[448,1024]{1,0:T(8,128)(2,1)}, bf16[448,1024]{1,0:T(8,128)(2,1)S(1)}, u32[]{:S(2)}, u32[]{:S(2)}) collective-permute-start(bf16[448,1024]{1,0:T(8,128)(2,1)} %pad_maximum_fusion.1), channel_id=1, source_target_pairs={{0,2},{1,3},{2,0},{3,1},{4,6},{5,7},{6,4},{7,5},{8,10},{9,11},{10,... | collective-permute-start | bytes 2752520 | tf_op jit(solution)/shard_map/ppermute | solution.py:18
  95.5 84.7 %collective-permute-start.7 = (bf16[768,1024]{1,0:T(8,128)(2,1)}, bf16[768,1024]{1,0:T(8,128)(2,1)}, u32[]{:S(2)}, u32[]{:S(2)}) collective-permute-start(bf16[768,1024]{1,0:T(8,128)(2,1)} %slice.36), channel_id=1, source_target_pairs={{0,2},{1,3},{2,0},{3,1},{4,6},{5,7},{6,4},{7,5},{8,10},{9,11},{10,... | collective-permute-start | bytes 4718600 | tf_op jit(solution)/shard_map/ppermute | solution.py:18
  121.3 53.4 %collective-permute-start.9 = (bf16[384,1024]{1,0:T(8,128)(2,1)S(1)}, bf16[384,1024]{1,0:T(8,128)(2,1)}, u32[]{:S(2)}, u32[]{:S(2)}) collective-permute-start(bf16[384,1024]{1,0:T(8,128)(2,1)S(1)} %copy-done.15), channel_id=1, source_target_pairs={{0,4},{1,5},{2,6},{3,7},{4,0},{5,1},{6,2},{7,3},{8,12},{9,13},{10,... | collective-permute-start | bytes 2359304 | tf_op jit(solution)/shard_map/ppermute | solution.py:18
  127.0 47.7 %collective-permute-start.10 = (bf16[256,768]{1,0:T(8,128)(2,1)S(1)}, bf16[256,768]{1,0:T(8,128)(2,1)S(1)}, u32[]{:S(2)}, u32[]{:S(2)}) collective-permute-start(bf16[256,768]{1,0:T(8,128)(2,1)S(1)} %convert_element_type.53), channel_id=1, source_target_pairs={{0,4},{1,5},{2,6},{3,7},{4,0},{5,1},{6,2},{7,3},{8,12},{9,13},{10,... | collective-permute-start | bytes 1179656 | tf_op jit(solution)/shard_map/ppermute | solution.py:18
  180.2 11.1 %collective-permute-start.11 = (bf16[256,768]{1,0:T(8,128)(2,1)S(1)}, bf16[256,768]{1,0:T(8,128)(2,1)}, u32[]{:S(2)}, u32[]{:S(2)}) collective-permute-start(bf16[256,768]{1,0:T(8,128)(2,1)S(1)} %add_convert_fusion.1), channel_id=1, source_target_pairs={{0,2},{1,3},{2,0},{3,1},{4,6},{5,7},{6,4},{7,5},{8,10},{9,11},{10,... | collective-permute-start | bytes 1179656 | tf_op jit(solution)/shard_map/ppermute | solution.py:18
  193.5 5.3 %collective-permute-start.12 = (bf16[512,768]{1,0:T(8,128)(2,1)}, bf16[512,768]{1,0:T(8,128)(2,1)}, u32[]{:S(2)}, u32[]{:S(2)}) collective-permute-start(bf16[512,768]{1,0:T(8,128)(2,1)} %pad_maximum_fusion.3), channel_id=1, source_target_pairs={{0,1},{1,0},{2,3},{3,2},{4,5},{5,4},{6,7},{7,6},{8,9},{9,8},{10,11... | collective-permute-start | bytes 2359304 | tf_op jit(solution)/shard_map/ppermute | solution.py:18
  194.5 49.4 %collective-permute-start.14 = (bf16[512,1024]{1,0:T(8,128)(2,1)}, bf16[512,1024]{1,0:T(8,128)(2,1)}, u32[]{:S(2)}, u32[]{:S(2)}) collective-permute-start(bf16[512,1024]{1,0:T(8,128)(2,1)} %slice.41), channel_id=1, source_target_pairs={{0,4},{1,5},{2,6},{3,7},{4,0},{5,1},{6,2},{7,3},{8,12},{9,13},{10,... | collective-permute-start | bytes 3145736 | tf_op jit(solution)/shard_map/ppermute | solution.py:18
  197.1 48.0 %collective-permute-start.13 = (bf16[512,1024]{1,0:T(8,128)(2,1)}, bf16[512,1024]{1,0:T(8,128)(2,1)}, u32[]{:S(2)}, u32[]{:S(2)}) collective-permute-start(bf16[512,1024]{1,0:T(8,128)(2,1)} %slice.40), channel_id=1, source_target_pairs={{0,2},{1,3},{2,0},{3,1},{4,6},{5,7},{6,4},{7,5},{8,10},{9,11},{10,... | collective-permute-start | bytes 3145736 | tf_op jit(solution)/shard_map/ppermute | solution.py:18
  246.2 82.1 %collective-permute-start.19 = (bf16[896,1024]{1,0:T(8,128)(2,1)}, bf16[896,1024]{1,0:T(8,128)(2,1)}, u32[]{:S(2)}, u32[]{:S(2)}) collective-permute-start(bf16[896,1024]{1,0:T(8,128)(2,1)} %get-tuple-element.79), channel_id=1, source_target_pairs={{0,4},{1,5},{2,6},{3,7},{4,0},{5,1},{6,2},{7,3},{8,12},{9,13},{10,... | collective-permute-start | bytes 5505032 | tf_op jit(solution)/shard_map/ppermute | solution.py:18
  250.9 68.2 %collective-permute-start.18 = (bf16[448,1024]{1,0:T(8,128)(2,1)S(1)}, bf16[448,1024]{1,0:T(8,128)(2,1)S(1)}, u32[]{:S(2)}, u32[]{:S(2)}) collective-permute-start(bf16[448,1024]{1,0:T(8,128)(2,1)S(1)} %pad_maximum_fusion.2), channel_id=1, source_target_pairs={{0,2},{1,3},{2,0},{3,1},{4,6},{5,7},{6,4},{7,5},{8,10},{9,11},{10,... | collective-permute-start | bytes 2752520 | tf_op jit(solution)/shard_map/ppermute | solution.py:18
  272.8 69.9 %collective-permute-start.21 = (bf16[512,1024]{1,0:T(8,128)(2,1)}, bf16[512,1024]{1,0:T(8,128)(2,1)}, u32[]{:S(2)}, u32[]{:S(2)}) collective-permute-start(bf16[512,1024]{1,0:T(8,128)(2,1)} %get-tuple-element.82), channel_id=1, source_target_pairs={{0,2},{1,3},{2,0},{3,1},{4,6},{5,7},{6,4},{7,5},{8,10},{9,11},{10,... | collective-permute-start | bytes 3145736 | tf_op jit(solution)/shard_map/ppermute | solution.py:18
  328.2 14.4 %collective-permute-start.20 = (bf16[256,256]{1,0:T(8,128)(2,1)S(1)}, bf16[256,256]{1,0:T(8,128)(2,1)S(1)}, u32[]{:S(2)}, u32[]{:S(2)}) collective-permute-start(bf16[256,256]{1,0:T(8,128)(2,1)S(1)} %convert_element_type.59), channel_id=1, source_target_pairs={{0,4},{1,5},{2,6},{3,7},{4,0},{5,1},{6,2},{7,3},{8,12},{9,13},{10,... | collective-permute-start | bytes 393224 | tf_op jit(solution)/shard_map/ppermute | solution.py:18
  328.3 19.9 %collective-permute-start.22 = (bf16[128,1024]{1,0:T(8,128)(2,1)}, bf16[128,1024]{1,0:T(8,128)(2,1)S(1)}, u32[]{:S(2)}, u32[]{:S(2)}) collective-permute-start(bf16[128,1024]{1,0:T(8,128)(2,1)} %get-tuple-element.84), channel_id=1, source_target_pairs={{0,4},{1,5},{2,6},{3,7},{4,0},{5,1},{6,2},{7,3},{8,12},{9,13},{10,... | collective-permute-start | bytes 786440 | tf_op jit(solution)/shard_map/ppermute | solution.py:18
  331.2 24.5 %collective-permute-start.16 = (bf16[512,1024]{1,0:T(8,128)(2,1)S(1)}, bf16[512,1024]{1,0:T(8,128)(2,1)S(1)}, u32[]{:S(2)}, u32[]{:S(2)}) collective-permute-start(bf16[512,1024]{1,0:T(8,128)(2,1)S(1)} %copy-done.17), channel_id=1, source_target_pairs={{0,1},{1,0},{2,3},{3,2},{4,5},{5,4},{6,7},{7,6},{8,9},{9,8},{10,11... | collective-permute-start | bytes 3145736 | tf_op jit(solution)/shard_map/ppermute | solution.py:18
  331.3 24.5 %collective-permute-start.17 = (bf16[512,1024]{1,0:T(8,128)(2,1)S(1)}, bf16[512,1024]{1,0:T(8,128)(2,1)S(1)}, u32[]{:S(2)}, u32[]{:S(2)}) collective-permute-start(bf16[512,1024]{1,0:T(8,128)(2,1)S(1)} %copy-done.16), channel_id=1, source_target_pairs={{0,1},{1,0},{2,3},{3,2},{4,5},{5,4},{6,7},{7,6},{8,9},{9,8},{10,11... | collective-permute-start | bytes 3145736 | tf_op jit(solution)/shard_map/ppermute | solution.py:18
  348.2 5.4 %collective-permute-start.23 = (bf16[256,256]{1,0:T(8,128)(2,1)S(1)}, bf16[256,256]{1,0:T(8,128)(2,1)S(1)}, u32[]{:S(2)}, u32[]{:S(2)}) collective-permute-start(bf16[256,256]{1,0:T(8,128)(2,1)S(1)} %add_convert_fusion.2), channel_id=1, source_target_pairs={{0,2},{1,3},{2,0},{3,1},{4,6},{5,7},{6,4},{7,5},{8,10},{9,11},{10,... | collective-permute-start | bytes 393224 | tf_op jit(solution)/shard_map/ppermute | solution.py:18
  355.3 8.7 %collective-permute-start.25 = (bf16[128,1024]{1,0:T(8,128)(2,1)S(1)}, bf16[128,1024]{1,0:T(8,128)(2,1)S(1)}, u32[]{:S(2)}, u32[]{:S(2)}) collective-permute-start(bf16[128,1024]{1,0:T(8,128)(2,1)S(1)} %copy-done.19), channel_id=1, source_target_pairs={{0,2},{1,3},{2,0},{3,1},{4,6},{5,7},{6,4},{7,5},{8,10},{9,11},{10,... | collective-permute-start | bytes 786440 | tf_op jit(solution)/shard_map/ppermute | solution.py:18
  (23 other events, 317.1 us)
